TPU v7x, 512 devices: a whole 4x8x8 slice. The times are simulated.
512 devices in a mesh: ctx: 64 (over y, z_hi, core), kvh: 8 (over x, z_lo).
Axes of the slice: x: 4, y: 8, z: 8 (z_hi: 4, z_lo: 2; z = z_hi * 2 + z_lo), core: 2. Of those that a mesh axis runs over, the one named last changes fastest.
Arguments:
- queries: bfloat16 [16384, 40, 128], P('ctx', 'kvh'), may hold values from -8 to 8
- key_rows: bfloat16 [16384, 8, 128], P('ctx', 'kvh'), may hold values from -8 to 8
- value_rows: bfloat16 [16384, 8, 128], P('ctx', 'kvh'), may hold values from -6 to 6
- vertical: int32 [8, 16], P('kvh'), may hold values from 0 to 127, as said below
- slash_offsets: int32 [8, 8], P('kvh'), may hold values from 0 to 15, as said below
Outputs:
- attended: bfloat16 [16384, 40, 128], P('ctx', 'kvh')
- profile: float32 [16384], P('ctx')
Inputs may be any that keep to these rules, and one draw needn't show every extreme that they name: `vertical`: each row names 16 different key blocks; the first is block 0. `slash_offsets`: each row names 8 different offsets; 0, 1 and 15 are always among them.
All inputs are finite; a program needn't handle non-finite values.
Results may differ from a plain program's by a relative error of at most 0.0075.
Values may be sent and summed in bfloat16 or wider, within the bound.
No kernel may reach another device: no remote copies, remote signals or barrier semaphores. Data moves between devices by JAX's collectives and lax.ppermute only.
A program may use at most 64 MiB of HBM per device.

v0:
```python
import math

import jax
import jax.numpy as jnp
from jax import lax
from jax.sharding import PartitionSpec as P

BLK = 128
LAST = 64
NV = 16
NS = 8
HEADS = 40


floor_score = -1e30


def broadcast(value, axis, source):
    kept = jnp.where(lax.axis_index(axis) == source, value, 0).astype(value.dtype)
    return lax.psum(kept, axis)


def on_device(queries, key_rows, value_rows, vertical, slash_offsets):
    local_rows = key_rows.shape[0]
    kv_heads = key_rows.shape[1]
    head_dim = key_rows.shape[2]
    group_size = queries.shape[1] // kv_heads
    blocks_dev = local_rows // BLK
    cycle_size = lax.axis_size("ctx")
    position = lax.axis_index("ctx")
    total_len = local_rows * cycle_size
    total_blocks = total_len // BLK
    score_scale = 1.0 / math.sqrt(head_dim)
    last_rows = queries[local_rows - LAST :]
    shared = broadcast(last_rows, "ctx", cycle_size - 1)
    q_estimate = shared.reshape(LAST, kv_heads, group_size, head_dim)
    est_scores = (
        jnp.einsum("qhgd,khd->hgqk", q_estimate, key_rows, preferred_element_type=jnp.float32)
        * score_scale
    )
    key_pos = position * local_rows + jnp.arange(local_rows, dtype=jnp.int32)
    last_pos = total_len - LAST + jnp.arange(LAST, dtype=jnp.int32)
    est_mask = key_pos[None, :] <= last_pos[:, None]
    est_scores = jnp.where(est_mask, est_scores, floor_score)
    local_max = jnp.max(est_scores, axis=-1)
    top = lax.pmax(local_max, "ctx")
    total = lax.psum(
        jnp.sum(jnp.where(est_mask, jnp.exp(est_scores - top[..., None]), 0.0), axis=-1), "ctx"
    )
    shares = jnp.where(est_mask, jnp.exp(est_scores - top[..., None]), 0.0) / total[..., None]
    partial_mass = jnp.sum(shares, axis=(0, 1, 2))
    summed_mass = lax.psum(partial_mass, "kvh")
    profile = summed_mass * (total_len / LAST / HEADS)
    head_index = jnp.arange(kv_heads, dtype=jnp.int32)
    slot_index = jnp.arange(NV + NS, dtype=jnp.int32)
    block_ids = position * blocks_dev + jnp.arange(blocks_dev, dtype=jnp.int32)
    chosen = jnp.concatenate(
        [
            jnp.broadcast_to(vertical[:, None, :], (kv_heads, blocks_dev, NV)),
            block_ids[None, :, None] - slash_offsets[:, None, :],
        ],
        axis=2,
    )
    in_range = (chosen >= 0) & (chosen <= block_ids[None, :, None])
    repeated = (
        (chosen[..., :, None] == chosen[..., None, :])
        & in_range[..., None, :]
        & (slot_index[None, :] < slot_index[:, None])
    )
    usable = in_range & jnp.logical_not(jnp.any(repeated, axis=-1))
    whole_k, whole_v = (
        lax.all_gather(key_rows, "ctx", axis=0, tiled=True),
        lax.all_gather(value_rows, "ctx", axis=0, tiled=True),
    )
    blocks_k = whole_k.reshape(total_blocks, BLK, kv_heads, head_dim)
    blocks_v = whole_v.reshape(total_blocks, BLK, kv_heads, head_dim)
    clipped_ids = jnp.clip(chosen, 0, total_blocks - 1)
    slot_k = blocks_k[clipped_ids, :, head_index[:, None, None], :]
    slot_v = blocks_v[clipped_ids, :, head_index[:, None, None], :]
    q_blocks = queries.reshape(blocks_dev, BLK, kv_heads, group_size, head_dim)
    inside = jnp.arange(BLK, dtype=jnp.int32)
    query_pos = block_ids[:, None] * BLK + inside[None, :]

    def attend_slot(carry, slot):
        accum, run_max, run_sum = carry
        k_slot, v_slot, slot_ids, slot_ok = slot
        scores = (
            jnp.einsum("bqhgd,hbkd->hbgqk", q_blocks, k_slot, preferred_element_type=jnp.float32)
            * score_scale
        )
        slot_pos = slot_ids[..., None] * BLK + inside
        allowed = slot_ok[..., None, None] & (
            slot_pos[:, :, None, :] <= query_pos[None, :, :, None]
        )
        allowed = allowed[:, :, None]
        scores = jnp.where(allowed, scores, floor_score)
        new_max = jnp.maximum(run_max, jnp.max(scores, axis=-1))
        factor = jnp.exp(run_max - new_max)
        weights = jnp.where(allowed, jnp.exp(scores - new_max[..., None]), 0.0)
        run_sum = run_sum * factor + jnp.sum(weights, axis=-1)
        accum = accum * factor[..., None] + jnp.einsum(
            "hbgqk,hbkd->hbgqd",
            weights.astype(jnp.bfloat16),
            v_slot,
            preferred_element_type=jnp.float32,
        )
        return ((accum, new_max, run_sum), None)

    start_acc = jnp.zeros((kv_heads, blocks_dev, group_size, BLK, head_dim), jnp.float32)
    start_max = jnp.full((kv_heads, blocks_dev, group_size, BLK), floor_score, jnp.float32)
    start_sum = jnp.zeros((kv_heads, blocks_dev, group_size, BLK), jnp.float32)
    slots_in = (
        jnp.moveaxis(slot_k, 2, 0),
        jnp.moveaxis(slot_v, 2, 0),
        jnp.moveaxis(chosen, 2, 0),
        jnp.moveaxis(usable, 2, 0),
    )
    (accum, run_max, run_sum), unused = lax.scan(
        attend_slot, (start_acc, start_max, start_sum), slots_in
    )
    result = accum / run_sum[..., None]
    attended = (
        jnp.transpose(result, (1, 3, 0, 2, 4))
        .reshape(local_rows, kv_heads * group_size, head_dim)
        .astype(jnp.bfloat16)
    )
    return (attended, profile)


def solution(mesh):
    return jax.shard_map(
        on_device,
        mesh=mesh,
        in_specs=(
            P("ctx", "kvh", None),
            P("ctx", "kvh", None),
            P("ctx", "kvh", None),
            P("kvh", None),
            P("kvh", None),
        ),
        out_specs=(P("ctx", "kvh", None), P("ctx")),
        check_vma=False,
    )
```

profile of v0, /device:TPU:1, one launch (start us, length us, event | category | flops | bytes accessed | tf_op | source)
XLA Modules:
  0.0 865.8 jit_solution(5242019711733383708)
XLA Ops:
  7.2 1.5 slice_select_fusion
  14.3 485.0 %all-reduce.3.cloned.1.call-done = bf16[64,5,128]{2,0,1:T(8,128)(2,1)} async-done(((bf16[64,5,128]{2,0,1:T(8,128)(2,1)}), bf16[64,5,128]{2,0,1:T(8,128)(2,1)}) %all-reduce.3.cloned.1.call-update) | async-done | bytes 81936 | tf_op jit(solution)/shard_map/psum | solution.py:20
  500.5 141.0 %pmax.7 = f32[5,64]{1,0:T(8,128)S(1)} all-reduce(f32[5,64]{1,0:T(8,128)S(1)} %get-tuple-element.160), channel_id=1, replica_groups=mesh['ctx'=64,'kvh'=8] {'ctx'}, use_global_device_ids=true, to_apply=%region_7.8 | all-reduce | flops 320 | bytes 2560 | tf_op jit(solution)/shard_map/pmax | solution.py:46
  641.6 139.7 %psum.22 = f32[5,64]{1,0:T(8,128)S(1)} all-reduce(f32[5,64]{1,0:T(8,128)S(1)} %fusion.28), channel_id=1, replica_groups=mesh['ctx'=64,'kvh'=8] {'ctx'}, use_global_device_ids=true, to_apply=%region_9.10 | all-reduce | flops 320 | bytes 2560 | tf_op jit(solution)/shard_map/psum | solution.py:47
  781.6 15.9 %psum.23 = f32[256]{0:T(256)S(1)} all-reduce(f32[256]{0:T(256)S(1)} %divide_reduce_fusion), channel_id=1, replica_groups=mesh['ctx'=64,'kvh'=8] {'kvh'}, use_global_device_ids=true, to_apply=%region_11.12 | all-reduce | flops 256 | bytes 2048 | tf_op jit(solution)/shard_map/psum | solution.py:52
  798.0 3.1 gather_fusion
  801.1 4.2 gather_fusion.1
  805.3 52.9 %while.15 = (s32[]{:T(128)}, f32[1,2,5,128,128]{4,3,2,1,0:T(8,128)S(1)}, f32[1,2,5,128]{3,2,1,0:T(8,128)S(1)}, f32[1,2,5,128]{3,2,1,0:T(8,128)S(1)}, pred[24,1,2...) while((s32[]{:T(128)}, ...), condition=%wide.region_4.5_spmd.clone, body=%wide.region_1.0_spmd.clone.sunk | while | flops 85925888 | bytes 3953335 | solution.py:118
  806.2 1.3 fusion.53
  808.4 1.3 fusion.53
  810.6 1.3 fusion.53
  812.8 1.3 fusion.53
  815.0 1.3 fusion.53
  817.2 1.3 fusion.53
  819.4 1.3 fusion.53
  821.6 1.3 fusion.53
  823.9 1.3 fusion.53
  826.1 1.3 fusion.53
  828.3 1.3 fusion.53
  830.5 1.3 fusion.53
  832.7 1.3 fusion.53
  841.5 1.3 fusion.53
  850.3 1.3 fusion.53
  852.5 1.3 fusion.53
  (284 shorter events, 38.9 us)
Async XLA Ops:
  7.2 492.1 %all-reduce.3.cloned.1.call-start = ((), (), s32[]{:S(2)}) async-start(), calls=%async_computation.2 | async-start | bytes 163840 | tf_op jit(solution)/shard_map/psum | solution.py:20
  8.8 789.3 %all-gather.3.cloned.1.call-start = ((), (), s32[]{:S(2)}) async-start(), calls=%async_computation | async-start | bytes 4259840 | tf_op jit(solution)/shard_map/all_gather | solution.py:72
  9.5 791.6 %all-gather.5.cloned.1.call-start = ((), (), s32[]{:S(2)}) async-start(), calls=%async_computation.1 | async-start | bytes 4259840 | tf_op jit(solution)/shard_map/all_gather | solution.py:73
Sparse Core Ops, SparseCore 0:
  11.5 487.7 all-reduce.2
  503.1 85.8 all-gather.2
  592.8 84.2 all-gather.4
where the time goes:
time: 870 us; the launch traced here: 866 us
  waiting for transfers between devices  486 us (56%)
  blocking collectives  297 us (34%)
  matrix products  38.9 us (4%)
  local copies, waits for them, and re-layouts  14.7 us (2%)
  between operations  13.9 us (2%)
  other arithmetic  13.3 us (2%)
    psum x1, waiting for transfers between devices, broadcast(): return lax.psum(kept, axis)  485 us
    pmax x1, blocking collectives, on_device(): top = lax.pmax(local_max, 'ctx')  141 us
    psum x1, blocking collectives, on_device(): lax.psum(jnp.sum(jnp.where(est_mask, jnp.exp(est_scores - top[..., None])...  140 us
    dot_general x24, matrix products, attend_slot(): jnp.einsum('hbgqk,hbkd->hbgqd', weights.astype(jnp.bfloat16), v_slot, pre...  31.2 us
  transfers between devices with their start and end apart: 3, of which 1 were waited for; matrix products, arithmetic and copies ran while one was open for 1% of the time, Pallas kernels for 0%

commit v1 on v0

v1 whole, which is shorter than its diff:
```python
import math

import jax
import jax.numpy as jnp
from jax import lax
from jax.experimental import pallas as pl
from jax.experimental.pallas import tpu as pltpu
from jax.sharding import Mesh
from jax.sharding import PartitionSpec as P

BLK = 128
LAST = 64
NV = 16
NS = 8
HEADS = 40
HD = 128
GROUP = 5
FAR = -1e30
LOG2E = math.log2(math.e)
C = ("zh", "core")
CTX = ("y", "zh", "core")


def spread(x, axis, n):
    return lax.all_to_all(jnp.broadcast_to(x, (n,) + x.shape), axis, 0, 0)


def estimate(q_t, key_rows, position, local, ny, nz):
    rows = GROUP * LAST
    total_len = local * ny * nz * 2
    scale = 1.0 / math.sqrt(HD)
    last = q_t[:, local - LAST :].reshape(ny, rows // ny, HD)
    part = lax.all_to_all(last, "y", 0, 0)[ny - 1]
    part = spread(part, C, 2 * nz)[2 * nz - 1]
    q_last = spread(part, "y", ny).reshape(rows, HD)
    scores = lax.dot_general(q_last, key_rows, (((1,), (1,)), ((), ())), preferred_element_type=jnp.float32) * scale
    key_pos = position * local + jnp.arange(local, dtype=jnp.int32)
    last_pos = total_len - LAST + jnp.arange(rows, dtype=jnp.int32) % LAST
    scores = jnp.where(key_pos[None, :] <= last_pos[:, None], scores, FAR)
    top = jnp.max(scores, axis=-1)
    total = jnp.sum(jnp.exp(scores - top[:, None]), axis=-1)
    both = lax.all_gather(jnp.stack([top, total]), "core")
    core = lax.axis_index("core")
    both = lax.dynamic_slice_in_dim(both.reshape(2, 2, 2, rows // 2), core, 1, 2)[:, :, 0]
    top = jnp.max(both[:, 0], axis=0)
    total = jnp.sum(both[:, 1] * jnp.exp(both[:, 0] - top), axis=0)
    every = spread(jnp.stack([top, total]), ("y", "zh"), ny * nz)
    top = jnp.max(every[:, 0], axis=0)
    total = jnp.sum(every[:, 1] * jnp.exp(every[:, 0] - top), axis=0)
    lse = spread(top + jnp.log(total), "core", 2).reshape(rows)
    mass = jnp.sum(jnp.exp(scores - lse[:, None]), axis=0)
    summed = jnp.sum(spread(mass, "kvh", lax.axis_size("kvh")), axis=0)
    return summed * (total_len / LAST / HEADS)


def attend_kernel(ids, bias, q, kv, out, k_vert, v_vert, k_near, v_near, s_buf, sems):
    near = NS
    copies = []
    n = 0

    def fetch(block, which, target):
        nonlocal n
        row = pl.multiple_of((block % 2) * BLK, BLK)
        copies.append(pltpu.make_async_copy(kv.at[block // 2, which, pl.ds(row, BLK)], target, sems.at[n]))
        copies[-1].start()
        n += 1

    for j in range(NV):
        fetch(ids[0, near + j], 0, k_vert.at[pl.ds(j * BLK, BLK)])
        fetch(ids[0, near + j], 1, v_vert.at[pl.ds(j * BLK, BLK)])
    for e in range(2):
        for j in range(near):
            fetch(ids[e, j], 0, k_near.at[e, pl.ds(j * BLK, BLK)])
            fetch(ids[e, j], 1, v_near.at[e, pl.ds(j * BLK, BLK)])
    for copy in copies:
        copy.wait()

    factor = LOG2E / math.sqrt(HD)
    nt = (((1,), (1,)), ((), ()))
    width_near = near * BLK
    causal = lax.broadcasted_iota(jnp.int32, (BLK, BLK), 1) <= lax.broadcasted_iota(jnp.int32, (BLK, BLK), 0)

    def scores(i):
        e, h = i % 2, i // 2
        tile = q[h, pl.ds(pl.multiple_of(e * BLK, BLK), BLK), :]
        a = lax.dot_general(tile, k_near[e], nt, preferred_element_type=jnp.float32) * factor + bias[e, :, :width_near]
        a = jnp.concatenate([jnp.where(causal, a[:, :BLK], FAR), a[:, BLK:]], axis=1)
        b = lax.dot_general(tile, k_vert[...], nt, preferred_element_type=jnp.float32) * factor + bias[e, :, width_near:]
        s_buf[i % 2, :, :width_near] = a
        s_buf[i % 2, :, width_near:] = b
        return jnp.maximum(jnp.max(a, axis=1, keepdims=True), jnp.max(b, axis=1, keepdims=True))

    def finish(i, top):
        e, h = i % 2, i // 2
        p = jnp.exp2(s_buf[i % 2] - top)
        total = jnp.sum(p, axis=1, keepdims=True)
        w = p.astype(jnp.bfloat16)
        o = jnp.dot(w[:, :width_near], v_near[e], preferred_element_type=jnp.float32)
        o += jnp.dot(w[:, width_near:], v_vert[...], preferred_element_type=jnp.float32)
        out[h, pl.ds(pl.multiple_of(e * BLK, BLK), BLK), :] = (o / total).astype(jnp.bfloat16)

    def step(i, top):
        later = scores(i + 1)
        finish(i, top)
        return later

    tiles = 2 * GROUP
    top = lax.fori_loop(0, tiles - 1, step, scores(0))
    finish(tiles - 1, top)


def attend(ids, bias, q_t, kv):
    local = q_t.shape[1]
    vmem = pl.BlockSpec(memory_space=pltpu.VMEM)
    return pl.pallas_call(
        attend_kernel,
        out_shape=jax.ShapeDtypeStruct((GROUP, local, HD), jnp.bfloat16),
        in_specs=[pl.BlockSpec(memory_space=pltpu.SMEM), vmem, vmem, pl.BlockSpec(memory_space=pl.ANY)],
        out_specs=vmem,
        scratch_shapes=[
            pltpu.VMEM((NV * BLK, HD), jnp.bfloat16),
            pltpu.VMEM((NV * BLK, HD), jnp.bfloat16),
            pltpu.VMEM((2, NS * BLK, HD), jnp.bfloat16),
            pltpu.VMEM((2, NS * BLK, HD), jnp.bfloat16),
            pltpu.VMEM((2, BLK, (NV + NS) * BLK), jnp.float32),
            pltpu.SemaphoreType.DMA((2 * NV + 4 * NS,)),
        ],
        compiler_params=pltpu.CompilerParams(vmem_limit_bytes=56 * 1024 * 1024),
        cost_estimate=pl.CostEstimate(flops=4 * 2 * GROUP * (NV + NS) * BLK**3, bytes_accessed=4 * 1024 * 1024, transcendentals=2 * GROUP * (NV + NS) * BLK**2),
    )(ids, bias, q_t, kv)


def lists(vertical, slash_offsets, position):
    own = (position * 2 + jnp.arange(2, dtype=jnp.int32))[:, None]
    slash = slash_offsets[0]
    others = jnp.where(slash[1:] == 0, slash[0], slash[1:])
    near = own - jnp.concatenate([jnp.zeros((1,), jnp.int32), others])[None, :]
    far = jnp.broadcast_to(vertical[0][None, :], (2, NV))
    again = jnp.any(far[:, :, None] == near[:, None, :], axis=-1)
    usable = jnp.concatenate([near >= 0, (far <= own) & jnp.logical_not(again)], axis=1)
    ids = jnp.maximum(jnp.concatenate([near, far], axis=1), 0)
    bias = jnp.where(usable, 0.0, FAR).astype(jnp.float32)
    bias = jnp.broadcast_to(bias[:, None, :, None], (2, 1, NV + NS, BLK)).reshape(2, 1, (NV + NS) * BLK)
    return ids, bias


def solution(mesh):
    ny, nz = 8, 4
    wide = Mesh(mesh.devices.reshape(ny, nz, 2, -1), ("y", "zh", "core", "kvh"))

    def on_device(queries, key_rows, value_rows, vertical, slash_offsets):
        local = key_rows.shape[0]
        position = (lax.axis_index("y") * nz + lax.axis_index("zh")) * 2 + lax.axis_index("core")
        q_t = jnp.transpose(queries, (1, 0, 2))
        k, v = key_rows[:, 0], value_rows[:, 0]
        kv = lax.all_gather(jnp.stack([k, v]), CTX)
        profile = estimate(q_t, k, position, local, ny, nz)
        ids, bias = lists(vertical, slash_offsets, position)
        attended = attend(ids, bias, q_t, kv)
        return jnp.transpose(attended, (1, 0, 2)), profile

    return jax.shard_map(
        on_device,
        mesh=wide,
        in_specs=(P(CTX, "kvh", None), P(CTX, "kvh", None), P(CTX, "kvh", None), P("kvh", None), P("kvh", None)),
        out_specs=(P(CTX, "kvh", None), P(CTX)),
        check_vma=False,
    )
```

time: 870 us -> 146 us (0.17)
  waiting for transfers between devices: 486 us -> 63.5 us
  blocking collectives: 297 us -> 7.84 us
  matrix products: 38.9 us -> 1.15 us
  starting transfers between devices: 0.12 us -> 32 us
  Pallas kernels: 0 us -> 14.5 us
  local copies, waits for them, and re-layouts: 14.7 us -> 5.62 us
    psum x1 -> x0, waiting for transfers between devices: 485 us -> none  [broadcast(): return lax.psum(kept, axis)]
    psum x2 -> x0, blocking collectives: 156 us -> none  [the longest x1 140 us: on_device(): lax.psum(jnp.sum(jnp.where(est_mask, jnp.exp(est_scores - top[..., None])...]
    pmax x1 -> x0, blocking collectives: 141 us -> none  [on_device(): top = lax.pmax(local_max, 'ctx')]
    dot_general x49 -> x1, matrix products: 38.9 us -> 1.15 us  [estimate(): lax.dot_general(q_last, key_rows, (((1,), (1,)), ((), ())), preferred_ele...]
    all_to_all x0 -> x5, waiting for transfers between devices: none -> 35.9 us  [the longest x4 31.5 us: spread(): return lax.all_to_all(jnp.broadcast_to(x, (n,) + x.shape), axis, 0, 0)]
    all_to_all x0 -> x5, starting transfers between devices: none -> 32 us  [the longest x4 24.3 us: spread(): return lax.all_to_all(jnp.broadcast_to(x, (n,) + x.shape), axis, 0, 0)]
    all_gather x2 -> x1, waiting for transfers between devices: 0.02 us -> 27.6 us  [on_device(): kv = lax.all_gather(jnp.stack([k, v]), CTX)]
    pallas_call x0 -> x1, Pallas kernels: none -> 14.5 us  [attend(): pl.pallas_call(attend_kernel, out_shape=jax.ShapeDtypeStruct((GROUP, loca...]
  transfers between devices with their start and end apart: 3 -> 6, of which waited for: 1 -> 6; matrix products, arithmetic and copies ran while one was open for 1% -> 8% of each run, Pallas kernels for 0% -> 0%
where the time goes in v1:
time: 146 us; the launch traced here: 145 us
  waiting for transfers between devices  63.5 us (43%)
  starting transfers between devices  32 us (22%)
  Pallas kernels  14.5 us (10%)
  between operations  14.1 us (10%)
  blocking collectives  7.84 us (5%)
  other arithmetic  6.52 us (4%)
  local copies, waits for them, and re-layouts  5.62 us (4%)
    all_to_all x4, waiting for transfers between devices, spread(): return lax.all_to_all(jnp.broadcast_to(x, (n,) + x.shape), axis, 0, 0)  31.5 us
    all_gather x1, waiting for transfers between devices, on_device(): kv = lax.all_gather(jnp.stack([k, v]), CTX)  27.6 us
    all_to_all x4, starting transfers between devices, spread(): return lax.all_to_all(jnp.broadcast_to(x, (n,) + x.shape), axis, 0, 0)  24.3 us
    pallas_call x1, Pallas kernels, attend(): pl.pallas_call(attend_kernel, out_shape=jax.ShapeDtypeStruct((GROUP, loca...  14.5 us
    all_to_all x1, starting transfers between devices, estimate(): part = lax.all_to_all(last, 'y', 0, 0)[ny - 1]  7.65 us
    all_to_all x1, blocking collectives, spread(): return lax.all_to_all(jnp.broadcast_to(x, (n,) + x.shape), axis, 0, 0)  4.84 us
    all_to_all x1, waiting for transfers between devices, estimate(): part = lax.all_to_all(last, 'y', 0, 0)[ny - 1]  4.4 us
    all_gather x1, blocking collectives, estimate(): both = lax.all_gather(jnp.stack([top, total]), 'core')  3 us
  transfers between devices with their start and end apart: 6, of which 6 were waited for; matrix products, arithmetic and copies ran while one was open for 8% of the time, Pallas kernels for 0%

profile of v1, /device:TPU:1, one launch (start us, length us, event | category | flops | bytes accessed | tf_op | source)
XLA Modules:
  0.0 145.3 jit_solution(7622579912337348710)
XLA Ops:
  7.2 1.5 %pad_maximum_fusion = bf16[2,256,128]{2,1,0:T(8,128)(2,1)} fusion(bf16[1,256,128]{2,1,0:T(8,128)(2,1)} %bitcast.63, bf16[1,256,128]{2,1,0:T(8,128)(2,1)} %bitcast.64), kind=kLoop, calls=%fused_computation.4 | loop fusion | flops 65536 | bytes 262144 | tf_op jit(solution)/shard_map/stack | solution.py:156
  8.8 1.5 %slice.44 = bf16[5,64,128]{2,1,0:T(8,128)(2,1)} slice(bf16[5,256,128]{2,1,0:T(8,128)(2,1)} %bitcast.58), slice={[0:5], [192:256], [0:128]} | slice | bytes 163840 | tf_op jit(solution)/shard_map/slice | solution.py:32
  10.3 7.7 %all-to-all-start = ((bf16[8,40,128]{2,1,0:T(8,128)(2,1)}), bf16[8,40,128]{2,1,0:T(8,128)(2,1)S(1)}, u32[]{:S(2)}, u32[]{:S(2)}) async-start(bf16[8,40,128]{2,1,0:T(8,128)(2,1)} %bitcast.9), calls=%async_computation | async-start | bytes 163840 | tf_op jit(solution)/shard_map/all_to_all | solution.py:33
  18.0 1.4 compare_select_fusion
  19.5 0.7 compare_reduce_fusion
  20.2 0.7 not_and_fusion
  21.0 4.4 %all-to-all-done = bf16[8,40,128]{2,1,0:T(8,128)(2,1)S(1)} async-done(((bf16[8,40,128]{2,1,0:T(8,128)(2,1)}), bf16[8,40,128]{2,1,0:T(8,128)(2,1)S(1)}, u32[]{:S(2)}, u32[]{:S(2)}) %all-to-all-start) | async-done | bytes 81952 | tf_op jit(solution)/shard_map/all_to_all | solution.py:33
  26.0 12.4 %all-to-all-start.1 = ((bf16[8,40,128]{2,1,0:T(8,128)(2,1)}), bf16[8,40,128]{2,1,0:T(8,128)(2,1)S(1)}, u32[]{:S(2)}, u32[]{:S(2)}) async-start(bf16[8,40,128]{2,1,0:T(8,128)(2,1)} %broadcast_in_dim.61), calls=%async_computation.1 | async-start | bytes 163840 | tf_op jit(solution)/shard_map/all_to_all | solution.py:25
  38.5 7.8 %all-to-all-done.1 = bf16[8,40,128]{2,1,0:T(8,128)(2,1)S(1)} async-done(((bf16[8,40,128]{2,1,0:T(8,128)(2,1)}), bf16[8,40,128]{2,1,0:T(8,128)(2,1)S(1)}, u32[]{:S(2)}, u32[]{:S(2)}) %all-to-all-start.1) | async-done | bytes 81952 | tf_op jit(solution)/shard_map/all_to_all | solution.py:25
  47.0 3.6 %all-to-all-start.2 = ((bf16[8,40,128]{2,1,0:T(8,128)(2,1)}), bf16[8,40,128]{2,1,0:T(8,128)(2,1)S(1)}, u32[]{:S(2)}, u32[]{:S(2)}) async-start(bf16[8,40,128]{2,1,0:T(8,128)(2,1)} %broadcast_in_dim.62), calls=%async_computation.2 | async-start | bytes 163840 | tf_op jit(solution)/shard_map/all_to_all | solution.py:25
  50.6 7.8 %all-to-all-done.2 = bf16[8,40,128]{2,1,0:T(8,128)(2,1)S(1)} async-done(((bf16[8,40,128]{2,1,0:T(8,128)(2,1)}), bf16[8,40,128]{2,1,0:T(8,128)(2,1)S(1)}, u32[]{:S(2)}, u32[]{:S(2)}) %all-to-all-start.2) | async-done | bytes 81952 | tf_op jit(solution)/shard_map/all_to_all | solution.py:25
  58.3 1.1 fusion.15
  59.7 3.0 %all-gather.2 = f32[2,2,320]{2,1,0:T(2,128)S(1)} all-gather(f32[1,2,320]{2,1,0:T(2,128)S(1)} %maximum_bitcast_fusion), channel_id=3, replica_groups=mesh['y'=8,'zh'=4,'core'=2,'kvh'=8] {'core'}, dimensions={0}, use_global_device_ids=true | all-gather | bytes 7680 | tf_op jit(solution)/shard_map/all_gather | solution.py:42
  62.9 0.7 broadcast_in_dim.64
  63.6 3.8 %all-to-all-start.3 = ((f32[32,2,160]{2,1,0:T(2,128)}), f32[32,2,160]{2,1,0:T(2,128)S(1)}, u32[]{:S(2)}, u32[]{:S(2)}) async-start(f32[32,2,160]{2,1,0:T(2,128)} %broadcast_in_dim.64), calls=%async_computation.3 | async-start | bytes 131072 | tf_op jit(solution)/shard_map/all_to_all | solution.py:25
  67.4 0.7 broadcast_in_dim.56
  68.1 0.7 add_maximum_fusion.ids
  68.7 9.9 %all-to-all-done.3 = f32[32,2,160]{2,1,0:T(2,128)S(1)} async-done(((f32[32,2,160]{2,1,0:T(2,128)}), f32[32,2,160]{2,1,0:T(2,128)S(1)}, u32[]{:S(2)}, u32[]{:S(2)}) %all-to-all-start.3) | async-done | bytes 40992 | tf_op jit(solution)/shard_map/all_to_all | solution.py:25
  78.7 4.8 %all_to_all.32 = f32[2,1,160]{2,1,0:T(1,128)S(1)} all-to-all(f32[2,1,160]{2,1,0:T(1,128)S(1)} %broadcast_in_dim.65), channel_id=1, replica_groups=mesh['y'=8,'zh'=4,'core'=2,'kvh'=8] {'core'}, dimensions={0} | all-to-all | bytes 2560 | tf_op jit(solution)/shard_map/all_to_all | solution.py:25
  84.4 4.5 %all-to-all-start.5 = ((f32[8,1,256]{2,1,0:T(1,128)}), f32[8,1,256]{2,1,0:T(1,128)S(1)}, u32[]{:S(2)}, u32[]{:S(2)}) async-start(f32[8,1,256]{2,1,0:T(1,128)} %broadcast_in_dim.66), calls=%async_computation.5 | async-start | bytes 16384 | tf_op jit(solution)/shard_map/all_to_all | solution.py:25
  89.0 6.0 %all-to-all-done.5 = f32[8,1,256]{2,1,0:T(1,128)S(1)} async-done(((f32[8,1,256]{2,1,0:T(1,128)}), f32[8,1,256]{2,1,0:T(1,128)S(1)}, u32[]{:S(2)}, u32[]{:S(2)}) %all-to-all-start.5) | async-done | bytes 8224 | tf_op jit(solution)/shard_map/all_to_all | solution.py:25
  95.6 27.6 %all-gather.5.cloned.1.call-done = bf16[128,256,128]{2,1,0:T(8,128)(2,1)} async-done(((bf16[2,256,128]{2,1,0:T(8,128)(2,1)}), bf16[128,256,128]{2,1,0:T(8,128)(2,1)}) %all-gather.5.cloned.1.call-update) | async-done | bytes 8388624 | tf_op jit(solution)/shard_map/all_gather | solution.py:156
  123.2 0.7 broadcast_in_dim.59
  123.9 14.5 %shard_map.68 = bf16[5,256,128]{2,1,0:T(8,128)(2,1)} custom-call(s32[2,24]{1,0:T(2,128)} %add_maximum_fusion.ids, f32[2,1,3072]{2,1,0:T(1,128)} %bitcast.61, bf16[5,256,128]{2,1,0:T(8,128)(2,1)} %bitcast.59, bf16[64,2,256,128]{3,2,1,0:T(8,128)(2,1)} %bitcast.57), custom_call_target="tpu_custom_call" | custom-call | flops 2013265920 | bytes 4194304 | tf_op jit(solution)/shard_map/pallas_call | solution.py:115
  (33 shorter events, 3.6 us)
Async XLA Ops:
  7.2 116.1 %all-gather.5.cloned.1.call-start = ((), (), s32[]{:S(2)}) async-start(), calls=%async_computation.6 | async-start | bytes 8519680 | tf_op jit(solution)/shard_map/all_gather | solution.py:156
  10.3 15.1 %all-to-all-start = ((bf16[8,40,128]{2,1,0:T(8,128)(2,1)}), bf16[8,40,128]{2,1,0:T(8,128)(2,1)S(1)}, u32[]{:S(2)}, u32[]{:S(2)}) async-start(bf16[8,40,128]{2,1,0:T(8,128)(2,1)} %bitcast.9), calls=%async_computation | async-start | bytes 163840 | tf_op jit(solution)/shard_map/all_to_all | solution.py:33
  26.0 20.3 %all-to-all-start.1 = ((bf16[8,40,128]{2,1,0:T(8,128)(2,1)}), bf16[8,40,128]{2,1,0:T(8,128)(2,1)S(1)}, u32[]{:S(2)}, u32[]{:S(2)}) async-start(bf16[8,40,128]{2,1,0:T(8,128)(2,1)} %broadcast_in_dim.61), calls=%async_computation.1 | async-start | bytes 163840 | tf_op jit(solution)/shard_map/all_to_all | solution.py:25
  47.0 11.3 %all-to-all-start.2 = ((bf16[8,40,128]{2,1,0:T(8,128)(2,1)}), bf16[8,40,128]{2,1,0:T(8,128)(2,1)S(1)}, u32[]{:S(2)}, u32[]{:S(2)}) async-start(bf16[8,40,128]{2,1,0:T(8,128)(2,1)} %broadcast_in_dim.62), calls=%async_computation.2 | async-start | bytes 163840 | tf_op jit(solution)/shard_map/all_to_all | solution.py:25
  63.6 15.0 %all-to-all-start.3 = ((f32[32,2,160]{2,1,0:T(2,128)}), f32[32,2,160]{2,1,0:T(2,128)S(1)}, u32[]{:S(2)}, u32[]{:S(2)}) async-start(f32[32,2,160]{2,1,0:T(2,128)} %broadcast_in_dim.64), calls=%async_computation.3 | async-start | bytes 131072 | tf_op jit(solution)/shard_map/all_to_all | solution.py:25
  84.4 10.6 %all-to-all-start.5 = ((f32[8,1,256]{2,1,0:T(1,128)}), f32[8,1,256]{2,1,0:T(1,128)S(1)}, u32[]{:S(2)}, u32[]{:S(2)}) async-start(f32[8,1,256]{2,1,0:T(1,128)} %broadcast_in_dim.66), calls=%async_computation.5 | async-start | bytes 16384 | tf_op jit(solution)/shard_map/all_to_all | solution.py:25
Sparse Core Ops, SparseCore 0:
  11.9 111.3 all-gather.4

commit v2 on v1

v2 whole, which is shorter than its diff:
```python
import functools
import math

import jax
import jax.numpy as jnp
from jax import lax
from jax.experimental import pallas as pl
from jax.experimental.pallas import tpu as pltpu
from jax.sharding import Mesh
from jax.sharding import PartitionSpec as P

BLK = 128
LAST = 64
NV = 16
NS = 8
HEADS = 40
HD = 128
GROUP = 5
FAR = -1e30
LOG2E = math.log2(math.e)
C = ("zh", "core")
CTX = ("y", "zh", "core")
NY, NZ = 8, 4
PER_ROW = 2 * NZ
PIECE = BLK // NY
LISTED = NV * PIECE
QROWS = 48
QALL = NY * QROWS
QREAL = GROUP * LAST
NT = (((1,), (1,)), ((), ()))
SMEM = pl.BlockSpec(memory_space=pltpu.SMEM)
VMEM = pl.BlockSpec(memory_space=pltpu.VMEM)
ANY = pl.BlockSpec(memory_space=pl.ANY)
F32 = jnp.float32
BF16 = jnp.bfloat16
LARGE = pltpu.CompilerParams(vmem_limit_bytes=60 * 1024 * 1024)
SMALL = pltpu.CompilerParams(vmem_limit_bytes=8 * 1024 * 1024)


def shape(kind, *dims):
    return jax.ShapeDtypeStruct(dims, kind)


def exchange(x, axis):
    return lax.all_to_all(x, axis, 0, 0)


def pack_kernel(q, k, v, sent, kv, last, sem):
    local = k.shape[0]
    copy = pltpu.make_async_copy(q.at[:, pl.ds(local - LAST, LAST)], last, sem)
    copy.start()
    for which, x in enumerate((k, v)):
        kv[which] = x[...]
        for y in range(NY):
            for b in range(2):
                sent[2 * y + which, b * PIECE : (b + 1) * PIECE, :] = x[b * BLK + y * PIECE : b * BLK + (y + 1) * PIECE, :]
    copy.wait()
    flat = last[...].reshape(QREAL, HD)
    flat = jnp.concatenate([flat, jnp.zeros((QALL - QREAL, HD), BF16)], axis=0)
    for d in range(2 * NY):
        sent[d, 2 * PIECE :, :] = flat[d // 2 * QROWS : (d // 2 + 1) * QROWS]


def pack(q_t, k, v):
    return pl.pallas_call(
        pack_kernel,
        out_shape=(shape(BF16, 2 * NY, 2 * PIECE + QROWS, HD), shape(BF16, 2, *k.shape)),
        in_specs=[ANY, VMEM, VMEM],
        out_specs=(VMEM, VMEM),
        scratch_shapes=[pltpu.VMEM((GROUP, LAST, HD), BF16), pltpu.SemaphoreType.DMA],
        compiler_params=LARGE,
    )(q_t, k, v)


def pick_kernel(ids, zh, r, after, out):
    for j in range(NV):
        c = ids[0, j]
        source = (c // 16) * 2 + (c // 2) % 2
        tile = r[source, pl.ds(pl.multiple_of((c % 2) * PIECE, PIECE), PIECE), :]
        tile = jnp.where((c // 4) % NZ == zh[0], tile, jnp.zeros_like(tile))
        for d in range(NZ):
            out[d, j * PIECE : (j + 1) * PIECE, :] = tile
    for d in range(NZ):
        out[d, LISTED:, :] = r[2 * NY - 1, 2 * PIECE :, :]


def pick(vertical, zh, r, after):
    return pl.pallas_call(
        pick_kernel,
        out_shape=shape(BF16, NZ, LISTED + QROWS, HD),
        in_specs=[SMEM, SMEM, VMEM, ANY],
        out_specs=VMEM,
        compiler_params=SMALL,
    )(vertical, zh, r, after)


def merge_kernel(r, out):
    whole = r[0, :LISTED, :]
    for z in range(1, NZ):
        whole = whole + r[z, :LISTED, :]
    for d in range(NY):
        out[d, :LISTED, :] = whole
        out[d, LISTED:, :] = r[NZ - 1, LISTED:, :]


def merge(r):
    return pl.pallas_call(merge_kernel, out_shape=shape(BF16, NY, LISTED + QROWS, HD), in_specs=[VMEM], out_specs=VMEM, compiler_params=SMALL)(r)


def estimate_kernel(total_len, position, r, k, scores, stats):
    local = k.shape[0]
    q = r[:, LISTED:, :].reshape(QALL, HD)
    s = lax.dot_general(k[...], q, NT, preferred_element_type=F32) * (1.0 / math.sqrt(HD))
    key_pos = position[0] * local + lax.broadcasted_iota(jnp.int32, (local, QALL), 0)
    last_pos = total_len - LAST + lax.broadcasted_iota(jnp.int32, (local, QALL), 1) % LAST
    s = jnp.where(key_pos <= last_pos, s, FAR)
    scores[...] = s
    top = jnp.max(s, axis=0, keepdims=True)
    total = jnp.sum(jnp.exp(s - top), axis=0, keepdims=True)
    both = jnp.concatenate([top, total], axis=0)
    for d in range(2 * NY):
        stats[d] = both


def estimate(position, r, k, total_len):
    local = k.shape[0]
    return pl.pallas_call(
        functools.partial(estimate_kernel, total_len),
        out_shape=(shape(F32, local, QALL), shape(F32, 2 * NY, 2, QALL)),
        in_specs=[SMEM, VMEM, VMEM],
        out_specs=(VMEM, VMEM),
        compiler_params=SMALL,
    )(position, r, k)


def joined(stats):
    n = stats.shape[0]
    top = stats[0, 0:1, :]
    for i in range(1, n):
        top = jnp.maximum(top, stats[i, 0:1, :])
    total = jnp.zeros_like(top)
    for i in range(n):
        total += stats[i, 1:2, :] * jnp.exp(stats[i, 0:1, :] - top)
    return top, total


def join_kernel(stats, after, out):
    both = jnp.concatenate(joined(stats), axis=0)
    for d in range(NZ):
        out[d] = both


def join(stats, after):
    return pl.pallas_call(join_kernel, out_shape=shape(F32, NZ, 2, QALL), in_specs=[VMEM, ANY], out_specs=VMEM, compiler_params=SMALL)(stats, after)


def mass_kernel(stats, scores, after, out):
    top, total = joined(stats)
    p = jnp.exp(scores[...] - (top + jnp.log(total)))
    real = (lax.broadcasted_iota(jnp.int32, (out.shape[0], QALL), 1) < QREAL).astype(F32)
    out[:, 0, :] = lax.dot_general(real, p, NT, precision=lax.Precision.HIGHEST, preferred_element_type=F32)


def mass(stats, scores, after, kvh):
    return pl.pallas_call(
        mass_kernel,
        out_shape=shape(F32, kvh, 1, scores.shape[0]),
        in_specs=[VMEM, VMEM, ANY],
        out_specs=VMEM,
        compiler_params=SMALL,
    )(stats, scores, after)


def attend_kernel(first, count, places, core, bias, q, mine, theirs, rows, earlier, *rest):
    if first:
        rest = rest[1:]
    out, token, q_buf, k_vert, v_vert, k_near, v_near, s_buf, o_buf, sems = rest
    token[...] = jnp.zeros_like(token)
    copies = []
    sem = lambda: sems.at[len(copies)]

    copies.append(pltpu.make_async_copy(q.at[pl.ds(first, count)], q_buf, sem()))
    copies[-1].start()
    for e in range(2):
        for j in range(NS):
            place = places[e, j]
            row = pl.ds(pl.multiple_of((place % 2) * BLK, BLK), BLK)
            for which, target in ((0, k_near), (1, v_near)):
                target = target.at[e, pl.ds(j * BLK, BLK)]
                copy = pltpu.make_async_copy(rows.at[place // 4, which, row], target, sem())
                other = pltpu.make_async_copy(earlier.at[place // 4, which, row], target, sem())
                pl.when((place // 2) % 2 == 0)(copy.start)
                pl.when((place // 2) % 2 == 1)(other.start)
                copies.append(copy)
    for which, target in ((0, k_vert), (1, v_vert)):
        copy = pltpu.make_async_copy(mine.at[:, pl.ds(0, LISTED)], target, sem())
        other = pltpu.make_async_copy(theirs.at[:, pl.ds(0, LISTED)], target, sem())
        pl.when(core[0] == which)(copy.start)
        pl.when(core[0] != which)(other.start)
        copies.append(copy)
    for copy in copies:
        copy.wait()

    factor = LOG2E / math.sqrt(HD)
    width_near = NS * BLK
    causal = lax.broadcasted_iota(jnp.int32, (BLK, BLK), 1) <= lax.broadcasted_iota(jnp.int32, (BLK, BLK), 0)

    def scores(i):
        e, h = i % 2, i // 2
        tile = q_buf[h, pl.ds(pl.multiple_of(e * BLK, BLK), BLK), :]
        a = lax.dot_general(tile, k_near[e], NT, preferred_element_type=F32) * factor + bias[e, :, :width_near]
        a = jnp.concatenate([jnp.where(causal, a[:, :BLK], FAR), a[:, BLK:]], axis=1)
        keys = k_vert[...].reshape(NV * BLK, HD)
        b = lax.dot_general(tile, keys, NT, preferred_element_type=F32) * factor + bias[e, :, width_near:]
        s_buf[i % 2, :, :width_near] = a
        s_buf[i % 2, :, width_near:] = b
        return jnp.maximum(jnp.max(a, axis=1, keepdims=True), jnp.max(b, axis=1, keepdims=True))

    def finish(i, top):
        e, h = i % 2, i // 2
        p = jnp.exp2(s_buf[i % 2] - top)
        total = jnp.sum(p, axis=1, keepdims=True)
        w = p.astype(BF16)
        o = jnp.dot(w[:, :width_near], v_near[e], preferred_element_type=F32)
        o += jnp.dot(w[:, width_near:], v_vert[...].reshape(NV * BLK, HD), preferred_element_type=F32)
        o_buf[h, pl.ds(pl.multiple_of(e * BLK, BLK), BLK), :] = (o / total).astype(BF16)

    def step(i, top):
        later = scores(i + 1)
        finish(i, top)
        return later

    tiles = 2 * count
    top = lax.fori_loop(0, tiles - 1, step, scores(0))
    finish(tiles - 1, top)
    copy = pltpu.make_async_copy(o_buf, out.at[pl.ds(first, count)], sems.at[0])
    copy.start()
    copy.wait()


def attend(first, count, places, core, bias, q_t, mine, theirs, rows, earlier, out=None):
    local = q_t.shape[1]
    args = (places, core, bias, q_t, mine, theirs, rows, earlier) + ((out,) if first else ())
    return pl.pallas_call(
        functools.partial(attend_kernel, first, count),
        out_shape=(shape(BF16, GROUP, local, HD), shape(F32, 8, 128)),
        in_specs=[SMEM, SMEM, VMEM] + [ANY] * (len(args) - 3),
        out_specs=(ANY, VMEM),
        scratch_shapes=[
            pltpu.VMEM((count, local, HD), BF16),
            pltpu.VMEM((NY, LISTED, HD), BF16),
            pltpu.VMEM((NY, LISTED, HD), BF16),
            pltpu.VMEM((2, NS * BLK, HD), BF16),
            pltpu.VMEM((2, NS * BLK, HD), BF16),
            pltpu.VMEM((2, BLK, (NV + NS) * BLK), F32),
            pltpu.VMEM((count, local, HD), BF16),
            pltpu.SemaphoreType.DMA((4 * NS + 3,)),
        ],
        input_output_aliases={len(args) - 1: 0} if first else {},
        compiler_params=LARGE,
        cost_estimate=pl.CostEstimate(
            flops=4 * 2 * count * (NV + NS) * BLK**3, bytes_accessed=4 * 1024 * 1024, transcendentals=2 * count * (NV + NS) * BLK**2
        ),
    )(*args)


def lists(vertical, slash_offsets, position):
    own = (position * 2 + jnp.arange(2, dtype=jnp.int32))[:, None]
    slash = slash_offsets[0]
    others = jnp.where(slash[1:] == 0, slash[0], slash[1:])
    near = own - jnp.concatenate([jnp.zeros((1,), jnp.int32), others])[None, :]
    far = jnp.broadcast_to(vertical[0][None, :], (2, NV))
    again = jnp.any(far[:, :, None] == near[:, None, :], axis=-1)
    usable = jnp.concatenate([near >= 0, (far <= own) & jnp.logical_not(again)], axis=1)
    bias = jnp.where(usable, 0.0, FAR).astype(F32)
    by_near = jnp.broadcast_to(bias[:, None, :NS, None], (2, 1, NS, BLK)).reshape(2, 1, NS * BLK)
    by_far = jnp.broadcast_to(bias[:, None, None, NS:, None], (2, 1, NY, NV, PIECE)).reshape(2, 1, NV * BLK)
    bias = jnp.concatenate([by_near, by_far], axis=2)
    kept = jnp.maximum(near, 0)
    before = (kept // 2 // PER_ROW != position // PER_ROW).astype(jnp.int32)
    places = ((kept // 2) % PER_ROW * 2 + before) * 2 + kept % 2
    return places, bias


def on_device(queries, key_rows, value_rows, vertical, slash_offsets):
    local = key_rows.shape[0]
    total_len = local * NY * PER_ROW
    zh, core = lax.axis_index("zh"), lax.axis_index("core")
    position = (lax.axis_index("y") * NZ + zh) * 2 + core
    q_t = jnp.transpose(queries, (1, 0, 2))
    k, v = key_rows[:, 0], value_rows[:, 0]

    sent, kv = pack(q_t, k, v)
    before = lax.ppermute(kv, "y", [(i, (i + 1) % NY) for i in range(NY)])
    rows, earlier = lax.all_gather(kv, C), lax.all_gather(before, C)
    r = exchange(sent, ("y", "core"))
    r = exchange(pick(vertical, zh.reshape(1), r, before), "zh")
    mine = exchange(merge(r), "y")
    theirs = lax.ppermute(mine, "core", [(0, 1), (1, 0)])
    scores, stats = estimate(position.reshape(1), mine, k, total_len)

    places, bias = lists(vertical, slash_offsets, position)
    given = (places, core.reshape(1), bias, q_t, mine, theirs, rows, earlier)
    out, token = attend(0, 2, *given)
    stats = exchange(join(exchange(stats, ("y", "core")), token), "zh")
    out, token = attend(2, 2, *given, out)
    part = exchange(mass(stats, scores, token, lax.axis_size("kvh")), "kvh")
    out, token = attend(4, 1, *given, out)
    profile = jnp.sum(part, axis=(0, 1)) * (total_len / LAST / HEADS)
    return jnp.transpose(out, (1, 0, 2)), profile


def solution(mesh):
    wide = Mesh(mesh.devices.reshape(NY, NZ, 2, -1), ("y", "zh", "core", "kvh"))
    return jax.shard_map(
        on_device,
        mesh=wide,
        in_specs=(P(CTX, "kvh", None), P(CTX, "kvh", None), P(CTX, "kvh", None), P("kvh", None), P("kvh", None)),
        out_specs=(P(CTX, "kvh", None), P(CTX)),
        check_vma=False,
    )
```

time: 146 us -> 133 us (0.911)
  waiting for transfers between devices: 63.5 us -> 36.4 us
  Pallas kernels: 14.5 us -> 29.4 us
  starting transfers between devices: 32 us -> 45.1 us
  blocking collectives: 7.84 us -> 0 us
  other arithmetic: 6.52 us -> 2.39 us
    all_gather x1 -> x2, waiting for transfers between devices: 27.6 us -> 0.01 us  [on_device(): rows, earlier = (lax.all_gather(kv, C), lax.all_gather(before, C))]
    pallas_call x1 -> x9, Pallas kernels: 14.5 us -> 29.4 us  [the longest x3 21.8 us: attend(): pl.pallas_call(functools.partial(attend_kernel, first, count), out_shape=...]
    all_to_all x5 -> x6, waiting for transfers between devices: 35.9 us -> 25.4 us  [exchange(): return lax.all_to_all(x, axis, 0, 0)]
    ppermute x0 -> x2, waiting for transfers between devices: none -> 10.2 us  [the longest x1 10.2 us: on_device(): before = lax.ppermute(kv, 'y', [(i, (i + 1) % NY) for i in range(NY)])]
    ppermute x0 -> x2, starting transfers between devices: none -> 7.31 us  [the longest x1 4.01 us: on_device(): theirs = lax.ppermute(mine, 'core', [(0, 1), (1, 0)])]
    all_to_all x5 -> x6, starting transfers between devices: 32 us -> 37.7 us  [exchange(): return lax.all_to_all(x, axis, 0, 0)]
    all_to_all x1 -> x0, blocking collectives: 4.84 us -> none  [spread(): return lax.all_to_all(jnp.broadcast_to(x, (n,) + x.shape), axis, 0, 0)]
    unnamed x1 -> x18, local copies, waits for them, and re-layouts: 0.01 us -> 4.18 us
  transfers between devices with their start and end apart: 6 -> 10, of which waited for: 6 -> 3; matrix products, arithmetic and copies ran while one was open for 8% -> 2% of each run, Pallas kernels for 0% -> 19%
where the time goes in v2:
time: 133 us; the launch traced here: 132 us
  starting transfers between devices  45.1 us (34%)
  waiting for transfers between devices  36.4 us (27%)
  Pallas kernels  29.4 us (22%)
  between operations  14.2 us (11%)
  local copies, waits for them, and re-layouts  4.51 us (3%)
  other arithmetic  2.39 us (2%)
    all_to_all x6, starting transfers between devices, exchange(): return lax.all_to_all(x, axis, 0, 0)  37.7 us
    all_to_all x6, waiting for transfers between devices, exchange(): return lax.all_to_all(x, axis, 0, 0)  25.4 us
    pallas_call x3, Pallas kernels, attend(): pl.pallas_call(functools.partial(attend_kernel, first, count), out_shape=...  21.8 us
    ppermute x1, waiting for transfers between devices, on_device(): before = lax.ppermute(kv, 'y', [(i, (i + 1) % NY) for i in range(NY)])  10.2 us
    unnamed x18, local copies, waits for them, and re-layouts  4.18 us
    ppermute x1, starting transfers between devices, on_device(): theirs = lax.ppermute(mine, 'core', [(0, 1), (1, 0)])  4.01 us
    ppermute x1, starting transfers between devices, on_device(): before = lax.ppermute(kv, 'y', [(i, (i + 1) % NY) for i in range(NY)])  3.3 us
  transfers between devices with their start and end apart: 10, of which 3 were waited for; matrix products, arithmetic and copies ran while one was open for 2% of the time, Pallas kernels for 19%

profile of v2, /device:TPU:1, one launch (start us, length us, event | category | flops | bytes accessed | tf_op | source)
XLA Modules:
  0.0 131.9 jit_solution(11397982019504915745)
XLA Ops:
  7.2 2.5 %shard_map.68 = (bf16[16,80,128]{2,1,0:T(8,128)(2,1)}, bf16[2,256,128]{2,1,0:T(8,128)(2,1)}) custom-call(bf16[5,256,128]{2,1,0:T(8,128)(2,1)} %bitcast.28, bf16[256,128]{1,0:T(8,128)(2,1)} %bitcast.18, bf16[256,128]{1,0:T(8,128)(2,1)} %bitcast.33), custom_call_target="tpu_custom_call" | custom-call | tf_op jit(solution)/shard_map/pallas_call | solution.py:65
  9.8 10.4 %all-to-all-start = ((bf16[16,80,128]{2,1,0:T(8,128)(2,1)}), bf16[16,80,128]{2,1,0:T(8,128)(2,1)S(1)}, u32[]{:S(2)}, u32[]{:S(2)}) async-start(bf16[16,80,128]{2,1,0:T(8,128)(2,1)} %get-tuple-element.11), calls=%async_computation | async-start | bytes 655360 | tf_op jit(solution)/shard_map/all_to_all | solution.py:45
  20.1 3.3 %collective-permute-start = (bf16[2,256,128]{2,1,0:T(8,128)(2,1)S(1)}, bf16[2,256,128]{2,1,0:T(8,128)(2,1)S(1)}, u32[]{:S(2)}, u32[]{:S(2)}) collective-permute-start(bf16[2,256,128]{2,1,0:T(8,128)(2,1)S(1)} %copy-done.7), channel_id=1, source_target_pairs={{0,64},{64,128},{128,192},{192,256},{256,320},{320,384},{384,448},... | collective-permute-start | bytes 393224 | tf_op jit(solution)/shard_map/ppermute | solution.py:294
  23.5 10.2 %collective-permute-done.after = bf16[2,256,128]{2,1,0:T(8,128)(2,1)S(1)} collective-permute-done((bf16[2,256,128]{2,1,0:T(8,128)(2,1)S(1)}, bf16[2,256,128]{2,1,0:T(8,128)(2,1)S(1)}, u32[]{:S(2)}, u32[]{:S(2)}) %collective-permute-start) | collective-permute-done | bytes 131104 | tf_op jit(solution)/shard_map/ppermute | solution.py:294
  34.3 1.6 %shard_map.69 = bf16[4,304,128]{2,1,0:T(8,128)(2,1)} custom-call(s32[1,16]{1,0:T(1,128)S(1)} %copy-done.3, s32[1]{0:T(128)} %bitcast.6.zh, bf16[16,80,128]{2,1,0:T(8,128)(2,1)S(1)} %all-to-all-done.r, bf16[2,256,128]{2,1,0:T(8,128)(2,1)S(1)} %collective-permute-done.after), custom_call_target="tpu_custom_call" | custom-call | tf_op jit(solution)/shard_map/pallas_call | solution.py:88
  35.8 8.4 %all-to-all-start.1 = ((bf16[4,304,128]{2,1,0:T(8,128)(2,1)}), bf16[4,304,128]{2,1,0:T(8,128)(2,1)S(1)}, u32[]{:S(2)}, u32[]{:S(2)}) async-start(bf16[4,304,128]{2,1,0:T(8,128)(2,1)} %shard_map.69), calls=%async_computation.1 | async-start | bytes 622592 | tf_op jit(solution)/shard_map/all_to_all | solution.py:45
  44.3 0.7 all-gather.7.cloned.1.call-update
  45.0 8.7 %all-to-all-done.1.r = bf16[4,304,128]{2,1,0:T(8,128)(2,1)S(1)} async-done(((bf16[4,304,128]{2,1,0:T(8,128)(2,1)}), bf16[4,304,128]{2,1,0:T(8,128)(2,1)S(1)}, u32[]{:S(2)}, u32[]{:S(2)}) %all-to-all-start.1) | async-done | bytes 311328 | tf_op jit(solution)/shard_map/all_to_all | solution.py:45
  53.7 0.9 shard_map.70
  54.6 7.0 %all-to-all-start.2 = ((bf16[8,304,128]{2,1,0:T(8,128)(2,1)}), bf16[8,304,128]{2,1,0:T(8,128)(2,1)S(1)}, u32[]{:S(2)}, u32[]{:S(2)}) async-start(bf16[8,304,128]{2,1,0:T(8,128)(2,1)} %shard_map.70), calls=%async_computation.2 | async-start | bytes 1245184 | tf_op jit(solution)/shard_map/all_to_all | solution.py:45
  63.3 16.8 %all-to-all-done.2.mine.r = bf16[8,304,128]{2,1,0:T(8,128)(2,1)S(1)} async-done(((bf16[8,304,128]{2,1,0:T(8,128)(2,1)}), bf16[8,304,128]{2,1,0:T(8,128)(2,1)S(1)}, u32[]{:S(2)}, u32[]{:S(2)}) %all-to-all-start.2) | async-done | bytes 622624 | tf_op jit(solution)/shard_map/all_to_all | solution.py:45
  80.0 4.0 %collective-permute-start.1 = (bf16[8,304,128]{2,1,0:T(8,128)(2,1)S(1)}, bf16[8,304,128]{2,1,0:T(8,128)(2,1)S(1)}, u32[]{:S(2)}, u32[]{:S(2)}) collective-permute-start(bf16[8,304,128]{2,1,0:T(8,128)(2,1)S(1)} %all-to-all-done.2.mine.r), channel_id=1, source_target_pairs={{0,8},{8,0},{1,9},{9,1},{2,10},{10,2},{3,11},{11,3},{4,12},{12,4},... | collective-permute-start | bytes 1867784 | tf_op jit(solution)/shard_map/ppermute | solution.py:299
  84.5 0.7 copy-done.2
  85.2 0.9 shard_map.74
  86.1 3.4 %all-to-all-start.3 = ((f32[16,2,384]{2,1,0:T(2,128)}), f32[16,2,384]{2,1,0:T(2,128)S(1)}, u32[]{:S(2)}, u32[]{:S(2)}) async-start(f32[16,2,384]{2,1,0:T(2,128)} %get-tuple-element.16), calls=%async_computation.3 | async-start | bytes 98304 | tf_op jit(solution)/shard_map/all_to_all | solution.py:45
  90.3 0.8 copy-done.6
  91.1 8.1 %shard_map.71 = (bf16[5,256,128]{2,1,0:T(8,128)(2,1)}, f32[8,128]{1,0:T(8,128)}) custom-call(s32[2,8]{1,0:T(2,128)} %get-tuple-element.21.places, s32[1]{0:T(128)} %bitcast.2.core, f32[2,1,3072]{2,1,0:T(1,128)} %pad_maximum_fusion.bias, bf16[5,256,128]{2,1,0:T(8,128)(2,1)} %bitcast.29, bf16[8,304,128]{2,1,0:T(8,128)(2,1)} %copy-done, ...), custom_call_target="tpu_custom_call" | custom-call | flops 805306368 | bytes 4194304 | tf_op jit(solution)/shard_map/pallas_call | solution.py:244
  99.2 0.7 copy-done.5
  100.6 3.6 %all-to-all-start.4 = ((f32[4,2,384]{2,1,0:T(2,128)}), f32[4,2,384]{2,1,0:T(2,128)S(1)}, u32[]{:S(2)}, u32[]{:S(2)}) async-start(f32[4,2,384]{2,1,0:T(2,128)} %shard_map.75), calls=%async_computation.4 | async-start | bytes 24576 | tf_op jit(solution)/shard_map/all_to_all | solution.py:45
  104.2 8.1 %shard_map.72 = (bf16[5,256,128]{2,1,0:T(8,128)(2,1)}, f32[8,128]{1,0:T(8,128)}) custom-call(s32[2,8]{1,0:T(2,128)} %get-tuple-element.21.places, s32[1]{0:T(128)} %bitcast.2.core, f32[2,1,3072]{2,1,0:T(1,128)} %pad_maximum_fusion.bias, bf16[5,256,128]{2,1,0:T(8,128)(2,1)} %bitcast.30, ...), custom_call_target="tpu_custom_call", output_to_operand_aliasing={{0}: (8, {})} | custom-call | flops 805306368 | bytes 4194304 | tf_op jit(solution)/shard_map/pallas_call | solution.py:244
  112.3 0.7 copy-done.4
  113.0 1.1 shard_map.76
  114.1 4.9 %all-to-all-start.5 = ((f32[8,1,256]{2,1,0:T(1,128)}), f32[8,1,256]{2,1,0:T(1,128)S(1)}, u32[]{:S(2)}, u32[]{:S(2)}) async-start(f32[8,1,256]{2,1,0:T(1,128)} %shard_map.76), calls=%async_computation.5 | async-start | bytes 16384 | tf_op jit(solution)/shard_map/all_to_all | solution.py:45
  119.0 5.5 %shard_map.73 = (bf16[5,256,128]{2,1,0:T(8,128)(2,1)}, f32[8,128]{1,0:T(8,128)}) custom-call(s32[2,8]{1,0:T(2,128)} %get-tuple-element.21.places, s32[1]{0:T(128)} %bitcast.2.core, f32[2,1,3072]{2,1,0:T(1,128)} %pad_maximum_fusion.bias, bf16[5,256,128]{2,1,0:T(8,128)(2,1)} %bitcast.31, ...), custom_call_target="tpu_custom_call", output_to_operand_aliasing={{0}: (8, {})} | custom-call | flops 402653184 | bytes 4194304 | tf_op jit(solution)/shard_map/pallas_call | solution.py:244
  (40 shorter events, 4.8 us)
Async XLA Ops:
  7.2 83.1 %all-gather.5.cloned.1.call-start = ((), (), s32[]{:S(2)}) async-start(), calls=%async_computation.6 | async-start | bytes 1179648 | tf_op jit(solution)/shard_map/all_gather | solution.py:295
  9.8 10.4 %copy-start.7 = (bf16[2,256,128]{2,1,0:T(8,128)(2,1)S(1)}, bf16[2,256,128]{2,1,0:T(8,128)(2,1)}, u32[]{:S(2)}) copy-start(bf16[2,256,128]{2,1,0:T(8,128)(2,1)} %get-tuple-element.12) | copy-start | bytes 393220
  9.8 23.8 %all-to-all-start = ((bf16[16,80,128]{2,1,0:T(8,128)(2,1)}), bf16[16,80,128]{2,1,0:T(8,128)(2,1)S(1)}, u32[]{:S(2)}, u32[]{:S(2)}) async-start(bf16[16,80,128]{2,1,0:T(8,128)(2,1)} %get-tuple-element.11), calls=%async_computation | async-start | bytes 655360 | tf_op jit(solution)/shard_map/all_to_all | solution.py:45
  20.1 13.5 %collective-permute-start = (bf16[2,256,128]{2,1,0:T(8,128)(2,1)S(1)}, bf16[2,256,128]{2,1,0:T(8,128)(2,1)S(1)}, u32[]{:S(2)}, u32[]{:S(2)}) collective-permute-start(bf16[2,256,128]{2,1,0:T(8,128)(2,1)S(1)} %copy-done.7), channel_id=1, source_target_pairs={{0,64},{64,128},{128,192},{192,256},{256,320},{320,384},{384,448},... | collective-permute-start | bytes 393224 | tf_op jit(solution)/shard_map/ppermute | solution.py:294
  33.6 2.2 %copy-start.1 = (bf16[2,256,128]{2,1,0:T(8,128)(2,1)}, bf16[2,256,128]{2,1,0:T(8,128)(2,1)S(1)}, u32[]{:S(2)}) copy-start(bf16[2,256,128]{2,1,0:T(8,128)(2,1)S(1)} %collective-permute-done.after) | copy-start | bytes 393220
  33.6 0.7 copy-start.3
  35.8 17.8 %all-to-all-start.1 = ((bf16[4,304,128]{2,1,0:T(8,128)(2,1)}), bf16[4,304,128]{2,1,0:T(8,128)(2,1)S(1)}, u32[]{:S(2)}, u32[]{:S(2)}) async-start(bf16[4,304,128]{2,1,0:T(8,128)(2,1)} %shard_map.69), calls=%async_computation.1 | async-start | bytes 622592 | tf_op jit(solution)/shard_map/all_to_all | solution.py:45
  44.3 46.0 %all-gather.7.cloned.1.call-start = ((), (), s32[]{:S(2)}) async-start(), calls=%async_computation.7 | async-start | bytes 1179648 | tf_op jit(solution)/shard_map/all_gather | solution.py:295
  54.6 25.5 %all-to-all-start.2 = ((bf16[8,304,128]{2,1,0:T(8,128)(2,1)}), bf16[8,304,128]{2,1,0:T(8,128)(2,1)S(1)}, u32[]{:S(2)}, u32[]{:S(2)}) async-start(bf16[8,304,128]{2,1,0:T(8,128)(2,1)} %shard_map.70), calls=%async_computation.2 | async-start | bytes 1245184 | tf_op jit(solution)/shard_map/all_to_all | solution.py:45
  61.6 0.7 copy-start.8
  80.0 10.2 %copy-start = (bf16[8,304,128]{2,1,0:T(8,128)(2,1)}, bf16[8,304,128]{2,1,0:T(8,128)(2,1)S(1)}, u32[]{:S(2)}) copy-start(bf16[8,304,128]{2,1,0:T(8,128)(2,1)S(1)} %all-to-all-done.2.mine.r) | copy-start | bytes 1867780
  80.0 10.2 %collective-permute-start.1 = (bf16[8,304,128]{2,1,0:T(8,128)(2,1)S(1)}, bf16[8,304,128]{2,1,0:T(8,128)(2,1)S(1)}, u32[]{:S(2)}, u32[]{:S(2)}) collective-permute-start(bf16[8,304,128]{2,1,0:T(8,128)(2,1)S(1)} %all-to-all-done.2.mine.r), channel_id=1, source_target_pairs={{0,8},{8,0},{1,9},{9,1},{2,10},{10,2},{3,11},{11,3},{4,12},{12,4},... | collective-permute-start | bytes 1867784 | tf_op jit(solution)/shard_map/ppermute | solution.py:299
  84.4 0.8 copy-start.2
  86.1 13.1 %all-to-all-start.3 = ((f32[16,2,384]{2,1,0:T(2,128)}), f32[16,2,384]{2,1,0:T(2,128)S(1)}, u32[]{:S(2)}, u32[]{:S(2)}) async-start(f32[16,2,384]{2,1,0:T(2,128)} %get-tuple-element.16), calls=%async_computation.3 | async-start | bytes 98304 | tf_op jit(solution)/shard_map/all_to_all | solution.py:45
  90.3 0.8 copy-start.6
  99.2 0.7 copy-start.5
  100.6 11.7 %all-to-all-start.4 = ((f32[4,2,384]{2,1,0:T(2,128)}), f32[4,2,384]{2,1,0:T(2,128)S(1)}, u32[]{:S(2)}, u32[]{:S(2)}) async-start(f32[4,2,384]{2,1,0:T(2,128)} %shard_map.75), calls=%async_computation.4 | async-start | bytes 24576 | tf_op jit(solution)/shard_map/all_to_all | solution.py:45
  112.3 0.7 copy-start.4
  114.1 10.4 %all-to-all-start.5 = ((f32[8,1,256]{2,1,0:T(1,128)}), f32[8,1,256]{2,1,0:T(1,128)S(1)}, u32[]{:S(2)}, u32[]{:S(2)}) async-start(f32[8,1,256]{2,1,0:T(1,128)} %shard_map.76), calls=%async_computation.5 | async-start | bytes 16384 | tf_op jit(solution)/shard_map/all_to_all | solution.py:45
Sparse Core Ops, SparseCore 0:
  10.1 39.2 all-gather.4
  51.6 35.8 all-gather.6

commit v3 on v2

--- a/solution.py
+++ b/solution.py
@@ -72,7 +72,7 @@
     )(q_t, k, v)
 
 
-def pick_kernel(ids, zh, r, after, out):
+def pick_kernel(ids, zh, r, out):
     for j in range(NV):
         c = ids[0, j]
         source = (c // 16) * 2 + (c // 2) % 2
@@ -84,17 +84,18 @@
         out[d, LISTED:, :] = r[2 * NY - 1, 2 * PIECE :, :]
 
 
-def pick(vertical, zh, r, after):
+def pick(vertical, zh, r):
     return pl.pallas_call(
         pick_kernel,
         out_shape=shape(BF16, NZ, LISTED + QROWS, HD),
-        in_specs=[SMEM, SMEM, VMEM, ANY],
+        in_specs=[SMEM, SMEM, VMEM],
         out_specs=VMEM,
         compiler_params=SMALL,
-    )(vertical, zh, r, after)
-
-
-def merge_kernel(r, out):
+    )(vertical, zh, r)
+
+
+def merge_kernel(r, kv, after, out, again):
+    again[...] = kv[...]
     whole = r[0, :LISTED, :]
     for z in range(1, NZ):
         whole = whole + r[z, :LISTED, :]
@@ -103,8 +104,34 @@
         out[d, LISTED:, :] = r[NZ - 1, LISTED:, :]
 
 
-def merge(r):
-    return pl.pallas_call(merge_kernel, out_shape=shape(BF16, NY, LISTED + QROWS, HD), in_specs=[VMEM], out_specs=VMEM, compiler_params=SMALL)(r)
+def merge(r, kv, after):
+    return pl.pallas_call(
+        merge_kernel,
+        out_shape=(shape(BF16, NY, LISTED + QROWS, HD), shape(BF16, *kv.shape)),
+        in_specs=[VMEM, VMEM, ANY],
+        out_specs=(VMEM, VMEM),
+        compiler_params=SMALL,
+    )(r, kv, after)
+
+
+def together_kernel(*refs):
+    *parts, out, sems = refs
+    copies = [pltpu.make_async_copy(part, out.at[i], sems.at[i]) for i, part in enumerate(parts)]
+    for copy in copies:
+        copy.start()
+    for copy in copies:
+        copy.wait()
+
+
+def together(parts):
+    return pl.pallas_call(
+        together_kernel,
+        out_shape=shape(BF16, len(parts), *parts[0].shape),
+        in_specs=[ANY] * len(parts),
+        out_specs=ANY,
+        scratch_shapes=[pltpu.SemaphoreType.DMA((len(parts),))],
+        compiler_params=SMALL,
+    )(*parts)
 
 
 def estimate_kernel(total_len, position, r, k, scores, stats):
@@ -171,7 +198,7 @@
     )(stats, scores, after)
 
 
-def attend_kernel(first, count, places, core, bias, q, mine, theirs, rows, earlier, *rest):
+def attend_kernel(first, count, places, core, bias, q, mine, theirs, near, near_theirs, *rest):
     if first:
         rest = rest[1:]
     out, token, q_buf, k_vert, v_vert, k_near, v_near, s_buf, o_buf, sems = rest
@@ -187,10 +214,10 @@
             row = pl.ds(pl.multiple_of((place % 2) * BLK, BLK), BLK)
             for which, target in ((0, k_near), (1, v_near)):
                 target = target.at[e, pl.ds(j * BLK, BLK)]
-                copy = pltpu.make_async_copy(rows.at[place // 4, which, row], target, sem())
-                other = pltpu.make_async_copy(earlier.at[place // 4, which, row], target, sem())
-                pl.when((place // 2) % 2 == 0)(copy.start)
-                pl.when((place // 2) % 2 == 1)(other.start)
+                copy = pltpu.make_async_copy(near.at[place // 4, which, row], target, sem())
+                other = pltpu.make_async_copy(near_theirs.at[place // 4, which, row], target, sem())
+                pl.when((place // 2) % 2 == core[0])(copy.start)
+                pl.when((place // 2) % 2 != core[0])(other.start)
                 copies.append(copy)
     for which, target in ((0, k_vert), (1, v_vert)):
         copy = pltpu.make_async_copy(mine.at[:, pl.ds(0, LISTED)], target, sem())
@@ -238,9 +265,9 @@
     copy.wait()
 
 
-def attend(first, count, places, core, bias, q_t, mine, theirs, rows, earlier, out=None):
+def attend(first, count, places, core, bias, q_t, mine, theirs, near, near_theirs, out=None):
     local = q_t.shape[1]
-    args = (places, core, bias, q_t, mine, theirs, rows, earlier) + ((out,) if first else ())
+    args = (places, core, bias, q_t, mine, theirs, near, near_theirs) + ((out,) if first else ())
     return pl.pallas_call(
         functools.partial(attend_kernel, first, count),
         out_shape=(shape(BF16, GROUP, local, HD), shape(F32, 8, 128)),
@@ -276,9 +303,8 @@
     by_near = jnp.broadcast_to(bias[:, None, :NS, None], (2, 1, NS, BLK)).reshape(2, 1, NS * BLK)
     by_far = jnp.broadcast_to(bias[:, None, None, NS:, None], (2, 1, NY, NV, PIECE)).reshape(2, 1, NV * BLK)
     bias = jnp.concatenate([by_near, by_far], axis=2)
-    kept = jnp.maximum(near, 0)
-    before = (kept // 2 // PER_ROW != position // PER_ROW).astype(jnp.int32)
-    places = ((kept // 2) % PER_ROW * 2 + before) * 2 + kept % 2
+    kept = jnp.where(near >= 0, near, own)
+    places = (position // 2 - kept // 4) * 4 + kept % 4
     return places, bias
 
 
@@ -291,16 +317,20 @@
     k, v = key_rows[:, 0], value_rows[:, 0]
 
     sent, kv = pack(q_t, k, v)
-    before = lax.ppermute(kv, "y", [(i, (i + 1) % NY) for i in range(NY)])
-    rows, earlier = lax.all_gather(kv, C), lax.all_gather(before, C)
+    back = lambda x, chips: lax.ppermute(x, ("y", "zh"), [(i, (i + chips) % (NY * NZ)) for i in range(NY * NZ)])
+    other_core = [(0, 1), (1, 0)]
+    four = back(kv, 4)
     r = exchange(sent, ("y", "core"))
-    r = exchange(pick(vertical, zh.reshape(1), r, before), "zh")
-    mine = exchange(merge(r), "y")
-    theirs = lax.ppermute(mine, "core", [(0, 1), (1, 0)])
+    r = exchange(pick(vertical, zh.reshape(1), r), "zh")
+    whole, kv = merge(r, kv, four)
+    mine = exchange(whole, "y")
+    near = together([kv, back(kv, 1), back(kv, 2), back(kv, 3), four])
+    near_theirs = lax.ppermute(near, "core", other_core)
+    theirs = lax.ppermute(mine, "core", other_core)
     scores, stats = estimate(position.reshape(1), mine, k, total_len)
 
     places, bias = lists(vertical, slash_offsets, position)
-    given = (places, core.reshape(1), bias, q_t, mine, theirs, rows, earlier)
+    given = (places, core.reshape(1), bias, q_t, mine, theirs, near, near_theirs)
     out, token = attend(0, 2, *given)
     stats = exchange(join(exchange(stats, ("y", "core")), token), "zh")
     out, token = attend(2, 2, *given, out)

time: 133 us -> 133 us (level)
  starting transfers between devices: 45.1 us -> 63.6 us
  between operations: 14.2 us -> 0.89 us
  waiting for transfers between devices: 36.4 us -> 30 us
    ppermute x2 -> x6, starting transfers between devices: 7.31 us -> 21 us  [the longest x4 14.1 us: on_device(): lax.ppermute(x, ('y', 'zh'), [(i, (i + chips) % (NY * NZ)) for i in range...]
    all_to_all x6, waiting for transfers between devices: 25.4 us -> 16.3 us  [exchange(): return lax.all_to_all(x, axis, 0, 0)]
    all_to_all x6, starting transfers between devices: 37.7 us -> 42.6 us  [exchange(): return lax.all_to_all(x, axis, 0, 0)]
    ppermute x2 -> x6, waiting for transfers between devices: 10.2 us -> 13.7 us  [the longest x4 13.7 us: on_device(): lax.ppermute(x, ('y', 'zh'), [(i, (i + chips) % (NY * NZ)) for i in range...]
    unnamed x18 -> x20, local copies, waits for them, and re-layouts: 4.18 us -> 3.76 us
  transfers between devices with their start and end apart: 10 -> 12, of which waited for: 3 -> 6; matrix products, arithmetic and copies ran while one was open for 2% -> 2% of each run, Pallas kernels for 19% -> 18%
where the time goes in v3:
time: 133 us; the launch traced here: 131 us
  starting transfers between devices  63.6 us (48%)
  Pallas kernels  30.3 us (23%)
  waiting for transfers between devices  30 us (23%)
  local copies, waits for them, and re-layouts  4.09 us (3%)
  other arithmetic  2.38 us (2%)
    all_to_all x6, starting transfers between devices, exchange(): return lax.all_to_all(x, axis, 0, 0)  42.6 us
    pallas_call x3, Pallas kernels, attend(): pl.pallas_call(functools.partial(attend_kernel, first, count), out_shape=...  21.8 us
    all_to_all x6, waiting for transfers between devices, exchange(): return lax.all_to_all(x, axis, 0, 0)  16.3 us
    ppermute x4, starting transfers between devices, on_device(): lax.ppermute(x, ('y', 'zh'), [(i, (i + chips) % (NY * NZ)) for i in range...  14.1 us
    ppermute x4, waiting for transfers between devices, on_device(): lax.ppermute(x, ('y', 'zh'), [(i, (i + chips) % (NY * NZ)) for i in range...  13.7 us
    ppermute x1, starting transfers between devices, on_device(): near_theirs = lax.ppermute(near, 'core', other_core)  4.89 us
    unnamed x20, local copies, waits for them, and re-layouts  3.76 us
  transfers between devices with their start and end apart: 12, of which 6 were waited for; matrix products, arithmetic and copies ran while one was open for 2% of the time, Pallas kernels for 18%

profile of v3, /device:TPU:1, one launch (start us, length us, event | category | flops | bytes accessed | tf_op | source)
XLA Modules:
  0.0 131.3 jit_solution(10005375751960551653)
XLA Ops:
  0.6 2.5 %shard_map.68 = (bf16[16,80,128]{2,1,0:T(8,128)(2,1)}, bf16[2,256,128]{2,1,0:T(8,128)(2,1)}) custom-call(bf16[5,256,128]{2,1,0:T(8,128)(2,1)} %bitcast.20, bf16[256,128]{1,0:T(8,128)(2,1)} %bitcast.16, bf16[256,128]{1,0:T(8,128)(2,1)} %bitcast.25), custom_call_target="tpu_custom_call" | custom-call | tf_op jit(solution)/shard_map/pallas_call | solution.py:65
  3.2 10.2 %all-to-all-start = ((bf16[16,80,128]{2,1,0:T(8,128)(2,1)}), bf16[16,80,128]{2,1,0:T(8,128)(2,1)S(1)}, u32[]{:S(2)}, u32[]{:S(2)}) async-start(bf16[16,80,128]{2,1,0:T(8,128)(2,1)} %get-tuple-element.13), calls=%async_computation | async-start | bytes 655360 | tf_op jit(solution)/shard_map/all_to_all | solution.py:45
  13.4 13.0 %all-to-all-done.r = bf16[16,80,128]{2,1,0:T(8,128)(2,1)S(1)} async-done(((bf16[16,80,128]{2,1,0:T(8,128)(2,1)}), bf16[16,80,128]{2,1,0:T(8,128)(2,1)S(1)}, u32[]{:S(2)}, u32[]{:S(2)}) %all-to-all-start) | async-done | bytes 327712 | tf_op jit(solution)/shard_map/all_to_all | solution.py:45
  26.4 1.6 %shard_map.69 = bf16[4,304,128]{2,1,0:T(8,128)(2,1)} custom-call(s32[1,16]{1,0:T(1,128)S(1)} %copy-done.4, s32[1]{0:T(128)} %bitcast.6.zh, bf16[16,80,128]{2,1,0:T(8,128)(2,1)S(1)} %all-to-all-done.r), custom_call_target="tpu_custom_call" | custom-call | tf_op jit(solution)/shard_map/pallas_call | solution.py:88
  28.0 8.6 %all-to-all-start.1 = ((bf16[4,304,128]{2,1,0:T(8,128)(2,1)}), bf16[4,304,128]{2,1,0:T(8,128)(2,1)S(1)}, u32[]{:S(2)}, u32[]{:S(2)}) async-start(bf16[4,304,128]{2,1,0:T(8,128)(2,1)} %shard_map.69), calls=%async_computation.1 | async-start | bytes 622592 | tf_op jit(solution)/shard_map/all_to_all | solution.py:45
  36.6 1.9 %collective-permute-start = (bf16[2,256,128]{2,1,0:T(8,128)(2,1)S(1)}, bf16[2,256,128]{2,1,0:T(8,128)(2,1)S(1)}, u32[]{:S(2)}, u32[]{:S(2)}) collective-permute-start(bf16[2,256,128]{2,1,0:T(8,128)(2,1)S(1)} %copy-done.3), channel_id=1, source_target_pairs={{0,64},{16,80},{32,96},{48,112},{64,128},{80,144},{96,160},{112,17... | collective-permute-start | bytes 393224 | tf_op jit(solution)/shard_map/ppermute | solution.py:320
  38.5 6.5 %collective-permute-done.after.refs_4_ = bf16[2,256,128]{2,1,0:T(8,128)(2,1)S(1)} collective-permute-done((bf16[2,256,128]{2,1,0:T(8,128)(2,1)S(1)}, bf16[2,256,128]{2,1,0:T(8,128)(2,1)S(1)}, u32[]{:S(2)}, u32[]{:S(2)}) %collective-permute-start) | collective-permute-done | bytes 131104 | tf_op jit(solution)/shard_map/ppermute | solution.py:320
  45.0 3.3 %all-to-all-done.1.r = bf16[4,304,128]{2,1,0:T(8,128)(2,1)S(1)} async-done(((bf16[4,304,128]{2,1,0:T(8,128)(2,1)}), bf16[4,304,128]{2,1,0:T(8,128)(2,1)S(1)}, u32[]{:S(2)}, u32[]{:S(2)}) %all-to-all-start.1) | async-done | bytes 311328 | tf_op jit(solution)/shard_map/all_to_all | solution.py:45
  48.3 0.9 shard_map.70
  49.2 3.5 %all-to-all-start.2 = ((bf16[8,304,128]{2,1,0:T(8,128)(2,1)}), bf16[8,304,128]{2,1,0:T(8,128)(2,1)S(1)}, u32[]{:S(2)}, u32[]{:S(2)}) async-start(bf16[8,304,128]{2,1,0:T(8,128)(2,1)} %get-tuple-element.15), calls=%async_computation.2 | async-start | bytes 1245184 | tf_op jit(solution)/shard_map/all_to_all | solution.py:45
  54.4 1.9 %collective-permute-start.2 = (bf16[2,256,128]{2,1,0:T(8,128)(2,1)S(1)}, bf16[2,256,128]{2,1,0:T(8,128)(2,1)S(1)}, u32[]{:S(2)}, u32[]{:S(2)}) collective-permute-start(bf16[2,256,128]{2,1,0:T(8,128)(2,1)S(1)} %get-tuple-element.16.refs_0_), channel_id=1, source_target_pairs={{0,16},{16,32},{32,48},{48,64},{64,80},{80,96},{96,112},{112,128},... | collective-permute-start | bytes 393224 | tf_op jit(solution)/shard_map/ppermute | solution.py:320
  56.3 5.8 %collective-permute-start.3 = (bf16[2,256,128]{2,1,0:T(8,128)(2,1)S(1)}, bf16[2,256,128]{2,1,0:T(8,128)(2,1)S(1)}, u32[]{:S(2)}, u32[]{:S(2)}) collective-permute-start(bf16[2,256,128]{2,1,0:T(8,128)(2,1)S(1)} %get-tuple-element.16.refs_0_), channel_id=1, source_target_pairs={{0,32},{16,48},{32,64},{48,80},{64,96},{80,112},{96,128},{112,144}... | collective-permute-start | bytes 393224 | tf_op jit(solution)/shard_map/ppermute | solution.py:320
  62.2 4.5 %collective-permute-start.4 = (bf16[2,256,128]{2,1,0:T(8,128)(2,1)S(1)}, bf16[2,256,128]{2,1,0:T(8,128)(2,1)S(1)}, u32[]{:S(2)}, u32[]{:S(2)}) collective-permute-start(bf16[2,256,128]{2,1,0:T(8,128)(2,1)S(1)} %get-tuple-element.16.refs_0_), channel_id=1, source_target_pairs={{0,48},{16,64},{32,80},{48,96},{64,112},{80,128},{96,144},{112,160... | collective-permute-start | bytes 393224 | tf_op jit(solution)/shard_map/ppermute | solution.py:320
  66.7 6.2 %collective-permute-done.2.refs_1_ = bf16[2,256,128]{2,1,0:T(8,128)(2,1)S(1)} collective-permute-done((bf16[2,256,128]{2,1,0:T(8,128)(2,1)S(1)}, bf16[2,256,128]{2,1,0:T(8,128)(2,1)S(1)}, u32[]{:S(2)}, u32[]{:S(2)}) %collective-permute-start.2) | collective-permute-done | bytes 131104 | tf_op jit(solution)/shard_map/ppermute | solution.py:320
  74.8 4.9 %collective-permute-start.5 = (bf16[5,2,256,128]{3,2,1,0:T(8,128)(2,1)S(1)}, bf16[5,2,256,128]{3,2,1,0:T(8,128)(2,1)S(1)}, u32[]{:S(2)}, u32[]{:S(2)}) collective-permute-start(bf16[5,2,256,128]{3,2,1,0:T(8,128)(2,1)S(1)} %shard_map.71.near), channel_id=1, source_target_pairs={{0,8},{8,0},{1,9},{9,1},{2,10},{10,2},{3,11},{11,3},{4,12},{12,4},... | collective-permute-start | bytes 1966088 | tf_op jit(solution)/shard_map/ppermute | solution.py:328
  79.7 1.9 %collective-permute-start.1 = (bf16[8,304,128]{2,1,0:T(8,128)(2,1)S(1)}, bf16[8,304,128]{2,1,0:T(8,128)(2,1)S(1)}, u32[]{:S(2)}, u32[]{:S(2)}) collective-permute-start(bf16[8,304,128]{2,1,0:T(8,128)(2,1)S(1)} %all-to-all-done.2.mine.r), channel_id=1, source_target_pairs={{0,8},{8,0},{1,9},{9,1},{2,10},{10,2},{3,11},{11,3},{4,12},{12,4},... | collective-permute-start | bytes 1867784 | tf_op jit(solution)/shard_map/ppermute | solution.py:329
  82.8 0.9 shard_map.75
  83.7 7.5 %all-to-all-start.3 = ((f32[16,2,384]{2,1,0:T(2,128)}), f32[16,2,384]{2,1,0:T(2,128)S(1)}, u32[]{:S(2)}, u32[]{:S(2)}) async-start(f32[16,2,384]{2,1,0:T(2,128)} %get-tuple-element.20), calls=%async_computation.3 | async-start | bytes 98304 | tf_op jit(solution)/shard_map/all_to_all | solution.py:45
  93.0 8.1 %shard_map.72 = (bf16[5,256,128]{2,1,0:T(8,128)(2,1)}, f32[8,128]{1,0:T(8,128)}) custom-call(s32[2,8]{1,0:T(2,128)} %get-tuple-element.25.places, s32[1]{0:T(128)} %bitcast.2.core, f32[2,1,3072]{2,1,0:T(1,128)} %pad_maximum_fusion.bias, bf16[5,256,128]{2,1,0:T(8,128)(2,1)} %bitcast.21, bf16[8,304,128]{2,1,0:T(8,128)(2,1)} %copy-done, ...), custom_call_target="tpu_custom_call" | custom-call | flops 805306368 | bytes 4194304 | tf_op jit(solution)/shard_map/pallas_call | solution.py:271
  102.5 8.8 %all-to-all-start.4 = ((f32[4,2,384]{2,1,0:T(2,128)}), f32[4,2,384]{2,1,0:T(2,128)S(1)}, u32[]{:S(2)}, u32[]{:S(2)}) async-start(f32[4,2,384]{2,1,0:T(2,128)} %shard_map.76), calls=%async_computation.4 | async-start | bytes 24576 | tf_op jit(solution)/shard_map/all_to_all | solution.py:45
  111.3 8.2 %shard_map.73 = (bf16[5,256,128]{2,1,0:T(8,128)(2,1)}, f32[8,128]{1,0:T(8,128)}) custom-call(s32[2,8]{1,0:T(2,128)} %get-tuple-element.25.places, s32[1]{0:T(128)} %bitcast.2.core, f32[2,1,3072]{2,1,0:T(1,128)} %pad_maximum_fusion.bias, bf16[5,256,128]{2,1,0:T(8,128)(2,1)} %bitcast.22, ...), custom_call_target="tpu_custom_call", output_to_operand_aliasing={{0}: (8, {})} | custom-call | flops 805306368 | bytes 4194304 | tf_op jit(solution)/shard_map/pallas_call | solution.py:271
  120.1 1.1 shard_map.77
  121.2 4.0 %all-to-all-start.5 = ((f32[8,1,256]{2,1,0:T(1,128)}), f32[8,1,256]{2,1,0:T(1,128)S(1)}, u32[]{:S(2)}, u32[]{:S(2)}) async-start(f32[8,1,256]{2,1,0:T(1,128)} %shard_map.77), calls=%async_computation.5 | async-start | bytes 16384 | tf_op jit(solution)/shard_map/all_to_all | solution.py:45
  125.1 5.5 %shard_map.74 = (bf16[5,256,128]{2,1,0:T(8,128)(2,1)}, f32[8,128]{1,0:T(8,128)}) custom-call(s32[2,8]{1,0:T(2,128)} %get-tuple-element.25.places, s32[1]{0:T(128)} %bitcast.2.core, f32[2,1,3072]{2,1,0:T(1,128)} %pad_maximum_fusion.bias, bf16[5,256,128]{2,1,0:T(8,128)(2,1)} %bitcast.23, ...), custom_call_target="tpu_custom_call", output_to_operand_aliasing={{0}: (8, {})} | custom-call | flops 402653184 | bytes 4194304 | tf_op jit(solution)/shard_map/pallas_call | solution.py:271
  (45 shorter events, 8.9 us)
Async XLA Ops:
  3.2 23.3 %all-to-all-start = ((bf16[16,80,128]{2,1,0:T(8,128)(2,1)}), bf16[16,80,128]{2,1,0:T(8,128)(2,1)S(1)}, u32[]{:S(2)}, u32[]{:S(2)}) async-start(bf16[16,80,128]{2,1,0:T(8,128)(2,1)} %get-tuple-element.13), calls=%async_computation | async-start | bytes 655360 | tf_op jit(solution)/shard_map/all_to_all | solution.py:45
  13.4 13.0 %copy-start.4 = (s32[1,16]{1,0:T(1,128)S(1)}, s32[1,16]{1,0:T(1,128)}, u32[]{:S(2)}) copy-start(s32[1,16]{1,0:T(1,128)} %ids.1) | copy-start | bytes 196
  28.0 8.6 %copy-start.3 = (bf16[2,256,128]{2,1,0:T(8,128)(2,1)S(1)}, bf16[2,256,128]{2,1,0:T(8,128)(2,1)}, u32[]{:S(2)}) copy-start(bf16[2,256,128]{2,1,0:T(8,128)(2,1)} %get-tuple-element.14.kv) | copy-start | bytes 393220
  28.0 20.3 %all-to-all-start.1 = ((bf16[4,304,128]{2,1,0:T(8,128)(2,1)}), bf16[4,304,128]{2,1,0:T(8,128)(2,1)S(1)}, u32[]{:S(2)}, u32[]{:S(2)}) async-start(bf16[4,304,128]{2,1,0:T(8,128)(2,1)} %shard_map.69), calls=%async_computation.1 | async-start | bytes 622592 | tf_op jit(solution)/shard_map/all_to_all | solution.py:45
  36.6 8.4 %collective-permute-start = (bf16[2,256,128]{2,1,0:T(8,128)(2,1)S(1)}, bf16[2,256,128]{2,1,0:T(8,128)(2,1)S(1)}, u32[]{:S(2)}, u32[]{:S(2)}) collective-permute-start(bf16[2,256,128]{2,1,0:T(8,128)(2,1)S(1)} %copy-done.3), channel_id=1, source_target_pairs={{0,64},{16,80},{32,96},{48,112},{64,128},{80,144},{96,160},{112,17... | collective-permute-start | bytes 393224 | tf_op jit(solution)/shard_map/ppermute | solution.py:320
  49.2 30.4 %all-to-all-start.2 = ((bf16[8,304,128]{2,1,0:T(8,128)(2,1)}), bf16[8,304,128]{2,1,0:T(8,128)(2,1)S(1)}, u32[]{:S(2)}, u32[]{:S(2)}) async-start(bf16[8,304,128]{2,1,0:T(8,128)(2,1)} %get-tuple-element.15), calls=%async_computation.2 | async-start | bytes 1245184 | tf_op jit(solution)/shard_map/all_to_all | solution.py:45
  52.8 0.7 copy-start.9
  54.4 18.6 %collective-permute-start.2 = (bf16[2,256,128]{2,1,0:T(8,128)(2,1)S(1)}, bf16[2,256,128]{2,1,0:T(8,128)(2,1)S(1)}, u32[]{:S(2)}, u32[]{:S(2)}) collective-permute-start(bf16[2,256,128]{2,1,0:T(8,128)(2,1)S(1)} %get-tuple-element.16.refs_0_), channel_id=1, source_target_pairs={{0,16},{16,32},{32,48},{48,64},{64,80},{80,96},{96,112},{112,128},... | collective-permute-start | bytes 393224 | tf_op jit(solution)/shard_map/ppermute | solution.py:320
  56.3 17.0 %collective-permute-start.3 = (bf16[2,256,128]{2,1,0:T(8,128)(2,1)S(1)}, bf16[2,256,128]{2,1,0:T(8,128)(2,1)S(1)}, u32[]{:S(2)}, u32[]{:S(2)}) collective-permute-start(bf16[2,256,128]{2,1,0:T(8,128)(2,1)S(1)} %get-tuple-element.16.refs_0_), channel_id=1, source_target_pairs={{0,32},{16,48},{32,64},{48,80},{64,96},{80,112},{96,128},{112,144}... | collective-permute-start | bytes 393224 | tf_op jit(solution)/shard_map/ppermute | solution.py:320
  62.2 11.7 %collective-permute-start.4 = (bf16[2,256,128]{2,1,0:T(8,128)(2,1)S(1)}, bf16[2,256,128]{2,1,0:T(8,128)(2,1)S(1)}, u32[]{:S(2)}, u32[]{:S(2)}) collective-permute-start(bf16[2,256,128]{2,1,0:T(8,128)(2,1)S(1)} %get-tuple-element.16.refs_0_), channel_id=1, source_target_pairs={{0,48},{16,64},{32,80},{48,96},{64,112},{80,128},{96,144},{112,160... | collective-permute-start | bytes 393224 | tf_op jit(solution)/shard_map/ppermute | solution.py:320
  74.8 17.2 %copy-start.1 = (bf16[5,2,256,128]{3,2,1,0:T(8,128)(2,1)}, bf16[5,2,256,128]{3,2,1,0:T(8,128)(2,1)S(1)}, u32[]{:S(2)}) copy-start(bf16[5,2,256,128]{3,2,1,0:T(8,128)(2,1)S(1)} %shard_map.71.near) | copy-start | bytes 1966084
  74.8 17.2 %collective-permute-start.5 = (bf16[5,2,256,128]{3,2,1,0:T(8,128)(2,1)S(1)}, bf16[5,2,256,128]{3,2,1,0:T(8,128)(2,1)S(1)}, u32[]{:S(2)}, u32[]{:S(2)}) collective-permute-start(bf16[5,2,256,128]{3,2,1,0:T(8,128)(2,1)S(1)} %shard_map.71.near), channel_id=1, source_target_pairs={{0,8},{8,0},{1,9},{9,1},{2,10},{10,2},{3,11},{11,3},{4,12},{12,4},... | collective-permute-start | bytes 1966088 | tf_op jit(solution)/shard_map/ppermute | solution.py:328
  79.7 12.3 %copy-start = (bf16[8,304,128]{2,1,0:T(8,128)(2,1)}, bf16[8,304,128]{2,1,0:T(8,128)(2,1)S(1)}, u32[]{:S(2)}) copy-start(bf16[8,304,128]{2,1,0:T(8,128)(2,1)S(1)} %all-to-all-done.2.mine.r) | copy-start | bytes 1867780
  79.7 12.3 %collective-permute-start.1 = (bf16[8,304,128]{2,1,0:T(8,128)(2,1)S(1)}, bf16[8,304,128]{2,1,0:T(8,128)(2,1)S(1)}, u32[]{:S(2)}, u32[]{:S(2)}) collective-permute-start(bf16[8,304,128]{2,1,0:T(8,128)(2,1)S(1)} %all-to-all-done.2.mine.r), channel_id=1, source_target_pairs={{0,8},{8,0},{1,9},{9,1},{2,10},{10,2},{3,11},{11,3},{4,12},{12,4},... | collective-permute-start | bytes 1867784 | tf_op jit(solution)/shard_map/ppermute | solution.py:329
  81.9 0.8 copy-start.2
  83.7 17.5 %all-to-all-start.3 = ((f32[16,2,384]{2,1,0:T(2,128)}), f32[16,2,384]{2,1,0:T(2,128)S(1)}, u32[]{:S(2)}, u32[]{:S(2)}) async-start(f32[16,2,384]{2,1,0:T(2,128)} %get-tuple-element.20), calls=%async_computation.3 | async-start | bytes 98304 | tf_op jit(solution)/shard_map/all_to_all | solution.py:45
  91.9 0.9 copy-start.7
  91.9 1.1 copy-start.8
  101.2 0.7 copy-start.6
  102.5 16.9 %all-to-all-start.4 = ((f32[4,2,384]{2,1,0:T(2,128)}), f32[4,2,384]{2,1,0:T(2,128)S(1)}, u32[]{:S(2)}, u32[]{:S(2)}) async-start(f32[4,2,384]{2,1,0:T(2,128)} %shard_map.76), calls=%async_computation.4 | async-start | bytes 24576 | tf_op jit(solution)/shard_map/all_to_all | solution.py:45
  119.4 0.7 copy-start.5
  121.2 9.5 %all-to-all-start.5 = ((f32[8,1,256]{2,1,0:T(1,128)}), f32[8,1,256]{2,1,0:T(1,128)S(1)}, u32[]{:S(2)}, u32[]{:S(2)}) async-start(f32[8,1,256]{2,1,0:T(1,128)} %shard_map.77), calls=%async_computation.5 | async-start | bytes 16384 | tf_op jit(solution)/shard_map/all_to_all | solution.py:45

commit v4 on v3

v4 whole, which is shorter than its diff:
```python
import functools
import math

import jax
import jax.numpy as jnp
from jax import lax
from jax.experimental import pallas as pl
from jax.experimental.pallas import tpu as pltpu
from jax.sharding import Mesh
from jax.sharding import PartitionSpec as P

BLK = 128
LAST = 64
NV = 16
NS = 8
HEADS = 40
HD = 128
GROUP = 5
FAR = -1e30
LOG2E = math.log2(math.e)
C = ("zh", "core")
CTX = ("y", "zh", "core")
NY, NZ = 8, 4
PER_ROW = 2 * NZ
CHIPS = NY * NZ
PIECE = BLK // CHIPS
LISTED = NV * PIECE
UNIT = NZ * LISTED
NEAR = NS * BLK // UNIT
BACK = 5
QROWS = 16
QREAL = GROUP * LAST // 2
QALL = 256
NT = (((1,), (1,)), ((), ()))
SMEM = pl.BlockSpec(memory_space=pltpu.SMEM)
VMEM = pl.BlockSpec(memory_space=pltpu.VMEM)
ANY = pl.BlockSpec(memory_space=pl.ANY)
F32 = jnp.float32
BF16 = jnp.bfloat16
LARGE = pltpu.CompilerParams(vmem_limit_bytes=60 * 1024 * 1024)
SMALL = pltpu.CompilerParams(vmem_limit_bytes=8 * 1024 * 1024)


def shape(kind, *dims):
    return jax.ShapeDtypeStruct(dims, kind)


def exchange(x, axis):
    return lax.all_to_all(x, axis, 0, 0)


def pack_kernel(position, q, k, v, sent, kv, last, sem):
    local = k.shape[0]
    copy = pltpu.make_async_copy(q.at[:, pl.ds(local - LAST, LAST)], last, sem)
    copy.start()
    both = jnp.concatenate([k[...], v[...]], axis=0)
    kv[...] = both.reshape(kv.shape)
    n = 2 * local
    row = lax.broadcasted_iota(jnp.int32, (n, n), 0)
    column = lax.broadcasted_iota(jnp.int32, (n, n), 1)
    source = ((row >> 3) & 1) * local + ((row >> 2) & 1) * BLK + (row >> 4) * PIECE + (row & 3)
    cut = jnp.dot((column == source).astype(BF16), both, preferred_element_type=F32).astype(BF16)
    sent[...] = cut.reshape(sent.shape)
    copy.wait()

    @pl.when(position[0] == 2 * CHIPS - 1)
    def _():
        flat = last[...].reshape(GROUP * LAST, HD)
        flat = jnp.concatenate([flat, jnp.zeros((n - GROUP * LAST, HD), BF16)], axis=0)
        sent[...] = flat.reshape(sent.shape)


def pack(position, q_t, k, v):
    local = k.shape[0]
    return pl.pallas_call(
        pack_kernel,
        out_shape=(shape(BF16, CHIPS, 16, HD), shape(BF16, 2, local, HD)),
        in_specs=[SMEM, ANY, VMEM, VMEM],
        out_specs=(VMEM, VMEM),
        scratch_shapes=[pltpu.VMEM((GROUP, LAST, HD), BF16), pltpu.SemaphoreType.DMA],
        compiler_params=LARGE,
    )(position, q_t, k, v)


def pick_kernel(ids, r, one, three, out, one_again):
    one_again[...] = one[...]
    rows = r[...].reshape(CHIPS * 16, HD)
    wanted = LISTED + QROWS
    row = lax.broadcasted_iota(jnp.int32, (wanted, HD), 0)
    source = jnp.where(row < LISTED + 8, CHIPS * 16 - 8 - LISTED + row, -1)
    for j in range(NV):
        source = jnp.where(row // PIECE == j, ids[0, j] * PIECE + row % PIECE, source)
    column = lax.broadcasted_iota(jnp.int32, (wanted, HD), 1)
    chosen = jnp.concatenate([(column + i == source).astype(BF16) for i in range(0, CHIPS * 16, HD)], axis=1)
    tile = jnp.dot(chosen, rows, preferred_element_type=F32).astype(BF16)
    for d in range(NZ):
        out[d] = tile


def pick(vertical, r, one, three):
    return pl.pallas_call(
        pick_kernel,
        out_shape=(shape(BF16, NZ, LISTED + QROWS, HD), shape(BF16, *one.shape)),
        in_specs=[SMEM, VMEM, VMEM, ANY],
        out_specs=(VMEM, VMEM),
        compiler_params=SMALL,
    )(vertical, r, one, three)


def merge_kernel(r, one, four, k_theirs, out, one_again):
    one_again[...] = one[...]
    q = jnp.concatenate([r[z, LISTED:, :].astype(F32)[:8] for z in range(NZ)], axis=0).astype(BF16)
    for d in range(NY):
        for z in range(NZ):
            out[d, z * LISTED : (z + 1) * LISTED, :] = r[z, :LISTED, :]
        out[d, UNIT:, :] = q


def merge(r, one, four, k_theirs):
    return pl.pallas_call(
        merge_kernel,
        out_shape=(shape(BF16, NY, UNIT + 8 * NZ, HD), shape(BF16, *one.shape)),
        in_specs=[VMEM, VMEM, ANY, ANY],
        out_specs=(VMEM, VMEM),
        compiler_params=SMALL,
    )(r, one, four, k_theirs)


def together_kernel(*refs):
    *parts, mine, out, sems = refs
    n = len(parts)
    each = parts[0].shape[0]
    copies = [pltpu.make_async_copy(part, out.at[pl.ds(each * i, each)], sems.at[i]) for i, part in enumerate(parts)]
    copies.append(pltpu.make_async_copy(mine.at[:, pl.ds(0, UNIT)], out.at[pl.ds(each * n, NY)], sems.at[n]))
    for copy in copies:
        copy.start()
    for copy in copies:
        copy.wait()


def together(parts, mine):
    n = len(parts)
    return pl.pallas_call(
        together_kernel,
        out_shape=shape(BF16, n * parts[0].shape[0] + NY, UNIT, HD),
        in_specs=[ANY] * (n + 1),
        out_specs=ANY,
        scratch_shapes=[pltpu.SemaphoreType.DMA((n + 1,))],
        compiler_params=SMALL,
    )(*parts, mine)


def estimate_kernel(total_len, position, r, k_mine, k_theirs, scores, stats):
    tokens = 2 * k_mine.shape[0]
    core = position[0] & 1
    q = r[:, UNIT:, :].reshape(QALL, HD)
    mine, theirs = k_mine[...], k_theirs[...]
    k = jnp.concatenate([jnp.where(core == 0, mine, theirs), jnp.where(core == 0, theirs, mine)], axis=0)
    s = lax.dot_general(k, q, NT, preferred_element_type=F32) * (1.0 / math.sqrt(HD))
    column = lax.broadcasted_iota(jnp.int32, (1, QALL), 1)
    last_pos = total_len - LAST + ((column >> 3) * 16 + core * 8 + (column & 7)) % LAST
    key_pos = (position[0] >> 1) * tokens + lax.broadcasted_iota(jnp.int32, (tokens, QALL), 0)
    s = jnp.where(key_pos <= last_pos, s, FAR)
    scores[...] = s
    top = jnp.max(s, axis=0, keepdims=True)
    total = jnp.sum(jnp.exp(s - top), axis=0, keepdims=True)
    both = jnp.concatenate([top, total], axis=0)
    for d in range(CHIPS):
        stats[d] = both


def estimate(position, r, k_mine, k_theirs, total_len):
    return pl.pallas_call(
        functools.partial(estimate_kernel, total_len),
        out_shape=(shape(F32, 2 * k_mine.shape[0], QALL), shape(F32, CHIPS, 2, QALL)),
        in_specs=[SMEM, VMEM, VMEM, VMEM],
        out_specs=(VMEM, VMEM),
        compiler_params=SMALL,
    )(position, r, k_mine, k_theirs)


def mass_kernel(stats, scores, after, out):
    tops, totals = stats[:, 0, :], stats[:, 1, :]
    top = jnp.max(tops, axis=0, keepdims=True)
    total = jnp.sum(totals * jnp.exp(tops - top), axis=0, keepdims=True)
    p = jnp.exp(scores[...] - (top + jnp.log(total)))
    kvh, local = out.shape[0] // 2, out.shape[2]
    real = (lax.broadcasted_iota(jnp.int32, (kvh, QALL), 1) < QREAL).astype(F32)
    mass = lax.dot_general(real, p, NT, precision=lax.Precision.HIGHEST, preferred_element_type=F32)
    for c in range(2):
        out[c * kvh : (c + 1) * kvh, 0, :] = mass[:, c * local : (c + 1) * local]


def mass(stats, scores, after, kvh):
    return pl.pallas_call(
        mass_kernel,
        out_shape=shape(F32, 2 * kvh, 1, scores.shape[0] // 2),
        in_specs=[VMEM, VMEM, ANY],
        out_specs=VMEM,
        compiler_params=SMALL,
    )(stats, scores, after)


def attend_kernel(e, vertical, slash, position, q, ours, theirs, *rest):
    if e:
        rest = rest[1:]
    out, token, q_buf, o_buf, k_all, v_all, sems = rest
    token[...] = jnp.zeros_like(token)
    core = position[0] & 1
    block = position[0] * 2 + e
    near = [block] + [block - jnp.where(slash[0, j] == 0, slash[0, 0], slash[0, j]) for j in range(1, NS)]
    copies = [pltpu.make_async_copy(q.at[:, pl.ds(e * BLK, BLK)], q_buf, sems.at[0])]
    copies[0].start()

    def fetch(from_ours, source, target):
        sem = sems.at[len(copies)]
        copy = pltpu.make_async_copy(source(ours), target, sem)
        other = pltpu.make_async_copy(source(theirs), target, sem)
        pl.when(from_ours)(copy.start)
        pl.when(jnp.logical_not(from_ours))(other.start)
        copies.append(copy)

    for j in range(NS):
        kept = jnp.where(near[j] >= 0, near[j], block)
        chips = (position[0] >> 1) - (kept >> 2)
        row = pl.multiple_of((kept & 1) * BLK, BLK)
        to = pl.ds(j % 2 * BLK, BLK)
        for which, target in ((0, k_all.at[j // 2, to]), (1, v_all.at[j // 2, to, pl.ds(0, HD)])):
            fetch(((kept >> 1) & 1) == core, lambda x: x.at[2 * chips + which, pl.ds(row, BLK)], target)
    to = pl.ds(NEAR, NY)
    for which, target in ((0, k_all.at[to]), (1, v_all.at[to, :, pl.ds(0, HD)])):
        fetch(core == which, lambda x: x.at[pl.ds(2 * BACK, NY)], target)
    v_all[:NEAR, :, HD:] = jnp.ones((NEAR, UNIT, HD), BF16)

    row = lax.broadcasted_iota(jnp.int32, (LISTED, HD), 0)
    drop = jnp.zeros((LISTED, HD), jnp.int32)
    for j in range(NV):
        c = vertical[0, j]
        bad = c > block
        for other in near:
            bad = bad | (c == other)
        drop = jnp.where(row // PIECE == j, bad.astype(jnp.int32), drop)
    drop = jnp.concatenate([drop.astype(F32)] * NZ, axis=0)
    keep = (1.0 - drop).astype(BF16)
    drop = drop.astype(BF16)
    for copy in copies:
        copy.wait()

    first = k_all[0, 0:1, :]
    for j in range(1, NS):

        @pl.when(near[j] < 0)
        def _(j=j):
            to = slice(j % 2 * BLK, (j % 2 + 1) * BLK)
            k_all[j // 2, to, :] = jnp.broadcast_to(first, (BLK, HD))
            v_all[j // 2, to, :] = jnp.zeros((BLK, 2 * HD), BF16)

    instead = first * drop
    for i in range(NEAR, NEAR + NY):
        k_all[i] = k_all[i] * keep + instead
        v_all[i, :, :HD] = v_all[i, :, :HD] * keep
        v_all[i, :, HD:] = keep

    factor = LOG2E / math.sqrt(HD)
    causal = lax.broadcasted_iota(jnp.int32, (BLK, BLK), 1) <= lax.broadcasted_iota(jnp.int32, (BLK, BLK), 0)
    keys = k_all[...].reshape((NV + NS) * BLK, HD)
    values = v_all[...].reshape((NV + NS) * BLK, 2 * HD)
    for h in range(0, GROUP, 2):
        n = min(2, GROUP - h)
        tile = q_buf[h : h + n].reshape(n * BLK, HD)
        s = lax.dot_general(tile, keys, NT, preferred_element_type=F32)
        own = jnp.where(jnp.concatenate([causal] * n, axis=0), s[:, :BLK], FAR)
        s = jnp.concatenate([own, s[:, BLK:]], axis=1)
        top = jnp.max(s, axis=1, keepdims=True) * factor
        w = jnp.exp2(s * factor - top).astype(BF16)
        o = jnp.dot(w, values, preferred_element_type=F32)
        o_buf[h : h + n] = (o[:, :HD] / o[:, HD:]).astype(BF16).reshape(n, BLK, HD)
    copy = pltpu.make_async_copy(o_buf, out.at[:, pl.ds(e * BLK, BLK)], sems.at[0])
    copy.start()
    copy.wait()


def attend(e, vertical, slash, position, q_t, ours, theirs, out=None):
    local = q_t.shape[1]
    args = (vertical, slash, position, q_t, ours, theirs) + ((out,) if e else ())
    return pl.pallas_call(
        functools.partial(attend_kernel, e),
        out_shape=(shape(BF16, GROUP, local, HD), shape(F32, 8, 128)),
        in_specs=[SMEM] * 3 + [ANY] * (len(args) - 3),
        out_specs=(ANY, VMEM),
        scratch_shapes=[
            pltpu.VMEM((GROUP, BLK, HD), BF16),
            pltpu.VMEM((GROUP, BLK, HD), BF16),
            pltpu.VMEM((NEAR + NY, UNIT, HD), BF16),
            pltpu.VMEM((NEAR + NY, UNIT, 2 * HD), BF16),
            pltpu.SemaphoreType.DMA((2 * NS + 3,)),
        ],
        input_output_aliases={len(args) - 1: 0} if e else {},
        compiler_params=LARGE,
        cost_estimate=pl.CostEstimate(
            flops=4 * GROUP * (NV + NS) * BLK**3, bytes_accessed=2 * 1024 * 1024, transcendentals=GROUP * (NV + NS) * BLK**2
        ),
    )(*args)


def on_device(queries, key_rows, value_rows, vertical, slash_offsets):
    local = key_rows.shape[0]
    total_len = local * NY * PER_ROW
    place = ((lax.axis_index("y") * NZ + lax.axis_index("zh")) * 2 + lax.axis_index("core")).reshape(1)
    q_t = jnp.transpose(queries, (1, 0, 2))
    k, v = key_rows[:, 0], value_rows[:, 0]

    sent, kv = pack(place, q_t, k, v)
    back = lambda x, chips: lax.ppermute(x, ("y", "zh"), [(i, (i + chips) % CHIPS) for i in range(CHIPS)])
    swap = lambda x: lax.ppermute(x, "core", [(0, 1), (1, 0)])
    k_theirs, one, three, four = swap(k), back(kv, 1), back(kv, 3), back(kv, 4)
    r = exchange(sent.reshape(2 * CHIPS, 8, HD), CTX).reshape(CHIPS, 16, HD)
    tile, again = pick(vertical, r, one, three)
    whole, again = merge(exchange(tile, "zh"), again, four, k_theirs)
    mine = exchange(whole, "y")
    scores, stats = estimate(place, mine, k, k_theirs, total_len)
    ours = together([kv, one, back(again, 1), three, four], mine)
    theirs = swap(ours)

    given = (vertical, slash_offsets, place, q_t, ours, theirs)
    out, token = attend(0, *given)
    stats = exchange(stats, ("y", "zh"))
    part = exchange(mass(stats, scores, token, lax.axis_size("kvh")), ("core", "kvh"))
    out, token = attend(1, *given, out)
    profile = jnp.sum(part, axis=(0, 1)) * (total_len / LAST / HEADS)
    return jnp.transpose(out, (1, 0, 2)), profile


def solution(mesh):
    wide = Mesh(mesh.devices.reshape(NY, NZ, 2, -1), ("y", "zh", "core", "kvh"))
    return jax.shard_map(
        on_device,
        mesh=wide,
        in_specs=(P(CTX, "kvh", None), P(CTX, "kvh", None), P(CTX, "kvh", None), P("kvh", None), P("kvh", None)),
        out_specs=(P(CTX, "kvh", None), P(CTX)),
        check_vma=False,
    )
```

time: 133 us -> 118 us (0.89)
  Pallas kernels: 30.3 us -> 21 us
  local copies, waits for them, and re-layouts: 4.09 us -> 1.34 us
  other arithmetic: 2.38 us -> 0.6 us
    ppermute x6, waiting for transfers between devices: 13.7 us -> 24.2 us  [the longest x4 23.3 us: on_device(): lax.ppermute(x, ('y', 'zh'), [(i, (i + chips) % CHIPS) for i in range(CHI...]
    all_to_all x6 -> x5, waiting for transfers between devices: 16.3 us -> 6.14 us  [exchange(): return lax.all_to_all(x, axis, 0, 0)]
    pallas_call x9 -> x7, Pallas kernels: 29.4 us -> 20 us  [the longest x2 13.1 us: attend(): pl.pallas_call(functools.partial(attend_kernel, e), out_shape=(shape(BF16...]
    unnamed x20 -> x10, local copies, waits for them, and re-layouts: 3.76 us -> 1.34 us
    all_to_all x6 -> x5, starting transfers between devices: 42.6 us -> 41 us  [exchange(): return lax.all_to_all(x, axis, 0, 0)]
  transfers between devices with their start and end apart: 12 -> 11, of which waited for: 6 -> 6; matrix products, arithmetic and copies ran while one was open for 2% -> 0% of each run, Pallas kernels for 18% -> 13%
where the time goes in v4:
time: 118 us; the launch traced here: 117 us
  starting transfers between devices  63 us (53%)
  waiting for transfers between devices  30.3 us (26%)
  Pallas kernels  21 us (18%)
  local copies, waits for them, and re-layouts  1.34 us (1%)
    all_to_all x5, starting transfers between devices, exchange(): return lax.all_to_all(x, axis, 0, 0)  41 us
    ppermute x4, waiting for transfers between devices, on_device(): lax.ppermute(x, ('y', 'zh'), [(i, (i + chips) % CHIPS) for i in range(CHI...  23.3 us
    pallas_call x2, Pallas kernels, attend(): pl.pallas_call(functools.partial(attend_kernel, e), out_shape=(shape(BF16...  13.1 us
    ppermute x4, starting transfers between devices, on_device(): lax.ppermute(x, ('y', 'zh'), [(i, (i + chips) % CHIPS) for i in range(CHI...  12.9 us
    ppermute x2, starting transfers between devices, on_device(): swap = lambda x: lax.ppermute(x, 'core', [(0, 1), (1, 0)])  9.06 us
    all_to_all x5, waiting for transfers between devices, exchange(): return lax.all_to_all(x, axis, 0, 0)  6.14 us
    pallas_call x1, Pallas kernels, pack(): pl.pallas_call(pack_kernel, out_shape=(shape(BF16, CHIPS, 16, HD), shape(...  2.52 us
  transfers between devices with their start and end apart: 11, of which 6 were waited for; matrix products, arithmetic and copies ran while one was open for 0% of the time, Pallas kernels for 13%

profile of v4, /device:TPU:1, one launch (start us, length us, event | category | flops | bytes accessed | tf_op | source)
XLA Modules:
  0.0 117.1 jit_solution(2725344894577448906)
XLA Ops:
  0.6 2.5 %shard_map.68 = (bf16[32,16,128]{2,1,0:T(8,128)(2,1)}, bf16[2,256,128]{2,1,0:T(8,128)(2,1)}) custom-call(s32[1]{0:T(128)} %bitcast.position, bf16[5,256,128]{2,1,0:T(8,128)(2,1)} %bitcast.11, bf16[256,128]{1,0:T(8,128)(2,1)} %bitcast.8, bf16[256,128]{1,0:T(8,128)(2,1)} %bitcast.15), custom_call_target="tpu_custom_call" | custom-call | tf_op jit(solution)/shard_map/pallas_call | solution.py:75
  3.2 17.8 %all-to-all-start = ((bf16[64,8,128]{2,1,0:T(8,128)(2,1)}), bf16[64,8,128]{2,1,0:T(8,128)(2,1)S(1)}, u32[]{:S(2)}, u32[]{:S(2)}) async-start(bf16[64,8,128]{2,1,0:T(8,128)(2,1)} %bitcast.14), calls=%async_computation | async-start | bytes 262144 | tf_op jit(solution)/shard_map/all_to_all | solution.py:49
  21.0 5.4 %collective-permute-start.1 = (bf16[2,256,128]{2,1,0:T(8,128)(2,1)}, bf16[2,256,128]{2,1,0:T(8,128)(2,1)S(1)}, u32[]{:S(2)}, u32[]{:S(2)}) collective-permute-start(bf16[2,256,128]{2,1,0:T(8,128)(2,1)} %get-tuple-element.13.refs_0_), channel_id=1, source_target_pairs={{0,48},{16,64},{32,80},{48,96},{64,112},{80,128},{96,144},{112,160... | collective-permute-start | bytes 393224 | tf_op jit(solution)/shard_map/ppermute | solution.py:314
  26.4 1.9 %collective-permute-start = (bf16[2,256,128]{2,1,0:T(8,128)(2,1)}, bf16[2,256,128]{2,1,0:T(8,128)(2,1)S(1)}, u32[]{:S(2)}, u32[]{:S(2)}) collective-permute-start(bf16[2,256,128]{2,1,0:T(8,128)(2,1)} %get-tuple-element.13.refs_0_), channel_id=1, source_target_pairs={{0,16},{16,32},{32,48},{48,64},{64,80},{80,96},{96,112},{112,128},... | collective-permute-start | bytes 393224 | tf_op jit(solution)/shard_map/ppermute | solution.py:314
  28.3 3.1 %collective-permute-start.2 = (bf16[2,256,128]{2,1,0:T(8,128)(2,1)}, bf16[2,256,128]{2,1,0:T(8,128)(2,1)S(1)}, u32[]{:S(2)}, u32[]{:S(2)}) collective-permute-start(bf16[2,256,128]{2,1,0:T(8,128)(2,1)} %get-tuple-element.13.refs_0_), channel_id=1, source_target_pairs={{0,64},{16,80},{32,96},{48,112},{64,128},{80,144},{96,160},{112,17... | collective-permute-start | bytes 393224 | tf_op jit(solution)/shard_map/ppermute | solution.py:314
  31.4 2.6 %collective-permute-done.1.three.refs_3_ = bf16[2,256,128]{2,1,0:T(8,128)(2,1)S(1)} collective-permute-done((bf16[2,256,128]{2,1,0:T(8,128)(2,1)}, bf16[2,256,128]{2,1,0:T(8,128)(2,1)S(1)}, u32[]{:S(2)}, u32[]{:S(2)}) %collective-permute-start.1) | collective-permute-done | bytes 131104 | tf_op jit(solution)/shard_map/ppermute | solution.py:314
  34.0 4.8 %collective-permute-done.one.refs_1_ = bf16[2,256,128]{2,1,0:T(8,128)(2,1)S(1)} collective-permute-done((bf16[2,256,128]{2,1,0:T(8,128)(2,1)}, bf16[2,256,128]{2,1,0:T(8,128)(2,1)S(1)}, u32[]{:S(2)}, u32[]{:S(2)}) %collective-permute-start) | collective-permute-done | bytes 131104 | tf_op jit(solution)/shard_map/ppermute | solution.py:314
  39.4 1.4 %shard_map.69 = (bf16[4,80,128]{2,1,0:T(8,128)(2,1)}, bf16[2,256,128]{2,1,0:T(8,128)(2,1)S(1)}) custom-call(s32[1,16]{1,0:T(1,128)S(1)} %copy-done.4, bf16[32,16,128]{2,1,0:T(8,128)(2,1)S(1)} %bitcast.7, bf16[2,256,128]{2,1,0:T(8,128)(2,1)S(1)} %collective-permute-done.one.refs_1_, bf16[2,256,128]{2,1,0:T(8,128)(2,1)S(1)} %collective-permute-done.1.three.refs_3_), custom_call_target="tpu_custom_call" | custom-call | tf_op jit(solution)/shard_map/pallas_call | solution.py:101
  40.8 3.3 %all-to-all-start.1 = ((bf16[4,80,128]{2,1,0:T(8,128)(2,1)}), bf16[4,80,128]{2,1,0:T(8,128)(2,1)S(1)}, u32[]{:S(2)}, u32[]{:S(2)}) async-start(bf16[4,80,128]{2,1,0:T(8,128)(2,1)} %get-tuple-element.15), calls=%async_computation.1 | async-start | bytes 163840 | tf_op jit(solution)/shard_map/all_to_all | solution.py:49
  44.1 4.6 %collective-permute-start.3 = (bf16[256,128]{1,0:T(8,128)(2,1)S(1)}, bf16[256,128]{1,0:T(8,128)(2,1)S(1)}, u32[]{:S(2)}, u32[]{:S(2)}) collective-permute-start(bf16[256,128]{1,0:T(8,128)(2,1)S(1)} %bitcast.9), channel_id=1, source_target_pairs={{0,8},{8,0},{1,9},{9,1},{2,10},{10,2},{3,11},{11,3},{4,12},{12,4},... | collective-permute-start | bytes 196616 | tf_op jit(solution)/shard_map/ppermute | solution.py:315
  49.6 1.5 %all-to-all-done.1.r = bf16[4,80,128]{2,1,0:T(8,128)(2,1)S(1)} async-done(((bf16[4,80,128]{2,1,0:T(8,128)(2,1)}), bf16[4,80,128]{2,1,0:T(8,128)(2,1)S(1)}, u32[]{:S(2)}, u32[]{:S(2)}) %all-to-all-start.1) | async-done | bytes 81952 | tf_op jit(solution)/shard_map/all_to_all | solution.py:49
  51.0 0.9 shard_map.70
  52.0 7.0 %all-to-all-start.2 = ((bf16[8,288,128]{2,1,0:T(8,128)(2,1)}), bf16[8,288,128]{2,1,0:T(8,128)(2,1)S(1)}, u32[]{:S(2)}, u32[]{:S(2)}) async-start(bf16[8,288,128]{2,1,0:T(8,128)(2,1)} %get-tuple-element.18), calls=%async_computation.2 | async-start | bytes 1179648 | tf_op jit(solution)/shard_map/all_to_all | solution.py:49
  58.9 2.5 %collective-permute-start.4 = (bf16[2,256,128]{2,1,0:T(8,128)(2,1)S(1)}, bf16[2,256,128]{2,1,0:T(8,128)(2,1)S(1)}, u32[]{:S(2)}, u32[]{:S(2)}) collective-permute-start(bf16[2,256,128]{2,1,0:T(8,128)(2,1)S(1)} %get-tuple-element.17), channel_id=1, source_target_pairs={{0,16},{16,32},{32,48},{48,64},{64,80},{80,96},{96,112},{112,128},... | collective-permute-start | bytes 393224 | tf_op jit(solution)/shard_map/ppermute | solution.py:314
  61.5 15.9 %collective-permute-done.4.refs_2_ = bf16[2,256,128]{2,1,0:T(8,128)(2,1)S(1)} collective-permute-done((bf16[2,256,128]{2,1,0:T(8,128)(2,1)S(1)}, bf16[2,256,128]{2,1,0:T(8,128)(2,1)S(1)}, u32[]{:S(2)}, u32[]{:S(2)}) %collective-permute-start.4) | collective-permute-done | bytes 131104 | tf_op jit(solution)/shard_map/ppermute | solution.py:314
  77.4 0.9 shard_map.71.ours
  78.3 4.5 %collective-permute-start.5 = (bf16[18,256,128]{2,1,0:T(8,128)(2,1)S(1)}, bf16[18,256,128]{2,1,0:T(8,128)(2,1)}, u32[]{:S(2)}, u32[]{:S(2)}) collective-permute-start(bf16[18,256,128]{2,1,0:T(8,128)(2,1)S(1)} %shard_map.71.ours), channel_id=1, source_target_pairs={{0,8},{8,0},{1,9},{9,1},{2,10},{10,2},{3,11},{11,3},{4,12},{12,4},... | collective-permute-start | bytes 3538952 | tf_op jit(solution)/shard_map/ppermute | solution.py:315
  82.8 1.0 shard_map.74
  83.8 6.9 %all-to-all-start.3 = ((f32[32,2,256]{2,1,0:T(2,128)}), f32[32,2,256]{2,1,0:T(2,128)S(1)}, u32[]{:S(2)}, u32[]{:S(2)}) async-start(f32[32,2,256]{2,1,0:T(2,128)} %get-tuple-element.21), calls=%async_computation.3 | async-start | bytes 131072 | tf_op jit(solution)/shard_map/all_to_all | solution.py:49
  90.8 6.5 %shard_map.72 = (bf16[5,256,128]{2,1,0:T(8,128)(2,1)}, f32[8,128]{1,0:T(8,128)}) custom-call(s32[1,16]{1,0:T(1,128)} %vertical.3, s32[1,8]{1,0:T(1,128)} %slash.3, s32[1]{0:T(128)} %bitcast.position, bf16[5,256,128]{2,1,0:T(8,128)(2,1)} %bitcast.12, bf16[18,256,128]{2,1,0:T(8,128)(2,1)} %copy-done, bf16[18,256,128]{2,1,0:T(8,128)(2,1)} %collective-permute-done.5.theirs), custom_call_target="tpu_custom_call" | custom-call | flops 1006632960 | bytes 2097152 | tf_op jit(solution)/shard_map/pallas_call | solution.py:286
  97.3 4.6 %all-to-all-done.3.stats = f32[32,2,256]{2,1,0:T(2,128)S(1)} async-done(((f32[32,2,256]{2,1,0:T(2,128)}), f32[32,2,256]{2,1,0:T(2,128)S(1)}, u32[]{:S(2)}, u32[]{:S(2)}) %all-to-all-start.3) | async-done | bytes 65568 | tf_op jit(solution)/shard_map/all_to_all | solution.py:49
  102.6 1.2 %shard_map.75 = f32[16,1,256]{2,1,0:T(1,128)} custom-call(f32[32,2,256]{2,1,0:T(2,128)S(1)} %all-to-all-done.3.stats, f32[512,256]{1,0:T(8,128)S(1)} %get-tuple-element.22.scores, f32[8,128]{1,0:T(8,128)S(1)} %copy-done.3), custom_call_target="tpu_custom_call" | custom-call | tf_op jit(solution)/shard_map/pallas_call | solution.py:195
  103.9 6.1 %all-to-all-start.4 = ((f32[16,1,256]{2,1,0:T(1,128)}), f32[16,1,256]{2,1,0:T(1,128)S(1)}, u32[]{:S(2)}, u32[]{:S(2)}) async-start(f32[16,1,256]{2,1,0:T(1,128)} %shard_map.75), calls=%async_computation.4 | async-start | bytes 32768 | tf_op jit(solution)/shard_map/all_to_all | solution.py:49
  109.9 6.5 %shard_map.73 = (bf16[5,256,128]{2,1,0:T(8,128)(2,1)}, f32[8,128]{1,0:T(8,128)}) custom-call(s32[1,16]{1,0:T(1,128)} %vertical.3, s32[1,8]{1,0:T(1,128)} %slash.3, s32[1]{0:T(128)} %bitcast.position, bf16[5,256,128]{2,1,0:T(8,128)(2,1)} %bitcast.13, bf16[18,256,128]{2,1,0:T(8,128)(2,1)} %copy-done, ...), custom_call_target="tpu_custom_call", output_to_operand_aliasing={{0}: (6, {})} | custom-call | flops 1006632960 | bytes 2097152 | tf_op jit(solution)/shard_map/pallas_call | solution.py:286
  (18 shorter events, 2.8 us)
Async XLA Ops:
  0.6 43.5 %copy-start.1 = (bf16[256,1,128]{2,0,1:T(8,128)(2,1)S(1)}, bf16[256,1,128]{2,0,1:T(8,128)(2,1)}, u32[]{:S(2)}) copy-start(bf16[256,1,128]{2,0,1:T(8,128)(2,1)} %param.6) | copy-start | bytes 196612
  3.2 74.2 %copy-start.2 = (bf16[2,256,128]{2,1,0:T(8,128)(2,1)S(1)}, bf16[2,256,128]{2,1,0:T(8,128)(2,1)}, u32[]{:S(2)}) copy-start(bf16[2,256,128]{2,1,0:T(8,128)(2,1)} %get-tuple-element.13.refs_0_) | copy-start | bytes 393220
  3.2 35.6 %all-to-all-start = ((bf16[64,8,128]{2,1,0:T(8,128)(2,1)}), bf16[64,8,128]{2,1,0:T(8,128)(2,1)S(1)}, u32[]{:S(2)}, u32[]{:S(2)}) async-start(bf16[64,8,128]{2,1,0:T(8,128)(2,1)} %bitcast.14), calls=%async_computation | async-start | bytes 262144 | tf_op jit(solution)/shard_map/all_to_all | solution.py:49
  21.0 13.0 %collective-permute-start.1 = (bf16[2,256,128]{2,1,0:T(8,128)(2,1)}, bf16[2,256,128]{2,1,0:T(8,128)(2,1)S(1)}, u32[]{:S(2)}, u32[]{:S(2)}) collective-permute-start(bf16[2,256,128]{2,1,0:T(8,128)(2,1)} %get-tuple-element.13.refs_0_), channel_id=1, source_target_pairs={{0,48},{16,64},{32,80},{48,96},{64,112},{80,128},{96,144},{112,160... | collective-permute-start | bytes 393224 | tf_op jit(solution)/shard_map/ppermute | solution.py:314
  26.4 12.4 %collective-permute-start = (bf16[2,256,128]{2,1,0:T(8,128)(2,1)}, bf16[2,256,128]{2,1,0:T(8,128)(2,1)S(1)}, u32[]{:S(2)}, u32[]{:S(2)}) collective-permute-start(bf16[2,256,128]{2,1,0:T(8,128)(2,1)} %get-tuple-element.13.refs_0_), channel_id=1, source_target_pairs={{0,16},{16,32},{32,48},{48,64},{64,80},{80,96},{96,112},{112,128},... | collective-permute-start | bytes 393224 | tf_op jit(solution)/shard_map/ppermute | solution.py:314
  28.3 21.2 %collective-permute-start.2 = (bf16[2,256,128]{2,1,0:T(8,128)(2,1)}, bf16[2,256,128]{2,1,0:T(8,128)(2,1)S(1)}, u32[]{:S(2)}, u32[]{:S(2)}) collective-permute-start(bf16[2,256,128]{2,1,0:T(8,128)(2,1)} %get-tuple-element.13.refs_0_), channel_id=1, source_target_pairs={{0,64},{16,80},{32,96},{48,112},{64,128},{80,144},{96,160},{112,17... | collective-permute-start | bytes 393224 | tf_op jit(solution)/shard_map/ppermute | solution.py:314
  38.8 0.7 copy-start.4
  40.8 10.2 %all-to-all-start.1 = ((bf16[4,80,128]{2,1,0:T(8,128)(2,1)}), bf16[4,80,128]{2,1,0:T(8,128)(2,1)S(1)}, u32[]{:S(2)}, u32[]{:S(2)}) async-start(bf16[4,80,128]{2,1,0:T(8,128)(2,1)} %get-tuple-element.15), calls=%async_computation.1 | async-start | bytes 163840 | tf_op jit(solution)/shard_map/all_to_all | solution.py:49
  44.1 5.4 %collective-permute-start.3 = (bf16[256,128]{1,0:T(8,128)(2,1)S(1)}, bf16[256,128]{1,0:T(8,128)(2,1)S(1)}, u32[]{:S(2)}, u32[]{:S(2)}) collective-permute-start(bf16[256,128]{1,0:T(8,128)(2,1)S(1)} %bitcast.9), channel_id=1, source_target_pairs={{0,8},{8,0},{1,9},{9,1},{2,10},{10,2},{3,11},{11,3},{4,12},{12,4},... | collective-permute-start | bytes 196616 | tf_op jit(solution)/shard_map/ppermute | solution.py:315
  52.0 25.4 %all-to-all-start.2 = ((bf16[8,288,128]{2,1,0:T(8,128)(2,1)}), bf16[8,288,128]{2,1,0:T(8,128)(2,1)S(1)}, u32[]{:S(2)}, u32[]{:S(2)}) async-start(bf16[8,288,128]{2,1,0:T(8,128)(2,1)} %get-tuple-element.18), calls=%async_computation.2 | async-start | bytes 1179648 | tf_op jit(solution)/shard_map/all_to_all | solution.py:49
  58.9 18.4 %collective-permute-start.4 = (bf16[2,256,128]{2,1,0:T(8,128)(2,1)S(1)}, bf16[2,256,128]{2,1,0:T(8,128)(2,1)S(1)}, u32[]{:S(2)}, u32[]{:S(2)}) collective-permute-start(bf16[2,256,128]{2,1,0:T(8,128)(2,1)S(1)} %get-tuple-element.17), channel_id=1, source_target_pairs={{0,16},{16,32},{32,48},{48,64},{64,80},{80,96},{96,112},{112,128},... | collective-permute-start | bytes 393224 | tf_op jit(solution)/shard_map/ppermute | solution.py:314
  78.3 12.5 %copy-start = (bf16[18,256,128]{2,1,0:T(8,128)(2,1)}, bf16[18,256,128]{2,1,0:T(8,128)(2,1)S(1)}, u32[]{:S(2)}) copy-start(bf16[18,256,128]{2,1,0:T(8,128)(2,1)S(1)} %shard_map.71.ours) | copy-start | bytes 3538948
  78.3 12.4 %collective-permute-start.5 = (bf16[18,256,128]{2,1,0:T(8,128)(2,1)S(1)}, bf16[18,256,128]{2,1,0:T(8,128)(2,1)}, u32[]{:S(2)}, u32[]{:S(2)}) collective-permute-start(bf16[18,256,128]{2,1,0:T(8,128)(2,1)S(1)} %shard_map.71.ours), channel_id=1, source_target_pairs={{0,8},{8,0},{1,9},{9,1},{2,10},{10,2},{3,11},{11,3},{4,12},{12,4},... | collective-permute-start | bytes 3538952 | tf_op jit(solution)/shard_map/ppermute | solution.py:315
  83.8 18.1 %all-to-all-start.3 = ((f32[32,2,256]{2,1,0:T(2,128)}), f32[32,2,256]{2,1,0:T(2,128)S(1)}, u32[]{:S(2)}, u32[]{:S(2)}) async-start(f32[32,2,256]{2,1,0:T(2,128)} %get-tuple-element.21), calls=%async_computation.3 | async-start | bytes 131072 | tf_op jit(solution)/shard_map/all_to_all | solution.py:49
  102.0 0.7 copy-start.3
  103.9 12.6 %all-to-all-start.4 = ((f32[16,1,256]{2,1,0:T(1,128)}), f32[16,1,256]{2,1,0:T(1,128)S(1)}, u32[]{:S(2)}, u32[]{:S(2)}) async-start(f32[16,1,256]{2,1,0:T(1,128)} %shard_map.75), calls=%async_computation.4 | async-start | bytes 32768 | tf_op jit(solution)/shard_map/all_to_all | solution.py:49

commit v5 on v4

v5 whole, which is shorter than its diff:
```python
import functools
import math

import jax
import jax.numpy as jnp
from jax import lax
from jax.experimental import pallas as pl
from jax.experimental.pallas import tpu as pltpu
from jax.sharding import Mesh
from jax.sharding import PartitionSpec as P

BLK = 128
LAST = 64
NV = 16
NS = 8
HEADS = 40
HD = 128
GROUP = 5
FAR = -1e30
LOG2E = math.log2(math.e)
CHIP = ("y", "zhi", "zlo")
CTX = CHIP + ("core",)
NY, NZ = 8, 4
PER_ROW = 2 * NZ
CHIPS = NY * NZ
PIECES = CHIPS // 2
PIECE = BLK // PIECES
LISTED = NV * PIECE
UNIT = LISTED
NEAR = NS * BLK // UNIT
BACK = 5
QROWS = 16
QREAL = GROUP * LAST // 2
QALL = 256
NT = (((1,), (1,)), ((), ()))
SMEM = pl.BlockSpec(memory_space=pltpu.SMEM)
VMEM = pl.BlockSpec(memory_space=pltpu.VMEM)
ANY = pl.BlockSpec(memory_space=pl.ANY)
F32 = jnp.float32
BF16 = jnp.bfloat16
LARGE = pltpu.CompilerParams(vmem_limit_bytes=60 * 1024 * 1024)
MIDDLE = pltpu.CompilerParams(vmem_limit_bytes=32 * 1024 * 1024)
SMALL = pltpu.CompilerParams(vmem_limit_bytes=8 * 1024 * 1024)


def shape(kind, *dims):
    return jax.ShapeDtypeStruct(dims, kind)


def exchange(x, axis):
    return lax.all_to_all(x, axis, 0, 0)


def pack_kernel(position, q, k, v, sent, kv, last, sem):
    local = k.shape[0]
    copy = pltpu.make_async_copy(q.at[:, pl.ds(local - LAST, LAST)], last, sem)
    copy.start()

    def spread(pieces):
        for y in range(NY):
            for zhi in range(NZ // 2):
                for zlo in range(2):
                    for c in range(2):
                        sent[((y * NZ // 2 + zhi) * 2 + zlo) * 2 + c] = pieces[c][2 * y + zlo]

    cut = []
    for which, x in enumerate((k, v)):
        kv[which * local // UNIT : (which + 1) * local // UNIT] = x[...].reshape(local // UNIT, UNIT, HD)
        x = x[...].astype(F32).reshape(2, PIECES, PIECE, HD)
        cut.append(jnp.concatenate([x[0], x[1]], axis=1).astype(BF16))
    spread(cut)
    copy.wait()

    @pl.when(position[0] == 2 * CHIPS - 1)
    def _():
        flat = last[...].reshape(GROUP * LAST, HD)
        flat = jnp.concatenate([flat, jnp.zeros((2 * local - GROUP * LAST, HD), BF16)], axis=0)
        flat = flat.reshape(PIECES, 2, 2 * PIECE, HD)
        spread([flat[:, 0], flat[:, 1]])


def pack(position, q_t, k, v):
    local = k.shape[0]
    return pl.pallas_call(
        pack_kernel,
        out_shape=(shape(BF16, 2 * CHIPS, 2 * PIECE, HD), shape(BF16, 2 * local // UNIT, UNIT, HD)),
        in_specs=[SMEM, ANY, VMEM, VMEM],
        out_specs=(VMEM, VMEM),
        scratch_shapes=[pltpu.VMEM((GROUP, LAST, HD), BF16), pltpu.SemaphoreType.DMA],
        compiler_params=LARGE,
    )(position, q_t, k, v)


def choose_kernel(ids, out):
    wanted, given = out.shape
    row = lax.broadcasted_iota(jnp.int32, (wanted, HD), 0)
    source = given - wanted + row
    for j in range(NV):
        source = jnp.where(row // PIECE == j, ids[0, j] * PIECE + row % PIECE, source)
    column = lax.broadcasted_iota(jnp.int32, (wanted, HD), 1)
    for i in range(0, given, HD):
        out[:, i : i + HD] = (column + i == source).astype(F32).astype(BF16)


def choose(vertical):
    return pl.pallas_call(
        choose_kernel,
        out_shape=shape(BF16, LISTED + QROWS, 4 * CHIPS * PIECE),
        in_specs=[SMEM],
        out_specs=VMEM,
        compiler_params=SMALL,
    )(vertical)


def pick_kernel(chosen, r, one, three, out):
    rows = r[...].reshape(4 * CHIPS * PIECE, HD)
    tile = jnp.dot(chosen[...], rows, preferred_element_type=F32).astype(BF16)
    for d in range(PIECES):
        out[d] = tile


def pick(chosen, r, one, three):
    return pl.pallas_call(
        pick_kernel,
        out_shape=shape(BF16, PIECES, LISTED + QROWS, HD),
        in_specs=[VMEM, VMEM, ANY, ANY],
        out_specs=VMEM,
        compiler_params=SMALL,
    )(chosen, r, one, three)


def together_kernel(*refs):
    *parts, mine, after, out, sems = refs
    n = len(parts)
    each = parts[0].shape[0]
    copies = [pltpu.make_async_copy(part, out.at[pl.ds(each * i, each)], sems.at[i]) for i, part in enumerate(parts)]
    copies.append(pltpu.make_async_copy(mine.at[:, pl.ds(0, LISTED)], out.at[pl.ds(each * n, PIECES)], sems.at[n]))
    for copy in copies:
        copy.start()
    for copy in copies:
        copy.wait()


def together(parts, mine, after):
    n = len(parts)
    return pl.pallas_call(
        together_kernel,
        out_shape=shape(BF16, n * parts[0].shape[0] + PIECES, UNIT, HD),
        in_specs=[ANY] * (n + 2),
        out_specs=ANY,
        scratch_shapes=[pltpu.SemaphoreType.DMA((n + 1,))],
        compiler_params=SMALL,
    )(*parts, mine, after)


def estimate_kernel(total_len, position, q, k_mine, k_theirs, scores, stats):
    tokens = 2 * k_mine.shape[0]
    core = position[0] & 1
    mine, theirs = k_mine[...], k_theirs[...]
    k = jnp.concatenate([jnp.where(core == 0, mine, theirs), jnp.where(core == 0, theirs, mine)], axis=0)
    s = lax.dot_general(k, q[...], NT, preferred_element_type=F32) * (1.0 / math.sqrt(HD))
    column = lax.broadcasted_iota(jnp.int32, (1, QALL), 1)
    last_pos = total_len - LAST + ((column >> 4) * 32 + core * 16 + (column & 15)) % LAST
    key_pos = (position[0] >> 1) * tokens + lax.broadcasted_iota(jnp.int32, (tokens, QALL), 0)
    s = jnp.where(key_pos <= last_pos, s, FAR)
    scores[...] = s
    top = jnp.max(s, axis=0, keepdims=True)
    total = jnp.sum(jnp.exp(s - top), axis=0, keepdims=True)
    both = jnp.concatenate([top, total], axis=0)
    for d in range(CHIPS):
        stats[d] = both


def estimate(position, q, k_mine, k_theirs, total_len):
    return pl.pallas_call(
        functools.partial(estimate_kernel, total_len),
        out_shape=(shape(F32, 2 * k_mine.shape[0], QALL), shape(F32, CHIPS, 2, QALL)),
        in_specs=[SMEM, VMEM, VMEM, VMEM],
        out_specs=(VMEM, VMEM),
        compiler_params=SMALL,
    )(position, q, k_mine, k_theirs)


def mass_kernel(factor, stats, scores, after, out):
    tops, totals = stats[:, 0, :], stats[:, 1, :]
    top = jnp.max(tops, axis=0, keepdims=True)
    total = jnp.sum(totals * jnp.exp(tops - top), axis=0, keepdims=True)
    p = jnp.exp(scores[...] - (top + jnp.log(total)))
    kvh, local = out.shape[0] // 2, out.shape[2]
    real = (lax.broadcasted_iota(jnp.int32, (kvh, QALL), 1) < QREAL).astype(BF16)
    high = p.astype(BF16)
    low = (p - high.astype(F32)).astype(BF16)
    mass = sum(lax.dot_general(real, x, NT, preferred_element_type=F32) for x in (high, low)) * factor
    for c in range(2):
        out[c * kvh : (c + 1) * kvh, 0, :] = mass[:, c * local : (c + 1) * local]


def mass(stats, scores, after, kvh, factor):
    return pl.pallas_call(
        functools.partial(mass_kernel, factor),
        out_shape=shape(F32, 2 * kvh, 1, scores.shape[0] // 2),
        in_specs=[VMEM, VMEM, ANY],
        out_specs=VMEM,
        compiler_params=SMALL,
    )(stats, scores, after)


def attend_kernel(e, vertical, slash, position, q, ours, theirs, *rest):
    if e:
        rest = rest[1:]
    out, token, q_buf, o_buf, k_all, v_all, sems = rest
    token[...] = jnp.zeros_like(token)
    core = position[0] & 1
    block = position[0] * 2 + e
    near = [block] + [block - jnp.where(slash[0, j] == 0, slash[0, 0], slash[0, j]) for j in range(1, NS)]
    copies = [pltpu.make_async_copy(q.at[:, pl.ds(e * BLK, BLK)], q_buf, sems.at[0])]
    copies[0].start()

    def fetch(from_ours, source, target):
        sem = sems.at[len(copies)]
        copy = pltpu.make_async_copy(source(ours), target, sem)
        other = pltpu.make_async_copy(source(theirs), target, sem)
        pl.when(from_ours)(copy.start)
        pl.when(jnp.logical_not(from_ours))(other.start)
        copies.append(copy)

    per = BLK // UNIT
    for j in range(NS):
        kept = jnp.where(near[j] >= 0, near[j], block)
        chips = (position[0] >> 1) - (kept >> 2)
        to = pl.ds(j * per, per)
        for which, target in ((0, k_all.at[to]), (1, v_all.at[to, :, pl.ds(0, HD)])):
            unit = (2 * chips + which) * 2 * per + (kept & 1) * per
            fetch(((kept >> 1) & 1) == core, lambda x: x.at[pl.ds(unit, per)], target)
    v_all[:NEAR, :, HD:] = jnp.ones((NEAR, UNIT, HD), BF16)

    row = lax.broadcasted_iota(jnp.int32, (UNIT, HD), 0)
    drop = jnp.zeros((UNIT, HD), jnp.int32)
    for j in range(NV):
        c = vertical[0, j]
        bad = c > block
        for other in near:
            bad = bad | (c == other)
        drop = jnp.where(row // PIECE == j, bad.astype(jnp.int32), drop)
    drop = drop.astype(F32)
    keep = (1.0 - drop).astype(BF16)
    drop = drop.astype(BF16)
    first = ours[e * per, 0:1, :]
    instead = first * drop
    listed = ours.shape[0] - PIECES
    for c, (k, v) in enumerate(((ours, theirs), (theirs, ours))):

        @pl.when(core == c)
        def _(k=k, v=v):
            for i in range(PIECES):
                k_all[NEAR + i] = k[listed + i] * keep + instead
                v_all[NEAR + i, :, :HD] = v[listed + i] * keep

    for i in range(PIECES):
        v_all[NEAR + i, :, HD:] = keep
    for copy in copies:
        copy.wait()
    for j in range(1, NS):

        @pl.when(near[j] < 0)
        def _(j=j):
            to = slice(j * per, (j + 1) * per)
            k_all[to] = jnp.broadcast_to(first, (per, UNIT, HD))
            v_all[to] = jnp.zeros((per, UNIT, 2 * HD), BF16)

    factor = LOG2E / math.sqrt(HD)
    causal = lax.broadcasted_iota(jnp.int32, (BLK, BLK), 1) <= lax.broadcasted_iota(jnp.int32, (BLK, BLK), 0)
    keys = k_all[...].reshape((NV + NS) * BLK, HD)
    values = v_all[...].reshape((NV + NS) * BLK, 2 * HD)
    pair = 2

    def score(h):
        n = min(pair, GROUP - h)
        tile = q_buf[h : h + n].reshape(n * BLK, HD)
        s = lax.dot_general(tile, keys, NT, preferred_element_type=F32)
        own = jnp.where(jnp.concatenate([causal] * n, axis=0), s[:, :BLK], FAR)
        s = jnp.concatenate([own, s[:, BLK:]], axis=1)
        return s, jnp.max(s, axis=1, keepdims=True) * factor

    def finish(h, s, top):
        n = min(pair, GROUP - h)
        w = jnp.exp2(s * factor - top).astype(BF16)
        o = jnp.dot(w, values, preferred_element_type=F32)
        o_buf[h : h + n] = (o[:, :HD] / o[:, HD:]).astype(BF16).reshape(n, BLK, HD)
        copies.append(pltpu.make_async_copy(o_buf.at[pl.ds(h, n)], out.at[pl.ds(h, n), pl.ds(e * BLK, BLK)], sems.at[h]))
        copies[-1].start()

    held = score(0)
    for h in range(0, GROUP, pair):
        later = score(h + pair) if h + pair < GROUP else None
        finish(h, *held)
        held = later
    for copy in copies[2 * NS + 1 :]:
        copy.wait()


def attend(e, vertical, slash, position, q_t, ours, theirs, out=None):
    local = q_t.shape[1]
    args = (vertical, slash, position, q_t, ours, theirs) + ((out,) if e else ())
    return pl.pallas_call(
        functools.partial(attend_kernel, e),
        out_shape=(shape(BF16, GROUP, local, HD), shape(F32, 8, 128)),
        in_specs=[SMEM] * 3 + [ANY, VMEM, VMEM] + [ANY] * (len(args) - 6),
        out_specs=(ANY, VMEM),
        scratch_shapes=[
            pltpu.VMEM((GROUP, BLK, HD), BF16),
            pltpu.VMEM((GROUP, BLK, HD), BF16),
            pltpu.VMEM((NEAR + PIECES, UNIT, HD), BF16),
            pltpu.VMEM((NEAR + PIECES, UNIT, 2 * HD), BF16),
            pltpu.SemaphoreType.DMA((2 * NS + 1,)),
        ],
        input_output_aliases={len(args) - 1: 0} if e else {},
        compiler_params=MIDDLE,
        cost_estimate=pl.CostEstimate(
            flops=4 * GROUP * (NV + NS) * BLK**3, bytes_accessed=2 * 1024 * 1024, transcendentals=GROUP * (NV + NS) * BLK**2
        ),
    )(*args)


def on_device(queries, key_rows, value_rows, vertical, slash_offsets):
    local = key_rows.shape[0]
    total_len = local * NY * PER_ROW
    place = lax.axis_index(CTX).reshape(1)
    q_t = jnp.transpose(queries, (1, 0, 2))
    k, v = key_rows[:, 0], value_rows[:, 0]

    sent, kv = pack(place, q_t, k, v)
    back = lambda x, chips: lax.ppermute(x, CHIP, [(i, (i + chips) % CHIPS) for i in range(CHIPS)])
    swap = lambda x: lax.ppermute(x, "core", [(0, 1), (1, 0)])
    one, three = back(kv, 1), back(kv, 3)
    r = exchange(sent, CTX)
    mine = exchange(pick(choose(vertical), r, one, three), ("y", "zlo"))
    k_theirs, two, four = swap(k), back(three, -1), back(kv, 4)
    scores, stats = estimate(place, mine[:, LISTED:].reshape(QALL, HD), k, k_theirs, total_len)
    ours = together([kv, one, two, three, four], mine, k_theirs)
    theirs = swap(ours)

    given = (vertical, slash_offsets, place, q_t, ours, theirs)
    out, token = attend(0, *given)
    stats = exchange(stats, CHIP)
    part = exchange(mass(stats, scores, token, lax.axis_size("kvh"), total_len / LAST / HEADS), ("core", "kvh"))
    out, token = attend(1, *given, out)
    profile = jnp.sum(part, axis=(0, 1))
    return jnp.transpose(out, (1, 0, 2)), profile


def solution(mesh):
    wide = Mesh(mesh.devices.reshape(NY, NZ // 2, 2, 2, -1), CTX + ("kvh",))
    return jax.shard_map(
        on_device,
        mesh=wide,
        in_specs=(P(CTX, "kvh", None), P(CTX, "kvh", None), P(CTX, "kvh", None), P("kvh", None), P("kvh", None)),
        out_specs=(P(CTX, "kvh", None), P(CTX)),
        check_vma=False,
    )
```

time: 118 us -> 109 us (0.924)
  starting transfers between devices: 63 us -> 57.1 us
  Pallas kernels: 21 us -> 19 us
    all_to_all x5 -> x4, starting transfers between devices: 41 us -> 36 us  [exchange(): return lax.all_to_all(x, axis, 0, 0)]
    ppermute x2, starting transfers between devices: 9.06 us -> 7.5 us  [on_device(): swap = lambda x: lax.ppermute(x, 'core', [(0, 1), (1, 0)])]
    pallas_call x2, Pallas kernels: 13.1 us -> 11.9 us  [attend(): pl.pallas_call(functools.partial(attend_kernel, e), out_shape=(shape(BF16...]
    all_to_all x5 -> x4, waiting for transfers between devices: 6.14 us -> 5.51 us  [exchange(): return lax.all_to_all(x, axis, 0, 0)]
  transfers between devices with their start and end apart: 11 -> 10, of which waited for: 6 -> 6; matrix products, arithmetic and copies ran while one was open for 0% -> 0% of each run, Pallas kernels for 13% -> 12%
where the time goes in v5:
time: 109 us; the launch traced here: 108 us
  starting transfers between devices  57.1 us (52%)
  waiting for transfers between devices  30.2 us (28%)
  Pallas kernels  19 us (17%)
    all_to_all x4, starting transfers between devices, exchange(): return lax.all_to_all(x, axis, 0, 0)  36 us
    ppermute x4, waiting for transfers between devices, on_device(): lax.ppermute(x, CHIP, [(i, (i + chips) % CHIPS) for i in range(CHIPS)])  23.8 us
    ppermute x4, starting transfers between devices, on_device(): lax.ppermute(x, CHIP, [(i, (i + chips) % CHIPS) for i in range(CHIPS)])  13.6 us
    pallas_call x2, Pallas kernels, attend(): pl.pallas_call(functools.partial(attend_kernel, e), out_shape=(shape(BF16...  11.9 us
    ppermute x2, starting transfers between devices, on_device(): swap = lambda x: lax.ppermute(x, 'core', [(0, 1), (1, 0)])  7.5 us
    all_to_all x4, waiting for transfers between devices, exchange(): return lax.all_to_all(x, axis, 0, 0)  5.51 us
    pallas_call x1, Pallas kernels, pack(): pl.pallas_call(pack_kernel, out_shape=(shape(BF16, 2 * CHIPS, 2 * PIECE,...  2.51 us
  transfers between devices with their start and end apart: 10, of which 6 were waited for; matrix products, arithmetic and copies ran while one was open for 0% of the time, Pallas kernels for 12%

profile of v5, /device:TPU:1, one launch (start us, length us, event | category | flops | bytes accessed | tf_op | source)
XLA Modules:
  0.0 108.4 jit_solution(344595526836284069)
XLA Ops:
  0.6 2.5 %shard_map.68 = (bf16[64,16,128]{2,1,0:T(8,128)(2,1)}, bf16[4,128,128]{2,1,0:T(8,128)(2,1)}) custom-call(s32[1]{0:T(128)} %bitcast.position, bf16[5,256,128]{2,1,0:T(8,128)(2,1)} %bitcast.6, bf16[256,128]{1,0:T(8,128)(2,1)} %bitcast.10, bf16[256,128]{1,0:T(8,128)(2,1)} %bitcast.13), custom_call_target="tpu_custom_call" | custom-call | tf_op jit(solution)/shard_map/pallas_call | solution.py:84
  3.2 17.6 %all-to-all-start = ((bf16[64,16,128]{2,1,0:T(8,128)(2,1)}), bf16[64,16,128]{2,1,0:T(8,128)(2,1)S(1)}, u32[]{:S(2)}, u32[]{:S(2)}) async-start(bf16[64,16,128]{2,1,0:T(8,128)(2,1)} %get-tuple-element.10), calls=%async_computation | async-start | bytes 524288 | tf_op jit(solution)/shard_map/all_to_all | solution.py:51
  20.8 5.4 %collective-permute-start.1 = (bf16[4,128,128]{2,1,0:T(8,128)(2,1)}, bf16[4,128,128]{2,1,0:T(8,128)(2,1)S(1)}, u32[]{:S(2)}, u32[]{:S(2)}) collective-permute-start(bf16[4,128,128]{2,1,0:T(8,128)(2,1)} %get-tuple-element.9.refs_0_), channel_id=1, source_target_pairs={{0,48},{16,64},{32,80},{48,96},{64,112},{80,128},{96,144},{112,160... | collective-permute-start | bytes 393224 | tf_op jit(solution)/shard_map/ppermute | solution.py:333
  26.2 1.9 %collective-permute-start = (bf16[4,128,128]{2,1,0:T(8,128)(2,1)}, bf16[4,128,128]{2,1,0:T(8,128)(2,1)S(1)}, u32[]{:S(2)}, u32[]{:S(2)}) collective-permute-start(bf16[4,128,128]{2,1,0:T(8,128)(2,1)} %get-tuple-element.9.refs_0_), channel_id=1, source_target_pairs={{0,16},{16,32},{32,48},{48,64},{64,80},{80,96},{96,112},{112,128},... | collective-permute-start | bytes 393224 | tf_op jit(solution)/shard_map/ppermute | solution.py:333
  28.2 0.6 copy-done.3
  29.4 6.2 %collective-permute-done.1.three.refs_3_ = bf16[4,128,128]{2,1,0:T(8,128)(2,1)S(1)} collective-permute-done((bf16[4,128,128]{2,1,0:T(8,128)(2,1)}, bf16[4,128,128]{2,1,0:T(8,128)(2,1)S(1)}, u32[]{:S(2)}, u32[]{:S(2)}) %collective-permute-start.1) | collective-permute-done | bytes 131104 | tf_op jit(solution)/shard_map/ppermute | solution.py:333
  35.7 5.4 %collective-permute-done.one.refs_1_ = bf16[4,128,128]{2,1,0:T(8,128)(2,1)S(1)} collective-permute-done((bf16[4,128,128]{2,1,0:T(8,128)(2,1)}, bf16[4,128,128]{2,1,0:T(8,128)(2,1)S(1)}, u32[]{:S(2)}, u32[]{:S(2)}) %collective-permute-start) | collective-permute-done | bytes 131104 | tf_op jit(solution)/shard_map/ppermute | solution.py:333
  41.0 1.1 shard_map.70
  42.1 5.1 %all-to-all-start.1 = ((bf16[16,144,128]{2,1,0:T(8,128)(2,1)}), bf16[16,144,128]{2,1,0:T(8,128)(2,1)S(1)}, u32[]{:S(2)}, u32[]{:S(2)}) async-start(bf16[16,144,128]{2,1,0:T(8,128)(2,1)} %shard_map.70), calls=%async_computation.1 | async-start | bytes 1179648 | tf_op jit(solution)/shard_map/all_to_all | solution.py:51
  47.2 3.4 %collective-permute-start.3 = (bf16[4,128,128]{2,1,0:T(8,128)(2,1)S(1)}, bf16[4,128,128]{2,1,0:T(8,128)(2,1)S(1)}, u32[]{:S(2)}, u32[]{:S(2)}) collective-permute-start(bf16[4,128,128]{2,1,0:T(8,128)(2,1)S(1)} %copy-done.2), channel_id=1, source_target_pairs={{0,64},{16,80},{32,96},{48,112},{64,128},{80,144},{96,160},{112,17... | collective-permute-start | bytes 393224 | tf_op jit(solution)/shard_map/ppermute | solution.py:333
  50.7 2.9 %collective-permute-start.2 = (bf16[4,128,128]{2,1,0:T(8,128)(2,1)S(1)}, bf16[4,128,128]{2,1,0:T(8,128)(2,1)S(1)}, u32[]{:S(2)}, u32[]{:S(2)}) collective-permute-start(bf16[4,128,128]{2,1,0:T(8,128)(2,1)S(1)} %collective-permute-done.1.three.refs_3_), channel_id=1, source_target_pairs={{0,496},{16,0},{32,16},{48,32},{64,48},{80,64},{96,80},{112,96},{1... | collective-permute-start | bytes 393224 | tf_op jit(solution)/shard_map/ppermute | solution.py:333
  53.5 4.9 %collective-permute-start.4 = (bf16[256,128]{1,0:T(8,128)(2,1)S(1)}, bf16[256,128]{1,0:T(8,128)(2,1)S(1)}, u32[]{:S(2)}, u32[]{:S(2)}) collective-permute-start(bf16[256,128]{1,0:T(8,128)(2,1)S(1)} %bitcast.11), channel_id=1, source_target_pairs={{0,8},{8,0},{1,9},{9,1},{2,10},{10,2},{3,11},{11,3},{4,12},{12,4},... | collective-permute-start | bytes 196616 | tf_op jit(solution)/shard_map/ppermute | solution.py:334
  58.5 0.9 collective-permute-done.4.refs_6_.k_theirs
  59.4 5.4 %collective-permute-done.3.refs_4_ = bf16[4,128,128]{2,1,0:T(8,128)(2,1)S(1)} collective-permute-done((bf16[4,128,128]{2,1,0:T(8,128)(2,1)S(1)}, bf16[4,128,128]{2,1,0:T(8,128)(2,1)S(1)}, u32[]{:S(2)}, u32[]{:S(2)}) %collective-permute-start.3) | collective-permute-done | bytes 131104 | tf_op jit(solution)/shard_map/ppermute | solution.py:333
  64.8 6.8 %collective-permute-done.2.refs_2_ = bf16[4,128,128]{2,1,0:T(8,128)(2,1)S(1)} collective-permute-done((bf16[4,128,128]{2,1,0:T(8,128)(2,1)S(1)}, bf16[4,128,128]{2,1,0:T(8,128)(2,1)S(1)}, u32[]{:S(2)}, u32[]{:S(2)}) %collective-permute-start.2) | collective-permute-done | bytes 131104 | tf_op jit(solution)/shard_map/ppermute | solution.py:333
  71.6 0.9 shard_map.71.ours
  72.5 2.6 %collective-permute-start.5 = (bf16[36,128,128]{2,1,0:T(8,128)(2,1)S(1)}, bf16[36,128,128]{2,1,0:T(8,128)(2,1)}, u32[]{:S(2)}, u32[]{:S(2)}) collective-permute-start(bf16[36,128,128]{2,1,0:T(8,128)(2,1)S(1)} %shard_map.71.ours), channel_id=1, source_target_pairs={{0,8},{8,0},{1,9},{9,1},{2,10},{10,2},{3,11},{11,3},{4,12},{12,4},... | collective-permute-start | bytes 3538952 | tf_op jit(solution)/shard_map/ppermute | solution.py:334
  75.1 1.0 shard_map.74
  76.1 5.6 %all-to-all-start.2 = ((f32[32,2,256]{2,1,0:T(2,128)}), f32[32,2,256]{2,1,0:T(2,128)S(1)}, u32[]{:S(2)}, u32[]{:S(2)}) async-start(f32[32,2,256]{2,1,0:T(2,128)} %get-tuple-element.13), calls=%async_computation.2 | async-start | bytes 131072 | tf_op jit(solution)/shard_map/all_to_all | solution.py:51
  81.8 5.7 %shard_map.72 = (bf16[5,256,128]{2,1,0:T(8,128)(2,1)}, f32[8,128]{1,0:T(8,128)S(1)}) custom-call(s32[1,16]{1,0:T(1,128)S(1)} %copy-done.4, s32[1,8]{1,0:T(1,128)S(1)} %copy-done.5, s32[1]{0:T(128)} %bitcast.position, bf16[5,256,128]{2,1,0:T(8,128)(2,1)S(1)} %bitcast.7, bf16[36,128,128]{2,1,0:T(8,128)(2,1)S(1)} %shard_map.71.ours, ...), custom_call_target="tpu_custom_call" | custom-call | flops 1006632960 | bytes 2097152 | tf_op jit(solution)/shard_map/pallas_call | solution.py:305
  87.5 5.5 %all-to-all-done.2.stats = f32[32,2,256]{2,1,0:T(2,128)S(1)} async-done(((f32[32,2,256]{2,1,0:T(2,128)}), f32[32,2,256]{2,1,0:T(2,128)S(1)}, u32[]{:S(2)}, u32[]{:S(2)}) %all-to-all-start.2) | async-done | bytes 65568 | tf_op jit(solution)/shard_map/all_to_all | solution.py:51
  93.0 1.0 shard_map.75
  93.9 7.6 %all-to-all-start.3 = ((f32[16,1,256]{2,1,0:T(1,128)}), f32[16,1,256]{2,1,0:T(1,128)S(1)}, u32[]{:S(2)}, u32[]{:S(2)}) async-start(f32[16,1,256]{2,1,0:T(1,128)} %shard_map.75), calls=%async_computation.3 | async-start | bytes 32768 | tf_op jit(solution)/shard_map/all_to_all | solution.py:51
  101.6 6.2 %shard_map.73 = (bf16[5,256,128]{2,1,0:T(8,128)(2,1)}, f32[8,128]{1,0:T(8,128)}) custom-call(s32[1,16]{1,0:T(1,128)S(1)} %copy-done.4, s32[1,8]{1,0:T(1,128)S(1)} %copy-done.5, s32[1]{0:T(128)} %bitcast.position, bf16[5,256,128]{2,1,0:T(8,128)(2,1)S(1)} %bitcast.8, bf16[36,128,128]{2,1,0:T(8,128)(2,1)S(1)} %shard_map.71.ours, ...), custom_call_target="tpu_custom_call", output_to_operand_aliasing={{0}: (6, {})} | custom-call | flops 1006632960 | bytes 2097152 | tf_op jit(solution)/shard_map/pallas_call | solution.py:305
  (18 shorter events, 1.3 us)
Async XLA Ops:
  3.2 37.9 %all-to-all-start = ((bf16[64,16,128]{2,1,0:T(8,128)(2,1)}), bf16[64,16,128]{2,1,0:T(8,128)(2,1)S(1)}, u32[]{:S(2)}, u32[]{:S(2)}) async-start(bf16[64,16,128]{2,1,0:T(8,128)(2,1)} %get-tuple-element.10), calls=%async_computation | async-start | bytes 524288 | tf_op jit(solution)/shard_map/all_to_all | solution.py:51
  20.8 14.9 %collective-permute-start.1 = (bf16[4,128,128]{2,1,0:T(8,128)(2,1)}, bf16[4,128,128]{2,1,0:T(8,128)(2,1)S(1)}, u32[]{:S(2)}, u32[]{:S(2)}) collective-permute-start(bf16[4,128,128]{2,1,0:T(8,128)(2,1)} %get-tuple-element.9.refs_0_), channel_id=1, source_target_pairs={{0,48},{16,64},{32,80},{48,96},{64,112},{80,128},{96,144},{112,160... | collective-permute-start | bytes 393224 | tf_op jit(solution)/shard_map/ppermute | solution.py:333
  26.2 14.8 %collective-permute-start = (bf16[4,128,128]{2,1,0:T(8,128)(2,1)}, bf16[4,128,128]{2,1,0:T(8,128)(2,1)S(1)}, u32[]{:S(2)}, u32[]{:S(2)}) collective-permute-start(bf16[4,128,128]{2,1,0:T(8,128)(2,1)} %get-tuple-element.9.refs_0_), channel_id=1, source_target_pairs={{0,16},{16,32},{32,48},{48,64},{64,80},{80,96},{96,112},{112,128},... | collective-permute-start | bytes 393224 | tf_op jit(solution)/shard_map/ppermute | solution.py:333
  28.1 0.7 copy-start.3
  29.4 17.8 %copy-start.2 = (bf16[4,128,128]{2,1,0:T(8,128)(2,1)S(1)}, bf16[4,128,128]{2,1,0:T(8,128)(2,1)}, u32[]{:S(2)}) copy-start(bf16[4,128,128]{2,1,0:T(8,128)(2,1)} %get-tuple-element.9.refs_0_) | copy-start | bytes 393220
  29.4 24.1 %copy-start.1 = (bf16[256,1,128]{2,0,1:T(8,128)(2,1)S(1)}, bf16[256,1,128]{2,0,1:T(8,128)(2,1)}, u32[]{:S(2)}) copy-start(bf16[256,1,128]{2,0,1:T(8,128)(2,1)} %param.6) | copy-start | bytes 196612
  42.1 29.5 %all-to-all-start.1 = ((bf16[16,144,128]{2,1,0:T(8,128)(2,1)}), bf16[16,144,128]{2,1,0:T(8,128)(2,1)S(1)}, u32[]{:S(2)}, u32[]{:S(2)}) async-start(bf16[16,144,128]{2,1,0:T(8,128)(2,1)} %shard_map.70), calls=%async_computation.1 | async-start | bytes 1179648 | tf_op jit(solution)/shard_map/all_to_all | solution.py:51
  47.2 34.6 %copy-start = (bf16[256,5,128]{2,0,1:T(8,128)(2,1)S(1)}, bf16[256,5,128]{2,0,1:T(8,128)(2,1)}, u32[]{:S(2)}) copy-start(bf16[256,5,128]{2,0,1:T(8,128)(2,1)} %param.5) | copy-start | bytes 983044
  47.2 34.6 %copy-start.4 = (s32[1,16]{1,0:T(1,128)S(1)}, s32[1,16]{1,0:T(1,128)}, u32[]{:S(2)}) copy-start(s32[1,16]{1,0:T(1,128)} %vertical.3) | copy-start | bytes 196
  47.2 34.6 %copy-start.5 = (s32[1,8]{1,0:T(1,128)S(1)}, s32[1,8]{1,0:T(1,128)}, u32[]{:S(2)}) copy-start(s32[1,8]{1,0:T(1,128)} %slash.3) | copy-start | bytes 100
  47.2 17.6 %collective-permute-start.3 = (bf16[4,128,128]{2,1,0:T(8,128)(2,1)S(1)}, bf16[4,128,128]{2,1,0:T(8,128)(2,1)S(1)}, u32[]{:S(2)}, u32[]{:S(2)}) collective-permute-start(bf16[4,128,128]{2,1,0:T(8,128)(2,1)S(1)} %copy-done.2), channel_id=1, source_target_pairs={{0,64},{16,80},{32,96},{48,112},{64,128},{80,144},{96,160},{112,17... | collective-permute-start | bytes 393224 | tf_op jit(solution)/shard_map/ppermute | solution.py:333
  50.7 20.9 %collective-permute-start.2 = (bf16[4,128,128]{2,1,0:T(8,128)(2,1)S(1)}, bf16[4,128,128]{2,1,0:T(8,128)(2,1)S(1)}, u32[]{:S(2)}, u32[]{:S(2)}) collective-permute-start(bf16[4,128,128]{2,1,0:T(8,128)(2,1)S(1)} %collective-permute-done.1.three.refs_3_), channel_id=1, source_target_pairs={{0,496},{16,0},{32,16},{48,32},{64,48},{80,64},{96,80},{112,96},{1... | collective-permute-start | bytes 393224 | tf_op jit(solution)/shard_map/ppermute | solution.py:333
  53.5 5.8 %collective-permute-start.4 = (bf16[256,128]{1,0:T(8,128)(2,1)S(1)}, bf16[256,128]{1,0:T(8,128)(2,1)S(1)}, u32[]{:S(2)}, u32[]{:S(2)}) collective-permute-start(bf16[256,128]{1,0:T(8,128)(2,1)S(1)} %bitcast.11), channel_id=1, source_target_pairs={{0,8},{8,0},{1,9},{9,1},{2,10},{10,2},{3,11},{11,3},{4,12},{12,4},... | collective-permute-start | bytes 196616 | tf_op jit(solution)/shard_map/ppermute | solution.py:334
  72.5 9.2 %collective-permute-start.5 = (bf16[36,128,128]{2,1,0:T(8,128)(2,1)S(1)}, bf16[36,128,128]{2,1,0:T(8,128)(2,1)}, u32[]{:S(2)}, u32[]{:S(2)}) collective-permute-start(bf16[36,128,128]{2,1,0:T(8,128)(2,1)S(1)} %shard_map.71.ours), channel_id=1, source_target_pairs={{0,8},{8,0},{1,9},{9,1},{2,10},{10,2},{3,11},{11,3},{4,12},{12,4},... | collective-permute-start | bytes 3538952 | tf_op jit(solution)/shard_map/ppermute | solution.py:334
  76.1 16.9 %all-to-all-start.2 = ((f32[32,2,256]{2,1,0:T(2,128)}), f32[32,2,256]{2,1,0:T(2,128)S(1)}, u32[]{:S(2)}, u32[]{:S(2)}) async-start(f32[32,2,256]{2,1,0:T(2,128)} %get-tuple-element.13), calls=%async_computation.2 | async-start | bytes 131072 | tf_op jit(solution)/shard_map/all_to_all | solution.py:51
  93.9 13.9 %all-to-all-start.3 = ((f32[16,1,256]{2,1,0:T(1,128)}), f32[16,1,256]{2,1,0:T(1,128)S(1)}, u32[]{:S(2)}, u32[]{:S(2)}) async-start(f32[16,1,256]{2,1,0:T(1,128)} %shard_map.75), calls=%async_computation.3 | async-start | bytes 32768 | tf_op jit(solution)/shard_map/all_to_all | solution.py:51

commit v6 on v5

--- a/solution.py
+++ b/solution.py
@@ -36,6 +36,7 @@
 SMEM = pl.BlockSpec(memory_space=pltpu.SMEM)
 VMEM = pl.BlockSpec(memory_space=pltpu.VMEM)
 ANY = pl.BlockSpec(memory_space=pl.ANY)
+HBM = pl.BlockSpec(memory_space=pltpu.HBM)
 F32 = jnp.float32
 BF16 = jnp.bfloat16
 LARGE = pltpu.CompilerParams(vmem_limit_bytes=60 * 1024 * 1024)
@@ -112,21 +113,21 @@
     )(vertical)
 
 
-def pick_kernel(chosen, r, one, three, out):
+def pick_kernel(chosen, r, three, four, k_theirs, out):
     rows = r[...].reshape(4 * CHIPS * PIECE, HD)
     tile = jnp.dot(chosen[...], rows, preferred_element_type=F32).astype(BF16)
     for d in range(PIECES):
         out[d] = tile
 
 
-def pick(chosen, r, one, three):
+def pick(chosen, r, three, four, k_theirs):
     return pl.pallas_call(
         pick_kernel,
         out_shape=shape(BF16, PIECES, LISTED + QROWS, HD),
-        in_specs=[VMEM, VMEM, ANY, ANY],
+        in_specs=[VMEM, VMEM, ANY, ANY, ANY],
         out_specs=VMEM,
         compiler_params=SMALL,
-    )(chosen, r, one, three)
+    )(chosen, r, three, four, k_theirs)
 
 
 def together_kernel(*refs):
@@ -205,48 +206,43 @@
     )(stats, scores, after)
 
 
-def attend_kernel(e, vertical, slash, position, q, ours, theirs, *rest):
-    if e:
-        rest = rest[1:]
-    out, token, q_buf, o_buf, k_all, v_all, sems = rest
-    token[...] = jnp.zeros_like(token)
-    core = position[0] & 1
+def block_numbers(e, slash, position):
     block = position[0] * 2 + e
-    near = [block] + [block - jnp.where(slash[0, j] == 0, slash[0, 0], slash[0, j]) for j in range(1, NS)]
-    copies = [pltpu.make_async_copy(q.at[:, pl.ds(e * BLK, BLK)], q_buf, sems.at[0])]
-    copies[0].start()
-
-    def fetch(from_ours, source, target):
-        sem = sems.at[len(copies)]
-        copy = pltpu.make_async_copy(source(ours), target, sem)
-        other = pltpu.make_async_copy(source(theirs), target, sem)
-        pl.when(from_ours)(copy.start)
-        pl.when(jnp.logical_not(from_ours))(other.start)
-        copies.append(copy)
-
+    return [block] + [block - jnp.where(slash[0, j] == 0, slash[0, 0], slash[0, j]) for j in range(1, NS)]
+
+
+def fetch(near, core, position, ours, theirs, k_all, v_all, sems):
     per = BLK // UNIT
+    copies = []
     for j in range(NS):
-        kept = jnp.where(near[j] >= 0, near[j], block)
+        kept = jnp.where(near[j] >= 0, near[j], near[0])
         chips = (position[0] >> 1) - (kept >> 2)
         to = pl.ds(j * per, per)
         for which, target in ((0, k_all.at[to]), (1, v_all.at[to, :, pl.ds(0, HD)])):
             unit = (2 * chips + which) * 2 * per + (kept & 1) * per
-            fetch(((kept >> 1) & 1) == core, lambda x: x.at[pl.ds(unit, per)], target)
-    v_all[:NEAR, :, HD:] = jnp.ones((NEAR, UNIT, HD), BF16)
-
+            copy = pltpu.make_async_copy(ours.at[pl.ds(unit, per)], target, sems.at[len(copies)])
+            other = pltpu.make_async_copy(theirs.at[pl.ds(unit, per)], target, sems.at[len(copies)])
+            from_ours = ((kept >> 1) & 1) == core
+            pl.when(from_ours)(copy.start)
+            pl.when(jnp.logical_not(from_ours))(other.start)
+            copies.append(copy)
+    return copies
+
+
+def fill(e, near, core, vertical, ours, theirs, k_all, v_all, copies):
+    per = BLK // UNIT
     row = lax.broadcasted_iota(jnp.int32, (UNIT, HD), 0)
     drop = jnp.zeros((UNIT, HD), jnp.int32)
     for j in range(NV):
         c = vertical[0, j]
-        bad = c > block
+        bad = c > near[0]
         for other in near:
             bad = bad | (c == other)
         drop = jnp.where(row // PIECE == j, bad.astype(jnp.int32), drop)
     drop = drop.astype(F32)
     keep = (1.0 - drop).astype(BF16)
-    drop = drop.astype(BF16)
     first = ours[e * per, 0:1, :]
-    instead = first * drop
+    instead = first * drop.astype(BF16)
     listed = ours.shape[0] - PIECES
     for c, (k, v) in enumerate(((ours, theirs), (theirs, ours))):
 
@@ -256,8 +252,6 @@
                 k_all[NEAR + i] = k[listed + i] * keep + instead
                 v_all[NEAR + i, :, :HD] = v[listed + i] * keep
 
-    for i in range(PIECES):
-        v_all[NEAR + i, :, HD:] = keep
     for copy in copies:
         copy.wait()
     for j in range(1, NS):
@@ -266,13 +260,26 @@
         def _(j=j):
             to = slice(j * per, (j + 1) * per)
             k_all[to] = jnp.broadcast_to(first, (per, UNIT, HD))
-            v_all[to] = jnp.zeros((per, UNIT, 2 * HD), BF16)
-
+            v_all[to, :, :HD] = jnp.zeros((per, UNIT, HD), BF16)
+
+    counts = [jnp.where(near[j // per] >= 0, jnp.ones((UNIT, HD), F32), 0.0).astype(BF16) for j in range(NEAR)]
+    return counts + [keep]
+
+
+def count(v_all, counts):
+    for j in range(NEAR):
+        v_all[j, :, HD:] = counts[j]
+    for i in range(NEAR, NEAR + PIECES):
+        v_all[i, :, HD:] = counts[NEAR]
+
+
+def heads(e, q_buf, o_buf, k_all, v_all, out, sems):
     factor = LOG2E / math.sqrt(HD)
     causal = lax.broadcasted_iota(jnp.int32, (BLK, BLK), 1) <= lax.broadcasted_iota(jnp.int32, (BLK, BLK), 0)
     keys = k_all[...].reshape((NV + NS) * BLK, HD)
     values = v_all[...].reshape((NV + NS) * BLK, 2 * HD)
     pair = 2
+    copies = []
 
     def score(h):
         n = min(pair, GROUP - h)
@@ -295,31 +302,82 @@
         later = score(h + pair) if h + pair < GROUP else None
         finish(h, *held)
         held = later
-    for copy in copies[2 * NS + 1 :]:
+    return copies
+
+
+def first_kernel(vertical, slash, position, q, ours, theirs, out, ours_next, theirs_next, token, q_buf, o_buf, k_all, v_all, k_next, v_next, sems, near_sems, next_sems):
+    token[...] = jnp.zeros_like(token)
+    core = position[0] & 1
+    copy = pltpu.make_async_copy(q.at[:, pl.ds(0, BLK)], q_buf, sems.at[0])
+    copy.start()
+    near = block_numbers(0, slash, position)
+    copies = fetch(near, core, position, ours, theirs, k_all, v_all, near_sems)
+    near_next = block_numbers(1, slash, position)
+    copies_next = fetch(near_next, core, position, ours, theirs, k_next, v_next, next_sems)
+    count(v_all, fill(0, near, core, vertical, ours, theirs, k_all, v_all, copies))
+    copy.wait()
+    written = heads(0, q_buf, o_buf, k_all, v_all, out, sems)
+    counts = fill(1, near_next, core, vertical, ours, theirs, k_next, v_next, copies_next)
+    n = NEAR + PIECES
+    ours_next[:n] = k_next[...]
+    theirs_next[:n] = v_next[...]
+    for j, x in enumerate(counts):
+        ours_next[n + j] = x
+    for copy in written:
         copy.wait()
 
 
-def attend(e, vertical, slash, position, q_t, ours, theirs, out=None):
-    local = q_t.shape[1]
-    args = (vertical, slash, position, q_t, ours, theirs) + ((out,) if e else ())
-    return pl.pallas_call(
-        functools.partial(attend_kernel, e),
-        out_shape=(shape(BF16, GROUP, local, HD), shape(F32, 8, 128)),
-        in_specs=[SMEM] * 3 + [ANY, VMEM, VMEM] + [ANY] * (len(args) - 6),
-        out_specs=(ANY, VMEM),
+def second_kernel(q, ours, theirs, before, out, q_buf, o_buf, v_all, sems):
+    n = NEAR + PIECES
+    copy = pltpu.make_async_copy(q.at[:, pl.ds(BLK, BLK)], q_buf, sems.at[0])
+    copy.start()
+    v_all[:, :, :HD] = theirs[:n]
+    count(v_all, [ours[n + j] for j in range(NEAR + 1)])
+    copy.wait()
+    for copy in heads(1, q_buf, o_buf, ours.at[pl.ds(0, n)], v_all, out, sems):
+        copy.wait()
+
+
+COST = pl.CostEstimate(flops=4 * GROUP * (NV + NS) * BLK**3, bytes_accessed=2 * 1024 * 1024, transcendentals=GROUP * (NV + NS) * BLK**2)
+KEYS = (NEAR + PIECES, UNIT, HD)
+VALUES = (NEAR + PIECES, UNIT, 2 * HD)
+TILE = (GROUP, BLK, HD)
+
+
+def attend_first(vertical, slash, position, q_t, ours, theirs):
+    return pl.pallas_call(
+        first_kernel,
+        out_shape=(shape(BF16, *q_t.shape), shape(BF16, *ours.shape), shape(BF16, *ours.shape), shape(F32, 8, 128)),
+        in_specs=[SMEM] * 3 + [HBM, VMEM, VMEM],
+        out_specs=(ANY, VMEM, VMEM, VMEM),
+        input_output_aliases={4: 1, 5: 2},
         scratch_shapes=[
-            pltpu.VMEM((GROUP, BLK, HD), BF16),
-            pltpu.VMEM((GROUP, BLK, HD), BF16),
-            pltpu.VMEM((NEAR + PIECES, UNIT, HD), BF16),
-            pltpu.VMEM((NEAR + PIECES, UNIT, 2 * HD), BF16),
-            pltpu.SemaphoreType.DMA((2 * NS + 1,)),
+            pltpu.VMEM(TILE, BF16),
+            pltpu.VMEM(TILE, BF16),
+            pltpu.VMEM(KEYS, BF16),
+            pltpu.VMEM(VALUES, BF16),
+            pltpu.VMEM(KEYS, BF16),
+            pltpu.VMEM(KEYS, BF16),
+            pltpu.SemaphoreType.DMA((GROUP,)),
+            pltpu.SemaphoreType.DMA((2 * NS,)),
+            pltpu.SemaphoreType.DMA((2 * NS,)),
         ],
-        input_output_aliases={len(args) - 1: 0} if e else {},
         compiler_params=MIDDLE,
-        cost_estimate=pl.CostEstimate(
-            flops=4 * GROUP * (NV + NS) * BLK**3, bytes_accessed=2 * 1024 * 1024, transcendentals=GROUP * (NV + NS) * BLK**2
-        ),
-    )(*args)
+        cost_estimate=COST,
+    )(vertical, slash, position, q_t, ours, theirs)
+
+
+def attend_second(q_t, ours, theirs, out):
+    return pl.pallas_call(
+        second_kernel,
+        out_shape=shape(BF16, *q_t.shape),
+        in_specs=[HBM, VMEM, VMEM, ANY],
+        out_specs=ANY,
+        scratch_shapes=[pltpu.VMEM(TILE, BF16), pltpu.VMEM(TILE, BF16), pltpu.VMEM(VALUES, BF16), pltpu.SemaphoreType.DMA((GROUP,))],
+        input_output_aliases={3: 0},
+        compiler_params=MIDDLE,
+        cost_estimate=COST,
+    )(q_t, ours, theirs, out)
 
 
 def on_device(queries, key_rows, value_rows, vertical, slash_offsets):
@@ -332,19 +390,18 @@
     sent, kv = pack(place, q_t, k, v)
     back = lambda x, chips: lax.ppermute(x, CHIP, [(i, (i + chips) % CHIPS) for i in range(CHIPS)])
     swap = lambda x: lax.ppermute(x, "core", [(0, 1), (1, 0)])
-    one, three = back(kv, 1), back(kv, 3)
+    three, four, k_theirs = back(kv, 3), back(kv, 4), swap(k)
     r = exchange(sent, CTX)
-    mine = exchange(pick(choose(vertical), r, one, three), ("y", "zlo"))
-    k_theirs, two, four = swap(k), back(three, -1), back(kv, 4)
+    mine = exchange(pick(choose(vertical), r, three, four, k_theirs), ("y", "zlo"))
+    one, two = back(kv, 1), back(three, -1)
     scores, stats = estimate(place, mine[:, LISTED:].reshape(QALL, HD), k, k_theirs, total_len)
-    ours = together([kv, one, two, three, four], mine, k_theirs)
+    ours = together([kv, one, two, three, four], mine, scores)
     theirs = swap(ours)
 
-    given = (vertical, slash_offsets, place, q_t, ours, theirs)
-    out, token = attend(0, *given)
+    out, ours, theirs, token = attend_first(vertical, slash_offsets, place, q_t, ours, theirs)
     stats = exchange(stats, CHIP)
     part = exchange(mass(stats, scores, token, lax.axis_size("kvh"), total_len / LAST / HEADS), ("core", "kvh"))
-    out, token = attend(1, *given, out)
+    out = attend_second(q_t, ours, theirs, out)
     profile = jnp.sum(part, axis=(0, 1))
     return jnp.transpose(out, (1, 0, 2)), profile
 

time: 109 us -> 107 us (0.982)
  waiting for transfers between devices: 30.2 us -> 22 us
  starting transfers between devices: 57.1 us -> 62.5 us
    ppermute x4, waiting for transfers between devices: 23.8 us -> 8.42 us  [on_device(): lax.ppermute(x, CHIP, [(i, (i + chips) % CHIPS) for i in range(CHIPS)])]
    all_to_all x4, waiting for transfers between devices: 5.51 us -> 13.6 us  [exchange(): return lax.all_to_all(x, axis, 0, 0)]
    ppermute x4, starting transfers between devices: 13.6 us -> 18 us  [on_device(): lax.ppermute(x, CHIP, [(i, (i + chips) % CHIPS) for i in range(CHIPS)])]
    all_to_all x4, starting transfers between devices: 36 us -> 37.7 us  [exchange(): return lax.all_to_all(x, axis, 0, 0)]
  transfers between devices with their start and end apart: 10 -> 10, of which waited for: 6 -> 5; matrix products, arithmetic and copies ran while one was open for 0% -> 0% of each run, Pallas kernels for 12% -> 13%
where the time goes in v6:
time: 107 us; the launch traced here: 106 us
  starting transfers between devices  62.5 us (58%)
  waiting for transfers between devices  22 us (21%)
  Pallas kernels  19.7 us (18%)
    all_to_all x4, starting transfers between devices, exchange(): return lax.all_to_all(x, axis, 0, 0)  37.7 us
    ppermute x4, starting transfers between devices, on_device(): lax.ppermute(x, CHIP, [(i, (i + chips) % CHIPS) for i in range(CHIPS)])  18 us
    all_to_all x4, waiting for transfers between devices, exchange(): return lax.all_to_all(x, axis, 0, 0)  13.6 us
    ppermute x4, waiting for transfers between devices, on_device(): lax.ppermute(x, CHIP, [(i, (i + chips) % CHIPS) for i in range(CHIPS)])  8.42 us
    pallas_call x1, Pallas kernels, attend_first(): pl.pallas_call(first_kernel, out_shape=(shape(BF16, *q_t.shape), shape(BF...  7.75 us
    ppermute x2, starting transfers between devices, on_device(): swap = lambda x: lax.ppermute(x, 'core', [(0, 1), (1, 0)])  6.84 us
    pallas_call x1, Pallas kernels, attend_second(): pl.pallas_call(second_kernel, out_shape=shape(BF16, *q_t.shape), in_specs...  4.88 us
    pallas_call x1, Pallas kernels, pack(): pl.pallas_call(pack_kernel, out_shape=(shape(BF16, 2 * CHIPS, 2 * PIECE,...  2.51 us
  transfers between devices with their start and end apart: 10, of which 5 were waited for; matrix products, arithmetic and copies ran while one was open for 0% of the time, Pallas kernels for 13%

profile of v6, /device:TPU:1, one launch (start us, length us, event | category | flops | bytes accessed | tf_op | source)
XLA Modules:
  0.0 106.4 jit_solution(16312332641822411245)
XLA Ops:
  0.6 2.5 %shard_map.68 = (bf16[64,16,128]{2,1,0:T(8,128)(2,1)}, bf16[4,128,128]{2,1,0:T(8,128)(2,1)}) custom-call(s32[1]{0:T(128)} %bitcast.1.position, bf16[5,256,128]{2,1,0:T(8,128)(2,1)} %bitcast.6, bf16[256,128]{1,0:T(8,128)(2,1)} %bitcast.10, bf16[256,128]{1,0:T(8,128)(2,1)} %bitcast.13), custom_call_target="tpu_custom_call" | custom-call | tf_op jit(solution)/shard_map/pallas_call | solution.py:85
  3.2 17.6 %all-to-all-start = ((bf16[64,16,128]{2,1,0:T(8,128)(2,1)}), bf16[64,16,128]{2,1,0:T(8,128)(2,1)S(1)}, u32[]{:S(2)}, u32[]{:S(2)}) async-start(bf16[64,16,128]{2,1,0:T(8,128)(2,1)} %get-tuple-element.11), calls=%async_computation | async-start | bytes 524288 | tf_op jit(solution)/shard_map/all_to_all | solution.py:52
  20.8 3.3 %collective-permute-start.3 = (bf16[4,128,128]{2,1,0:T(8,128)(2,1)}, bf16[4,128,128]{2,1,0:T(8,128)(2,1)S(1)}, u32[]{:S(2)}, u32[]{:S(2)}) collective-permute-start(bf16[4,128,128]{2,1,0:T(8,128)(2,1)} %get-tuple-element.10.refs_0_), channel_id=1, source_target_pairs={{0,64},{16,80},{32,96},{48,112},{64,128},{80,144},{96,160},{112,17... | collective-permute-start | bytes 393224 | tf_op jit(solution)/shard_map/ppermute | solution.py:391
  24.1 5.2 %collective-permute-start.1 = (bf16[4,128,128]{2,1,0:T(8,128)(2,1)}, bf16[4,128,128]{2,1,0:T(8,128)(2,1)S(1)}, u32[]{:S(2)}, u32[]{:S(2)}) collective-permute-start(bf16[4,128,128]{2,1,0:T(8,128)(2,1)} %get-tuple-element.10.refs_0_), channel_id=1, source_target_pairs={{0,48},{16,64},{32,80},{48,96},{64,112},{80,128},{96,144},{112,160... | collective-permute-start | bytes 393224 | tf_op jit(solution)/shard_map/ppermute | solution.py:391
  29.3 2.8 %collective-permute-start.4 = (bf16[256,128]{1,0:T(8,128)(2,1)}, bf16[256,128]{1,0:T(8,128)(2,1)S(1)}, u32[]{:S(2)}, u32[]{:S(2)}) collective-permute-start(bf16[256,128]{1,0:T(8,128)(2,1)} %bitcast.11), channel_id=1, source_target_pairs={{0,8},{8,0},{1,9},{9,1},{2,10},{10,2},{3,11},{11,3},{4,12},{12,4},... | collective-permute-start | bytes 196616 | tf_op jit(solution)/shard_map/ppermute | solution.py:392
  32.2 0.6 copy-done.3
  32.8 0.6 shard_map.69.chosen
  33.5 5.0 %collective-permute-done.1.three.refs_3_ = bf16[4,128,128]{2,1,0:T(8,128)(2,1)S(1)} collective-permute-done((bf16[4,128,128]{2,1,0:T(8,128)(2,1)}, bf16[4,128,128]{2,1,0:T(8,128)(2,1)S(1)}, u32[]{:S(2)}, u32[]{:S(2)}) %collective-permute-start.1) | collective-permute-done | bytes 131104 | tf_op jit(solution)/shard_map/ppermute | solution.py:391
  38.4 1.1 shard_map.70
  39.5 7.3 %all-to-all-start.1 = ((bf16[16,144,128]{2,1,0:T(8,128)(2,1)}), bf16[16,144,128]{2,1,0:T(8,128)(2,1)S(1)}, u32[]{:S(2)}, u32[]{:S(2)}) async-start(bf16[16,144,128]{2,1,0:T(8,128)(2,1)} %shard_map.70), calls=%async_computation.1 | async-start | bytes 1179648 | tf_op jit(solution)/shard_map/all_to_all | solution.py:52
  46.8 4.2 %collective-permute-start = (bf16[4,128,128]{2,1,0:T(8,128)(2,1)S(1)}, bf16[4,128,128]{2,1,0:T(8,128)(2,1)S(1)}, u32[]{:S(2)}, u32[]{:S(2)}) collective-permute-start(bf16[4,128,128]{2,1,0:T(8,128)(2,1)S(1)} %copy-done.2), channel_id=1, source_target_pairs={{0,16},{16,32},{32,48},{48,64},{64,80},{80,96},{96,112},{112,128},... | collective-permute-start | bytes 393224 | tf_op jit(solution)/shard_map/ppermute | solution.py:391
  51.0 5.3 %collective-permute-start.2 = (bf16[4,128,128]{2,1,0:T(8,128)(2,1)S(1)}, bf16[4,128,128]{2,1,0:T(8,128)(2,1)S(1)}, u32[]{:S(2)}, u32[]{:S(2)}) collective-permute-start(bf16[4,128,128]{2,1,0:T(8,128)(2,1)S(1)} %collective-permute-done.1.three.refs_3_), channel_id=1, source_target_pairs={{0,496},{16,0},{32,16},{48,32},{64,48},{80,64},{96,80},{112,96},{1... | collective-permute-start | bytes 393224 | tf_op jit(solution)/shard_map/ppermute | solution.py:391
  56.3 9.5 %all-to-all-done.1.refs_5_ = bf16[16,144,128]{2,1,0:T(8,128)(2,1)S(1)} async-done(((bf16[16,144,128]{2,1,0:T(8,128)(2,1)}), bf16[16,144,128]{2,1,0:T(8,128)(2,1)S(1)}, u32[]{:S(2)}, u32[]{:S(2)}) %all-to-all-start.1) | async-done | bytes 589856 | tf_op jit(solution)/shard_map/all_to_all | solution.py:52
  65.9 1.0 shard_map.71
  66.9 3.5 %collective-permute-done.2.refs_2_ = bf16[4,128,128]{2,1,0:T(8,128)(2,1)S(1)} collective-permute-done((bf16[4,128,128]{2,1,0:T(8,128)(2,1)S(1)}, bf16[4,128,128]{2,1,0:T(8,128)(2,1)S(1)}, u32[]{:S(2)}, u32[]{:S(2)}) %collective-permute-start.2) | collective-permute-done | bytes 131104 | tf_op jit(solution)/shard_map/ppermute | solution.py:391
  70.3 0.9 shard_map.72.ours
  71.3 4.0 %collective-permute-start.5 = (bf16[36,128,128]{2,1,0:T(8,128)(2,1)S(1)}, bf16[36,128,128]{2,1,0:T(8,128)(2,1)}, u32[]{:S(2)}, u32[]{:S(2)}) collective-permute-start(bf16[36,128,128]{2,1,0:T(8,128)(2,1)S(1)} %shard_map.72.ours), channel_id=1, source_target_pairs={{0,8},{8,0},{1,9},{9,1},{2,10},{10,2},{3,11},{11,3},{4,12},{12,4},... | collective-permute-start | bytes 3538952 | tf_op jit(solution)/shard_map/ppermute | solution.py:392
  75.3 7.1 %all-to-all-start.2 = ((f32[32,2,256]{2,1,0:T(2,128)}), f32[32,2,256]{2,1,0:T(2,128)S(1)}, u32[]{:S(2)}, u32[]{:S(2)}) async-start(f32[32,2,256]{2,1,0:T(2,128)} %get-tuple-element.16), calls=%async_computation.2 | async-start | bytes 131072 | tf_op jit(solution)/shard_map/all_to_all | solution.py:52
  82.5 7.8 %shard_map.73 = (bf16[5,256,128]{2,1,0:T(8,128)(2,1)}, bf16[36,128,128]{2,1,0:T(8,128)(2,1)S(1)}, bf16[36,128,128]{2,1,0:T(8,128)(2,1)}, f32[8,128]{1,0:T(8,128)S(1)}) custom-call(s32[1,16]{1,0:T(1,128)S(1)} %copy-done.4, s32[1,8]{1,0:T(1,128)S(1)} %copy-done.5, s32[1]{0:T(128)} %bitcast.1.position, ...), custom_call_target="tpu_custom_call", output_to_operand_aliasing={{1}: (4, {}), {2}: (5, {})} | custom-call | flops 1006632960 | bytes 2097152 | tf_op jit(solution)/shard_map/pallas_call | solution.py:348
  90.2 3.4 %all-to-all-done.2.stats = f32[32,2,256]{2,1,0:T(2,128)S(1)} async-done(((f32[32,2,256]{2,1,0:T(2,128)}), f32[32,2,256]{2,1,0:T(2,128)S(1)}, u32[]{:S(2)}, u32[]{:S(2)}) %all-to-all-start.2) | async-done | bytes 65568 | tf_op jit(solution)/shard_map/all_to_all | solution.py:52
  93.6 1.0 shard_map.75
  94.6 5.6 %all-to-all-start.3 = ((f32[16,1,256]{2,1,0:T(1,128)}), f32[16,1,256]{2,1,0:T(1,128)S(1)}, u32[]{:S(2)}, u32[]{:S(2)}) async-start(f32[16,1,256]{2,1,0:T(1,128)} %shard_map.75), calls=%async_computation.3 | async-start | bytes 32768 | tf_op jit(solution)/shard_map/all_to_all | solution.py:52
  100.3 4.9 %shard_map.74 = bf16[5,256,128]{2,1,0:T(8,128)(2,1)} custom-call(bf16[5,256,128]{2,1,0:T(8,128)(2,1)S(1)} %bitcast.8, bf16[36,128,128]{2,1,0:T(8,128)(2,1)S(1)} %get-tuple-element.13.ours, bf16[36,128,128]{2,1,0:T(8,128)(2,1)} %get-tuple-element.14.theirs, bf16[5,256,128]{2,1,0:T(8,128)(2,1)} %get-tuple-element.15.before), custom_call_target="tpu_custom_call", output_to_operand_aliasing={{}: (3, {})} | custom-call | flops 1006632960 | bytes 2097152 | tf_op jit(solution)/shard_map/pallas_call | solution.py:371
  105.1 0.6 all-to-all-done.3
  (18 shorter events, 0.6 us)
Async XLA Ops:
  3.2 35.3 %all-to-all-start = ((bf16[64,16,128]{2,1,0:T(8,128)(2,1)}), bf16[64,16,128]{2,1,0:T(8,128)(2,1)S(1)}, u32[]{:S(2)}, u32[]{:S(2)}) async-start(bf16[64,16,128]{2,1,0:T(8,128)(2,1)} %get-tuple-element.11), calls=%async_computation | async-start | bytes 524288 | tf_op jit(solution)/shard_map/all_to_all | solution.py:52
  20.8 12.7 %collective-permute-start.3 = (bf16[4,128,128]{2,1,0:T(8,128)(2,1)}, bf16[4,128,128]{2,1,0:T(8,128)(2,1)S(1)}, u32[]{:S(2)}, u32[]{:S(2)}) collective-permute-start(bf16[4,128,128]{2,1,0:T(8,128)(2,1)} %get-tuple-element.10.refs_0_), channel_id=1, source_target_pairs={{0,64},{16,80},{32,96},{48,112},{64,128},{80,144},{96,160},{112,17... | collective-permute-start | bytes 393224 | tf_op jit(solution)/shard_map/ppermute | solution.py:391
  24.1 14.3 %collective-permute-start.1 = (bf16[4,128,128]{2,1,0:T(8,128)(2,1)}, bf16[4,128,128]{2,1,0:T(8,128)(2,1)S(1)}, u32[]{:S(2)}, u32[]{:S(2)}) collective-permute-start(bf16[4,128,128]{2,1,0:T(8,128)(2,1)} %get-tuple-element.10.refs_0_), channel_id=1, source_target_pairs={{0,48},{16,64},{32,80},{48,96},{64,112},{80,128},{96,144},{112,160... | collective-permute-start | bytes 393224 | tf_op jit(solution)/shard_map/ppermute | solution.py:391
  29.3 4.1 %collective-permute-start.4 = (bf16[256,128]{1,0:T(8,128)(2,1)}, bf16[256,128]{1,0:T(8,128)(2,1)S(1)}, u32[]{:S(2)}, u32[]{:S(2)}) collective-permute-start(bf16[256,128]{1,0:T(8,128)(2,1)} %bitcast.11), channel_id=1, source_target_pairs={{0,8},{8,0},{1,9},{9,1},{2,10},{10,2},{3,11},{11,3},{4,12},{12,4},... | collective-permute-start | bytes 196616 | tf_op jit(solution)/shard_map/ppermute | solution.py:392
  32.2 0.7 copy-start.3
  33.4 13.4 %copy-start.2 = (bf16[4,128,128]{2,1,0:T(8,128)(2,1)S(1)}, bf16[4,128,128]{2,1,0:T(8,128)(2,1)}, u32[]{:S(2)}) copy-start(bf16[4,128,128]{2,1,0:T(8,128)(2,1)} %get-tuple-element.10.refs_0_) | copy-start | bytes 393220
  33.5 32.4 %copy-start.1 = (bf16[256,1,128]{2,0,1:T(8,128)(2,1)S(1)}, bf16[256,1,128]{2,0,1:T(8,128)(2,1)}, u32[]{:S(2)}) copy-start(bf16[256,1,128]{2,0,1:T(8,128)(2,1)} %param.6) | copy-start | bytes 196612
  39.5 26.3 %all-to-all-start.1 = ((bf16[16,144,128]{2,1,0:T(8,128)(2,1)}), bf16[16,144,128]{2,1,0:T(8,128)(2,1)S(1)}, u32[]{:S(2)}, u32[]{:S(2)}) async-start(bf16[16,144,128]{2,1,0:T(8,128)(2,1)} %shard_map.70), calls=%async_computation.1 | async-start | bytes 1179648 | tf_op jit(solution)/shard_map/all_to_all | solution.py:52
  46.8 20.1 %collective-permute-start = (bf16[4,128,128]{2,1,0:T(8,128)(2,1)S(1)}, bf16[4,128,128]{2,1,0:T(8,128)(2,1)S(1)}, u32[]{:S(2)}, u32[]{:S(2)}) collective-permute-start(bf16[4,128,128]{2,1,0:T(8,128)(2,1)S(1)} %copy-done.2), channel_id=1, source_target_pairs={{0,16},{16,32},{32,48},{48,64},{64,80},{80,96},{96,112},{112,128},... | collective-permute-start | bytes 393224 | tf_op jit(solution)/shard_map/ppermute | solution.py:391
  51.0 19.3 %collective-permute-start.2 = (bf16[4,128,128]{2,1,0:T(8,128)(2,1)S(1)}, bf16[4,128,128]{2,1,0:T(8,128)(2,1)S(1)}, u32[]{:S(2)}, u32[]{:S(2)}) collective-permute-start(bf16[4,128,128]{2,1,0:T(8,128)(2,1)S(1)} %collective-permute-done.1.three.refs_3_), channel_id=1, source_target_pairs={{0,496},{16,0},{32,16},{48,32},{64,48},{80,64},{96,80},{112,96},{1... | collective-permute-start | bytes 393224 | tf_op jit(solution)/shard_map/ppermute | solution.py:391
  70.3 12.1 %copy-start = (bf16[256,5,128]{2,0,1:T(8,128)(2,1)S(1)}, bf16[256,5,128]{2,0,1:T(8,128)(2,1)}, u32[]{:S(2)}) copy-start(bf16[256,5,128]{2,0,1:T(8,128)(2,1)} %param.5) | copy-start | bytes 983044
  70.3 12.1 %copy-start.4 = (s32[1,16]{1,0:T(1,128)S(1)}, s32[1,16]{1,0:T(1,128)}, u32[]{:S(2)}) copy-start(s32[1,16]{1,0:T(1,128)} %vertical.1) | copy-start | bytes 196
  70.3 12.1 %copy-start.5 = (s32[1,8]{1,0:T(1,128)S(1)}, s32[1,8]{1,0:T(1,128)}, u32[]{:S(2)}) copy-start(s32[1,8]{1,0:T(1,128)} %slash.1) | copy-start | bytes 100
  71.3 11.2 %collective-permute-start.5 = (bf16[36,128,128]{2,1,0:T(8,128)(2,1)S(1)}, bf16[36,128,128]{2,1,0:T(8,128)(2,1)}, u32[]{:S(2)}, u32[]{:S(2)}) collective-permute-start(bf16[36,128,128]{2,1,0:T(8,128)(2,1)S(1)} %shard_map.72.ours), channel_id=1, source_target_pairs={{0,8},{8,0},{1,9},{9,1},{2,10},{10,2},{3,11},{11,3},{4,12},{12,4},... | collective-permute-start | bytes 3538952 | tf_op jit(solution)/shard_map/ppermute | solution.py:392
  75.3 18.4 %all-to-all-start.2 = ((f32[32,2,256]{2,1,0:T(2,128)}), f32[32,2,256]{2,1,0:T(2,128)S(1)}, u32[]{:S(2)}, u32[]{:S(2)}) async-start(f32[32,2,256]{2,1,0:T(2,128)} %get-tuple-element.16), calls=%async_computation.2 | async-start | bytes 131072 | tf_op jit(solution)/shard_map/all_to_all | solution.py:52
  94.6 11.1 %all-to-all-start.3 = ((f32[16,1,256]{2,1,0:T(1,128)}), f32[16,1,256]{2,1,0:T(1,128)S(1)}, u32[]{:S(2)}, u32[]{:S(2)}) async-start(f32[16,1,256]{2,1,0:T(1,128)} %shard_map.75), calls=%async_computation.3 | async-start | bytes 32768 | tf_op jit(solution)/shard_map/all_to_all | solution.py:52

commit v7 on v6

--- a/solution.py
+++ b/solution.py
@@ -113,21 +113,21 @@
     )(vertical)
 
 
-def pick_kernel(chosen, r, three, four, k_theirs, out):
+def pick_kernel(chosen, r, three, k_theirs, out):
     rows = r[...].reshape(4 * CHIPS * PIECE, HD)
     tile = jnp.dot(chosen[...], rows, preferred_element_type=F32).astype(BF16)
     for d in range(PIECES):
         out[d] = tile
 
 
-def pick(chosen, r, three, four, k_theirs):
+def pick(chosen, r, three, k_theirs):
     return pl.pallas_call(
         pick_kernel,
         out_shape=shape(BF16, PIECES, LISTED + QROWS, HD),
-        in_specs=[VMEM, VMEM, ANY, ANY, ANY],
+        in_specs=[VMEM, VMEM, ANY, ANY],
         out_specs=VMEM,
         compiler_params=SMALL,
-    )(chosen, r, three, four, k_theirs)
+    )(chosen, r, three, k_theirs)
 
 
 def together_kernel(*refs):
@@ -390,10 +390,10 @@
     sent, kv = pack(place, q_t, k, v)
     back = lambda x, chips: lax.ppermute(x, CHIP, [(i, (i + chips) % CHIPS) for i in range(CHIPS)])
     swap = lambda x: lax.ppermute(x, "core", [(0, 1), (1, 0)])
-    three, four, k_theirs = back(kv, 3), back(kv, 4), swap(k)
+    three, k_theirs = back(kv, 3), swap(k)
     r = exchange(sent, CTX)
-    mine = exchange(pick(choose(vertical), r, three, four, k_theirs), ("y", "zlo"))
-    one, two = back(kv, 1), back(three, -1)
+    mine = exchange(pick(choose(vertical), r, three, k_theirs), ("y", "zlo"))
+    one, two, four = back(kv, 1), back(three, -1), back(kv, 4)
     scores, stats = estimate(place, mine[:, LISTED:].reshape(QALL, HD), k, k_theirs, total_len)
     ours = together([kv, one, two, three, four], mine, scores)
     theirs = swap(ours)

time: 107 us -> 106 us (level)
  starting transfers between devices: 62.5 us -> 61 us
    ppermute x4, waiting for transfers between devices: 8.42 us -> 12 us  [on_device(): lax.ppermute(x, CHIP, [(i, (i + chips) % CHIPS) for i in range(CHIPS)])]
    all_to_all x4, waiting for transfers between devices: 13.6 us -> 10.6 us  [exchange(): return lax.all_to_all(x, axis, 0, 0)]
    ppermute x2, starting transfers between devices: 6.84 us -> 5.32 us  [on_device(): swap = lambda x: lax.ppermute(x, 'core', [(0, 1), (1, 0)])]
  transfers between devices with their start and end apart: 10 -> 10, of which waited for: 5 -> 7; matrix products, arithmetic and copies ran while one was open for 0% -> 0% of each run, Pallas kernels for 13% -> 13%
where the time goes in v7:
time: 106 us; the launch traced here: 105 us
  starting transfers between devices  61 us (58%)
  waiting for transfers between devices  22.6 us (21%)
  Pallas kernels  19.7 us (19%)
    all_to_all x4, starting transfers between devices, exchange(): return lax.all_to_all(x, axis, 0, 0)  37.5 us
    ppermute x4, starting transfers between devices, on_device(): lax.ppermute(x, CHIP, [(i, (i + chips) % CHIPS) for i in range(CHIPS)])  18.2 us
    ppermute x4, waiting for transfers between devices, on_device(): lax.ppermute(x, CHIP, [(i, (i + chips) % CHIPS) for i in range(CHIPS)])  12 us
    all_to_all x4, waiting for transfers between devices, exchange(): return lax.all_to_all(x, axis, 0, 0)  10.6 us
    pallas_call x1, Pallas kernels, attend_first(): pl.pallas_call(first_kernel, out_shape=(shape(BF16, *q_t.shape), shape(BF...  7.74 us
    ppermute x2, starting transfers between devices, on_device(): swap = lambda x: lax.ppermute(x, 'core', [(0, 1), (1, 0)])  5.32 us
    pallas_call x1, Pallas kernels, attend_second(): pl.pallas_call(second_kernel, out_shape=shape(BF16, *q_t.shape), in_specs...  4.88 us
    pallas_call x1, Pallas kernels, pack(): pl.pallas_call(pack_kernel, out_shape=(shape(BF16, 2 * CHIPS, 2 * PIECE,...  2.51 us
  transfers between devices with their start and end apart: 10, of which 7 were waited for; matrix products, arithmetic and copies ran while one was open for 0% of the time, Pallas kernels for 13%

profile of v7, /device:TPU:1, one launch (start us, length us, event | category | flops | bytes accessed | tf_op | source)
XLA Modules:
  0.0 105.5 jit_solution(17872202757868740402)
XLA Ops:
  0.6 2.5 %shard_map.68 = (bf16[64,16,128]{2,1,0:T(8,128)(2,1)}, bf16[4,128,128]{2,1,0:T(8,128)(2,1)}) custom-call(s32[1]{0:T(128)} %bitcast.1.position, bf16[5,256,128]{2,1,0:T(8,128)(2,1)} %bitcast.6, bf16[256,128]{1,0:T(8,128)(2,1)} %bitcast.10, bf16[256,128]{1,0:T(8,128)(2,1)} %bitcast.13), custom_call_target="tpu_custom_call" | custom-call | tf_op jit(solution)/shard_map/pallas_call | solution.py:85
  3.2 17.6 %all-to-all-start = ((bf16[64,16,128]{2,1,0:T(8,128)(2,1)}), bf16[64,16,128]{2,1,0:T(8,128)(2,1)S(1)}, u32[]{:S(2)}, u32[]{:S(2)}) async-start(bf16[64,16,128]{2,1,0:T(8,128)(2,1)} %get-tuple-element.11), calls=%async_computation | async-start | bytes 524288 | tf_op jit(solution)/shard_map/all_to_all | solution.py:52
  20.8 5.4 %collective-permute-start.1 = (bf16[4,128,128]{2,1,0:T(8,128)(2,1)}, bf16[4,128,128]{2,1,0:T(8,128)(2,1)S(1)}, u32[]{:S(2)}, u32[]{:S(2)}) collective-permute-start(bf16[4,128,128]{2,1,0:T(8,128)(2,1)} %get-tuple-element.10.refs_0_), channel_id=1, source_target_pairs={{0,48},{16,64},{32,80},{48,96},{64,112},{80,128},{96,144},{112,160... | collective-permute-start | bytes 393224 | tf_op jit(solution)/shard_map/ppermute | solution.py:391
  26.2 2.6 %collective-permute-start.4 = (bf16[256,128]{1,0:T(8,128)(2,1)}, bf16[256,128]{1,0:T(8,128)(2,1)S(1)}, u32[]{:S(2)}, u32[]{:S(2)}) collective-permute-start(bf16[256,128]{1,0:T(8,128)(2,1)} %bitcast.11), channel_id=1, source_target_pairs={{0,8},{8,0},{1,9},{9,1},{2,10},{10,2},{3,11},{11,3},{4,12},{12,4},... | collective-permute-start | bytes 196616 | tf_op jit(solution)/shard_map/ppermute | solution.py:392
  28.8 0.6 copy-done.3
  30.1 5.6 %collective-permute-done.1.three.refs_3_ = bf16[4,128,128]{2,1,0:T(8,128)(2,1)S(1)} collective-permute-done((bf16[4,128,128]{2,1,0:T(8,128)(2,1)}, bf16[4,128,128]{2,1,0:T(8,128)(2,1)S(1)}, u32[]{:S(2)}, u32[]{:S(2)}) %collective-permute-start.1) | collective-permute-done | bytes 131104 | tf_op jit(solution)/shard_map/ppermute | solution.py:391
  35.7 0.7 all-to-all-done.r
  36.4 1.1 %shard_map.70 = bf16[16,144,128]{2,1,0:T(8,128)(2,1)} custom-call(bf16[144,1024]{1,0:T(8,128)(2,1)S(1)} %shard_map.69.chosen, bf16[64,16,128]{2,1,0:T(8,128)(2,1)S(1)} %all-to-all-done.r, bf16[4,128,128]{2,1,0:T(8,128)(2,1)S(1)} %collective-permute-done.1.three.refs_3_, bf16[256,128]{1,0:T(8,128)(2,1)S(1)} %collective-permute-done.4.k_theirs), custom_call_target="tpu_custom_call" | custom-call | tf_op jit(solution)/shard_map/pallas_call | solution.py:124
  37.4 7.2 %all-to-all-start.1 = ((bf16[16,144,128]{2,1,0:T(8,128)(2,1)}), bf16[16,144,128]{2,1,0:T(8,128)(2,1)S(1)}, u32[]{:S(2)}, u32[]{:S(2)}) async-start(bf16[16,144,128]{2,1,0:T(8,128)(2,1)} %shard_map.70), calls=%async_computation.1 | async-start | bytes 1179648 | tf_op jit(solution)/shard_map/all_to_all | solution.py:52
  44.7 3.3 %collective-permute-start.3 = (bf16[4,128,128]{2,1,0:T(8,128)(2,1)S(1)}, bf16[4,128,128]{2,1,0:T(8,128)(2,1)S(1)}, u32[]{:S(2)}, u32[]{:S(2)}) collective-permute-start(bf16[4,128,128]{2,1,0:T(8,128)(2,1)S(1)} %copy-done.2), channel_id=1, source_target_pairs={{0,64},{16,80},{32,96},{48,112},{64,128},{80,144},{96,160},{112,17... | collective-permute-start | bytes 393224 | tf_op jit(solution)/shard_map/ppermute | solution.py:391
  47.9 4.0 %collective-permute-start = (bf16[4,128,128]{2,1,0:T(8,128)(2,1)S(1)}, bf16[4,128,128]{2,1,0:T(8,128)(2,1)S(1)}, u32[]{:S(2)}, u32[]{:S(2)}) collective-permute-start(bf16[4,128,128]{2,1,0:T(8,128)(2,1)S(1)} %copy-done.2), channel_id=1, source_target_pairs={{0,16},{16,32},{32,48},{48,64},{64,80},{80,96},{96,112},{112,128},... | collective-permute-start | bytes 393224 | tf_op jit(solution)/shard_map/ppermute | solution.py:391
  51.9 5.5 %collective-permute-start.2 = (bf16[4,128,128]{2,1,0:T(8,128)(2,1)S(1)}, bf16[4,128,128]{2,1,0:T(8,128)(2,1)S(1)}, u32[]{:S(2)}, u32[]{:S(2)}) collective-permute-start(bf16[4,128,128]{2,1,0:T(8,128)(2,1)S(1)} %collective-permute-done.1.three.refs_3_), channel_id=1, source_target_pairs={{0,496},{16,0},{32,16},{48,32},{64,48},{80,64},{96,80},{112,96},{1... | collective-permute-start | bytes 393224 | tf_op jit(solution)/shard_map/ppermute | solution.py:391
  57.5 5.8 %all-to-all-done.1.refs_5_ = bf16[16,144,128]{2,1,0:T(8,128)(2,1)S(1)} async-done(((bf16[16,144,128]{2,1,0:T(8,128)(2,1)}), bf16[16,144,128]{2,1,0:T(8,128)(2,1)S(1)}, u32[]{:S(2)}, u32[]{:S(2)}) %all-to-all-start.1) | async-done | bytes 589856 | tf_op jit(solution)/shard_map/all_to_all | solution.py:52
  63.3 1.0 shard_map.71
  64.3 3.8 %collective-permute-done.refs_1_ = bf16[4,128,128]{2,1,0:T(8,128)(2,1)S(1)} collective-permute-done((bf16[4,128,128]{2,1,0:T(8,128)(2,1)S(1)}, bf16[4,128,128]{2,1,0:T(8,128)(2,1)S(1)}, u32[]{:S(2)}, u32[]{:S(2)}) %collective-permute-start) | collective-permute-done | bytes 131104 | tf_op jit(solution)/shard_map/ppermute | solution.py:391
  68.1 2.6 %collective-permute-done.2.refs_2_ = bf16[4,128,128]{2,1,0:T(8,128)(2,1)S(1)} collective-permute-done((bf16[4,128,128]{2,1,0:T(8,128)(2,1)S(1)}, bf16[4,128,128]{2,1,0:T(8,128)(2,1)S(1)}, u32[]{:S(2)}, u32[]{:S(2)}) %collective-permute-start.2) | collective-permute-done | bytes 131104 | tf_op jit(solution)/shard_map/ppermute | solution.py:391
  70.7 0.9 shard_map.72.ours
  71.7 2.8 %collective-permute-start.5 = (bf16[36,128,128]{2,1,0:T(8,128)(2,1)S(1)}, bf16[36,128,128]{2,1,0:T(8,128)(2,1)}, u32[]{:S(2)}, u32[]{:S(2)}) collective-permute-start(bf16[36,128,128]{2,1,0:T(8,128)(2,1)S(1)} %shard_map.72.ours), channel_id=1, source_target_pairs={{0,8},{8,0},{1,9},{9,1},{2,10},{10,2},{3,11},{11,3},{4,12},{12,4},... | collective-permute-start | bytes 3538952 | tf_op jit(solution)/shard_map/ppermute | solution.py:392
  74.5 7.0 %all-to-all-start.2 = ((f32[32,2,256]{2,1,0:T(2,128)}), f32[32,2,256]{2,1,0:T(2,128)S(1)}, u32[]{:S(2)}, u32[]{:S(2)}) async-start(f32[32,2,256]{2,1,0:T(2,128)} %get-tuple-element.16), calls=%async_computation.2 | async-start | bytes 131072 | tf_op jit(solution)/shard_map/all_to_all | solution.py:52
  81.5 7.7 %shard_map.73 = (bf16[5,256,128]{2,1,0:T(8,128)(2,1)}, bf16[36,128,128]{2,1,0:T(8,128)(2,1)S(1)}, bf16[36,128,128]{2,1,0:T(8,128)(2,1)}, f32[8,128]{1,0:T(8,128)S(1)}) custom-call(s32[1,16]{1,0:T(1,128)S(1)} %copy-done.4, s32[1,8]{1,0:T(1,128)S(1)} %copy-done.5, s32[1]{0:T(128)} %bitcast.1.position, ...), custom_call_target="tpu_custom_call", output_to_operand_aliasing={{1}: (4, {}), {2}: (5, {})} | custom-call | flops 1006632960 | bytes 2097152 | tf_op jit(solution)/shard_map/pallas_call | solution.py:348
  89.2 3.5 %all-to-all-done.2.stats = f32[32,2,256]{2,1,0:T(2,128)S(1)} async-done(((f32[32,2,256]{2,1,0:T(2,128)}), f32[32,2,256]{2,1,0:T(2,128)S(1)}, u32[]{:S(2)}, u32[]{:S(2)}) %all-to-all-start.2) | async-done | bytes 65568 | tf_op jit(solution)/shard_map/all_to_all | solution.py:52
  92.7 1.0 shard_map.75
  93.7 5.7 %all-to-all-start.3 = ((f32[16,1,256]{2,1,0:T(1,128)}), f32[16,1,256]{2,1,0:T(1,128)S(1)}, u32[]{:S(2)}, u32[]{:S(2)}) async-start(f32[16,1,256]{2,1,0:T(1,128)} %shard_map.75), calls=%async_computation.3 | async-start | bytes 32768 | tf_op jit(solution)/shard_map/all_to_all | solution.py:52
  99.4 4.9 %shard_map.74 = bf16[5,256,128]{2,1,0:T(8,128)(2,1)} custom-call(bf16[5,256,128]{2,1,0:T(8,128)(2,1)S(1)} %bitcast.8, bf16[36,128,128]{2,1,0:T(8,128)(2,1)S(1)} %get-tuple-element.13.ours, bf16[36,128,128]{2,1,0:T(8,128)(2,1)} %get-tuple-element.14.theirs, bf16[5,256,128]{2,1,0:T(8,128)(2,1)} %get-tuple-element.15.before), custom_call_target="tpu_custom_call", output_to_operand_aliasing={{}: (3, {})} | custom-call | flops 1006632960 | bytes 2097152 | tf_op jit(solution)/shard_map/pallas_call | solution.py:371
  (18 shorter events, 1.9 us)
Async XLA Ops:
  3.2 33.2 %all-to-all-start = ((bf16[64,16,128]{2,1,0:T(8,128)(2,1)}), bf16[64,16,128]{2,1,0:T(8,128)(2,1)S(1)}, u32[]{:S(2)}, u32[]{:S(2)}) async-start(bf16[64,16,128]{2,1,0:T(8,128)(2,1)} %get-tuple-element.11), calls=%async_computation | async-start | bytes 524288 | tf_op jit(solution)/shard_map/all_to_all | solution.py:52
  20.8 14.9 %collective-permute-start.1 = (bf16[4,128,128]{2,1,0:T(8,128)(2,1)}, bf16[4,128,128]{2,1,0:T(8,128)(2,1)S(1)}, u32[]{:S(2)}, u32[]{:S(2)}) collective-permute-start(bf16[4,128,128]{2,1,0:T(8,128)(2,1)} %get-tuple-element.10.refs_0_), channel_id=1, source_target_pairs={{0,48},{16,64},{32,80},{48,96},{64,112},{80,128},{96,144},{112,160... | collective-permute-start | bytes 393224 | tf_op jit(solution)/shard_map/ppermute | solution.py:391
  26.2 3.9 %collective-permute-start.4 = (bf16[256,128]{1,0:T(8,128)(2,1)}, bf16[256,128]{1,0:T(8,128)(2,1)S(1)}, u32[]{:S(2)}, u32[]{:S(2)}) collective-permute-start(bf16[256,128]{1,0:T(8,128)(2,1)} %bitcast.11), channel_id=1, source_target_pairs={{0,8},{8,0},{1,9},{9,1},{2,10},{10,2},{3,11},{11,3},{4,12},{12,4},... | collective-permute-start | bytes 196616 | tf_op jit(solution)/shard_map/ppermute | solution.py:392
  28.8 0.7 copy-start.3
  30.1 14.6 %copy-start.2 = (bf16[4,128,128]{2,1,0:T(8,128)(2,1)S(1)}, bf16[4,128,128]{2,1,0:T(8,128)(2,1)}, u32[]{:S(2)}) copy-start(bf16[4,128,128]{2,1,0:T(8,128)(2,1)} %get-tuple-element.10.refs_0_) | copy-start | bytes 393220
  30.1 33.2 %copy-start.1 = (bf16[256,1,128]{2,0,1:T(8,128)(2,1)S(1)}, bf16[256,1,128]{2,0,1:T(8,128)(2,1)}, u32[]{:S(2)}) copy-start(bf16[256,1,128]{2,0,1:T(8,128)(2,1)} %param.6) | copy-start | bytes 196612
  37.4 25.9 %all-to-all-start.1 = ((bf16[16,144,128]{2,1,0:T(8,128)(2,1)}), bf16[16,144,128]{2,1,0:T(8,128)(2,1)S(1)}, u32[]{:S(2)}, u32[]{:S(2)}) async-start(bf16[16,144,128]{2,1,0:T(8,128)(2,1)} %shard_map.70), calls=%async_computation.1 | async-start | bytes 1179648 | tf_op jit(solution)/shard_map/all_to_all | solution.py:52
  44.7 19.7 %collective-permute-start.3 = (bf16[4,128,128]{2,1,0:T(8,128)(2,1)S(1)}, bf16[4,128,128]{2,1,0:T(8,128)(2,1)S(1)}, u32[]{:S(2)}, u32[]{:S(2)}) collective-permute-start(bf16[4,128,128]{2,1,0:T(8,128)(2,1)S(1)} %copy-done.2), channel_id=1, source_target_pairs={{0,64},{16,80},{32,96},{48,112},{64,128},{80,144},{96,160},{112,17... | collective-permute-start | bytes 393224 | tf_op jit(solution)/shard_map/ppermute | solution.py:391
  47.9 20.1 %collective-permute-start = (bf16[4,128,128]{2,1,0:T(8,128)(2,1)S(1)}, bf16[4,128,128]{2,1,0:T(8,128)(2,1)S(1)}, u32[]{:S(2)}, u32[]{:S(2)}) collective-permute-start(bf16[4,128,128]{2,1,0:T(8,128)(2,1)S(1)} %copy-done.2), channel_id=1, source_target_pairs={{0,16},{16,32},{32,48},{48,64},{64,80},{80,96},{96,112},{112,128},... | collective-permute-start | bytes 393224 | tf_op jit(solution)/shard_map/ppermute | solution.py:391
  51.9 18.8 %collective-permute-start.2 = (bf16[4,128,128]{2,1,0:T(8,128)(2,1)S(1)}, bf16[4,128,128]{2,1,0:T(8,128)(2,1)S(1)}, u32[]{:S(2)}, u32[]{:S(2)}) collective-permute-start(bf16[4,128,128]{2,1,0:T(8,128)(2,1)S(1)} %collective-permute-done.1.three.refs_3_), channel_id=1, source_target_pairs={{0,496},{16,0},{32,16},{48,32},{64,48},{80,64},{96,80},{112,96},{1... | collective-permute-start | bytes 393224 | tf_op jit(solution)/shard_map/ppermute | solution.py:391
  70.7 10.7 %copy-start = (bf16[256,5,128]{2,0,1:T(8,128)(2,1)S(1)}, bf16[256,5,128]{2,0,1:T(8,128)(2,1)}, u32[]{:S(2)}) copy-start(bf16[256,5,128]{2,0,1:T(8,128)(2,1)} %param.5) | copy-start | bytes 983044
  70.7 10.7 %copy-start.4 = (s32[1,16]{1,0:T(1,128)S(1)}, s32[1,16]{1,0:T(1,128)}, u32[]{:S(2)}) copy-start(s32[1,16]{1,0:T(1,128)} %vertical.1) | copy-start | bytes 196
  70.7 10.7 %copy-start.5 = (s32[1,8]{1,0:T(1,128)S(1)}, s32[1,8]{1,0:T(1,128)}, u32[]{:S(2)}) copy-start(s32[1,8]{1,0:T(1,128)} %slash.1) | copy-start | bytes 100
  71.7 9.8 %collective-permute-start.5 = (bf16[36,128,128]{2,1,0:T(8,128)(2,1)S(1)}, bf16[36,128,128]{2,1,0:T(8,128)(2,1)}, u32[]{:S(2)}, u32[]{:S(2)}) collective-permute-start(bf16[36,128,128]{2,1,0:T(8,128)(2,1)S(1)} %shard_map.72.ours), channel_id=1, source_target_pairs={{0,8},{8,0},{1,9},{9,1},{2,10},{10,2},{3,11},{11,3},{4,12},{12,4},... | collective-permute-start | bytes 3538952 | tf_op jit(solution)/shard_map/ppermute | solution.py:392
  74.5 18.2 %all-to-all-start.2 = ((f32[32,2,256]{2,1,0:T(2,128)}), f32[32,2,256]{2,1,0:T(2,128)S(1)}, u32[]{:S(2)}, u32[]{:S(2)}) async-start(f32[32,2,256]{2,1,0:T(2,128)} %get-tuple-element.16), calls=%async_computation.2 | async-start | bytes 131072 | tf_op jit(solution)/shard_map/all_to_all | solution.py:52
  93.7 11.2 %all-to-all-start.3 = ((f32[16,1,256]{2,1,0:T(1,128)}), f32[16,1,256]{2,1,0:T(1,128)S(1)}, u32[]{:S(2)}, u32[]{:S(2)}) async-start(f32[16,1,256]{2,1,0:T(1,128)} %shard_map.75), calls=%async_computation.3 | async-start | bytes 32768 | tf_op jit(solution)/shard_map/all_to_all | solution.py:52

commit v8 on v7

--- a/solution.py
+++ b/solution.py
@@ -52,10 +52,11 @@
     return lax.all_to_all(x, axis, 0, 0)
 
 
-def pack_kernel(position, q, k, v, sent, kv, last, sem):
+def pack_kernel(position, q, k, v, sent, kv, k_buf, v_buf, last, sems):
     local = k.shape[0]
-    copy = pltpu.make_async_copy(q.at[:, pl.ds(local - LAST, LAST)], last, sem)
-    copy.start()
+    loads = [pltpu.make_async_copy(x, y, sems.at[i]) for i, (x, y) in enumerate(((k, k_buf), (v, v_buf), (q.at[:, pl.ds(local - LAST, LAST)], last)))]
+    for copy in loads:
+        copy.start()
 
     def spread(pieces):
         for y in range(NY):
@@ -65,12 +66,13 @@
                         sent[((y * NZ // 2 + zhi) * 2 + zlo) * 2 + c] = pieces[c][2 * y + zlo]
 
     cut = []
-    for which, x in enumerate((k, v)):
+    for which, x in enumerate((k_buf, v_buf)):
+        loads[which].wait()
         kv[which * local // UNIT : (which + 1) * local // UNIT] = x[...].reshape(local // UNIT, UNIT, HD)
         x = x[...].astype(F32).reshape(2, PIECES, PIECE, HD)
         cut.append(jnp.concatenate([x[0], x[1]], axis=1).astype(BF16))
     spread(cut)
-    copy.wait()
+    loads[2].wait()
 
     @pl.when(position[0] == 2 * CHIPS - 1)
     def _():
@@ -85,9 +87,14 @@
     return pl.pallas_call(
         pack_kernel,
         out_shape=(shape(BF16, 2 * CHIPS, 2 * PIECE, HD), shape(BF16, 2 * local // UNIT, UNIT, HD)),
-        in_specs=[SMEM, ANY, VMEM, VMEM],
+        in_specs=[SMEM, ANY, ANY, ANY],
         out_specs=(VMEM, VMEM),
-        scratch_shapes=[pltpu.VMEM((GROUP, LAST, HD), BF16), pltpu.SemaphoreType.DMA],
+        scratch_shapes=[
+            pltpu.VMEM(k.shape, BF16),
+            pltpu.VMEM(v.shape, BF16),
+            pltpu.VMEM((GROUP, LAST, HD), BF16),
+            pltpu.SemaphoreType.DMA((3,)),
+        ],
         compiler_params=LARGE,
     )(position, q_t, k, v)
 
@@ -320,10 +327,11 @@
     counts = fill(1, near_next, core, vertical, ours, theirs, k_next, v_next, copies_next)
     n = NEAR + PIECES
     ours_next[:n] = k_next[...]
-    theirs_next[:n] = v_next[...]
+    copy = pltpu.make_async_copy(v_next, theirs_next.at[pl.ds(0, n)], sems.at[GROUP])
+    copy.start()
     for j, x in enumerate(counts):
         ours_next[n + j] = x
-    for copy in written:
+    for copy in written + [copy]:
         copy.wait()
 
 
@@ -331,9 +339,11 @@
     n = NEAR + PIECES
     copy = pltpu.make_async_copy(q.at[:, pl.ds(BLK, BLK)], q_buf, sems.at[0])
     copy.start()
-    v_all[:, :, :HD] = theirs[:n]
+    values = pltpu.make_async_copy(theirs.at[pl.ds(0, n)], v_all.at[:, :, pl.ds(0, HD)], sems.at[1])
+    values.start()
     count(v_all, [ours[n + j] for j in range(NEAR + 1)])
     copy.wait()
+    values.wait()
     for copy in heads(1, q_buf, o_buf, ours.at[pl.ds(0, n)], v_all, out, sems):
         copy.wait()
 
@@ -349,7 +359,7 @@
         first_kernel,
         out_shape=(shape(BF16, *q_t.shape), shape(BF16, *ours.shape), shape(BF16, *ours.shape), shape(F32, 8, 128)),
         in_specs=[SMEM] * 3 + [HBM, VMEM, VMEM],
-        out_specs=(ANY, VMEM, VMEM, VMEM),
+        out_specs=(ANY, VMEM, ANY, VMEM),
         input_output_aliases={4: 1, 5: 2},
         scratch_shapes=[
             pltpu.VMEM(TILE, BF16),
@@ -358,7 +368,7 @@
             pltpu.VMEM(VALUES, BF16),
             pltpu.VMEM(KEYS, BF16),
             pltpu.VMEM(KEYS, BF16),
-            pltpu.SemaphoreType.DMA((GROUP,)),
+            pltpu.SemaphoreType.DMA((GROUP + 1,)),
             pltpu.SemaphoreType.DMA((2 * NS,)),
             pltpu.SemaphoreType.DMA((2 * NS,)),
         ],
@@ -371,7 +381,7 @@
     return pl.pallas_call(
         second_kernel,
         out_shape=shape(BF16, *q_t.shape),
-        in_specs=[HBM, VMEM, VMEM, ANY],
+        in_specs=[HBM, VMEM, ANY, ANY],
         out_specs=ANY,
         scratch_shapes=[pltpu.VMEM(TILE, BF16), pltpu.VMEM(TILE, BF16), pltpu.VMEM(VALUES, BF16), pltpu.SemaphoreType.DMA((GROUP,))],
         input_output_aliases={3: 0},

time: 106 us -> 105 us (level)
  Pallas kernels: 19.7 us -> 17.9 us
where the time goes in v8:
time: 105 us
  starting transfers between devices  61 us (58%)
  waiting for transfers between devices  23.6 us (22%)
  Pallas kernels  17.9 us (17%)
    all_to_all x4, starting transfers between devices, exchange(): return lax.all_to_all(x, axis, 0, 0)  37.5 us
    ppermute x4, starting transfers between devices, on_device(): lax.ppermute(x, CHIP, [(i, (i + chips) % CHIPS) for i in range(CHIPS)])  18.2 us
    ppermute x4, waiting for transfers between devices, on_device(): lax.ppermute(x, CHIP, [(i, (i + chips) % CHIPS) for i in range(CHIPS)])  12 us
    all_to_all x4, waiting for transfers between devices, exchange(): return lax.all_to_all(x, axis, 0, 0)  11.6 us
    pallas_call x1, Pallas kernels, attend_first(): pl.pallas_call(first_kernel, out_shape=(shape(BF16, *q_t.shape), shape(BF...  7.18 us
    ppermute x2, starting transfers between devices, on_device(): swap = lambda x: lax.ppermute(x, 'core', [(0, 1), (1, 0)])  5.32 us
    pallas_call x1, Pallas kernels, attend_second(): pl.pallas_call(second_kernel, out_shape=shape(BF16, *q_t.shape), in_specs...  4.45 us
  transfers between devices with their start and end apart: 10, of which 7 were waited for; matrix products, arithmetic and copies ran while one was open for 0% of the time, Pallas kernels for 13%

profile of v8, /device:TPU:1, one launch (start us, length us, event | category | flops | bytes accessed | tf_op | source)
XLA Modules:
  0.0 104.7 jit_solution(12643593627860856056)
XLA Ops:
  0.6 1.7 %shard_map.68 = (bf16[64,16,128]{2,1,0:T(8,128)(2,1)}, bf16[4,128,128]{2,1,0:T(8,128)(2,1)}) custom-call(s32[1]{0:T(128)} %bitcast.1.position, bf16[5,256,128]{2,1,0:T(8,128)(2,1)} %bitcast.6, bf16[256,128]{1,0:T(8,128)(2,1)} %bitcast.10, bf16[256,128]{1,0:T(8,128)(2,1)} %bitcast.13), custom_call_target="tpu_custom_call" | custom-call | tf_op jit(solution)/shard_map/pallas_call | solution.py:87
  2.4 17.6 %all-to-all-start = ((bf16[64,16,128]{2,1,0:T(8,128)(2,1)}), bf16[64,16,128]{2,1,0:T(8,128)(2,1)S(1)}, u32[]{:S(2)}, u32[]{:S(2)}) async-start(bf16[64,16,128]{2,1,0:T(8,128)(2,1)} %get-tuple-element.11), calls=%async_computation | async-start | bytes 524288 | tf_op jit(solution)/shard_map/all_to_all | solution.py:52
  20.0 5.4 %collective-permute-start.1 = (bf16[4,128,128]{2,1,0:T(8,128)(2,1)}, bf16[4,128,128]{2,1,0:T(8,128)(2,1)S(1)}, u32[]{:S(2)}, u32[]{:S(2)}) collective-permute-start(bf16[4,128,128]{2,1,0:T(8,128)(2,1)} %get-tuple-element.10.refs_0_), channel_id=1, source_target_pairs={{0,48},{16,64},{32,80},{48,96},{64,112},{80,128},{96,144},{112,160... | collective-permute-start | bytes 393224 | tf_op jit(solution)/shard_map/ppermute | solution.py:401
  25.4 2.6 %collective-permute-start.4 = (bf16[256,128]{1,0:T(8,128)(2,1)}, bf16[256,128]{1,0:T(8,128)(2,1)S(1)}, u32[]{:S(2)}, u32[]{:S(2)}) collective-permute-start(bf16[256,128]{1,0:T(8,128)(2,1)} %bitcast.11), channel_id=1, source_target_pairs={{0,8},{8,0},{1,9},{9,1},{2,10},{10,2},{3,11},{11,3},{4,12},{12,4},... | collective-permute-start | bytes 196616 | tf_op jit(solution)/shard_map/ppermute | solution.py:402
  29.3 5.6 %collective-permute-done.1.three.refs_3_ = bf16[4,128,128]{2,1,0:T(8,128)(2,1)S(1)} collective-permute-done((bf16[4,128,128]{2,1,0:T(8,128)(2,1)}, bf16[4,128,128]{2,1,0:T(8,128)(2,1)S(1)}, u32[]{:S(2)}, u32[]{:S(2)}) %collective-permute-start.1) | collective-permute-done | bytes 131104 | tf_op jit(solution)/shard_map/ppermute | solution.py:401
  34.9 0.7 all-to-all-done.r
  35.6 1.1 %shard_map.70 = bf16[16,144,128]{2,1,0:T(8,128)(2,1)} custom-call(bf16[144,1024]{1,0:T(8,128)(2,1)S(1)} %shard_map.69.chosen, bf16[64,16,128]{2,1,0:T(8,128)(2,1)S(1)} %all-to-all-done.r, bf16[4,128,128]{2,1,0:T(8,128)(2,1)S(1)} %collective-permute-done.1.three.refs_3_, bf16[256,128]{1,0:T(8,128)(2,1)S(1)} %collective-permute-done.4.k_theirs), custom_call_target="tpu_custom_call" | custom-call | tf_op jit(solution)/shard_map/pallas_call | solution.py:131
  36.7 7.2 %all-to-all-start.1 = ((bf16[16,144,128]{2,1,0:T(8,128)(2,1)}), bf16[16,144,128]{2,1,0:T(8,128)(2,1)S(1)}, u32[]{:S(2)}, u32[]{:S(2)}) async-start(bf16[16,144,128]{2,1,0:T(8,128)(2,1)} %shard_map.70), calls=%async_computation.1 | async-start | bytes 1179648 | tf_op jit(solution)/shard_map/all_to_all | solution.py:52
  43.9 3.3 %collective-permute-start.3 = (bf16[4,128,128]{2,1,0:T(8,128)(2,1)S(1)}, bf16[4,128,128]{2,1,0:T(8,128)(2,1)S(1)}, u32[]{:S(2)}, u32[]{:S(2)}) collective-permute-start(bf16[4,128,128]{2,1,0:T(8,128)(2,1)S(1)} %copy-done.2), channel_id=1, source_target_pairs={{0,64},{16,80},{32,96},{48,112},{64,128},{80,144},{96,160},{112,17... | collective-permute-start | bytes 393224 | tf_op jit(solution)/shard_map/ppermute | solution.py:401
  47.2 4.0 %collective-permute-start = (bf16[4,128,128]{2,1,0:T(8,128)(2,1)S(1)}, bf16[4,128,128]{2,1,0:T(8,128)(2,1)S(1)}, u32[]{:S(2)}, u32[]{:S(2)}) collective-permute-start(bf16[4,128,128]{2,1,0:T(8,128)(2,1)S(1)} %copy-done.2), channel_id=1, source_target_pairs={{0,16},{16,32},{32,48},{48,64},{64,80},{80,96},{96,112},{112,128},... | collective-permute-start | bytes 393224 | tf_op jit(solution)/shard_map/ppermute | solution.py:401
  51.2 5.5 %collective-permute-start.2 = (bf16[4,128,128]{2,1,0:T(8,128)(2,1)S(1)}, bf16[4,128,128]{2,1,0:T(8,128)(2,1)S(1)}, u32[]{:S(2)}, u32[]{:S(2)}) collective-permute-start(bf16[4,128,128]{2,1,0:T(8,128)(2,1)S(1)} %collective-permute-done.1.three.refs_3_), channel_id=1, source_target_pairs={{0,496},{16,0},{32,16},{48,32},{64,48},{80,64},{96,80},{112,96},{1... | collective-permute-start | bytes 393224 | tf_op jit(solution)/shard_map/ppermute | solution.py:401
  56.7 5.8 %all-to-all-done.1.refs_5_ = bf16[16,144,128]{2,1,0:T(8,128)(2,1)S(1)} async-done(((bf16[16,144,128]{2,1,0:T(8,128)(2,1)}), bf16[16,144,128]{2,1,0:T(8,128)(2,1)S(1)}, u32[]{:S(2)}, u32[]{:S(2)}) %all-to-all-start.1) | async-done | bytes 589856 | tf_op jit(solution)/shard_map/all_to_all | solution.py:52
  62.5 1.0 shard_map.71
  63.5 3.8 %collective-permute-done.refs_1_ = bf16[4,128,128]{2,1,0:T(8,128)(2,1)S(1)} collective-permute-done((bf16[4,128,128]{2,1,0:T(8,128)(2,1)S(1)}, bf16[4,128,128]{2,1,0:T(8,128)(2,1)S(1)}, u32[]{:S(2)}, u32[]{:S(2)}) %collective-permute-start) | collective-permute-done | bytes 131104 | tf_op jit(solution)/shard_map/ppermute | solution.py:401
  67.3 2.6 %collective-permute-done.2.refs_2_ = bf16[4,128,128]{2,1,0:T(8,128)(2,1)S(1)} collective-permute-done((bf16[4,128,128]{2,1,0:T(8,128)(2,1)S(1)}, bf16[4,128,128]{2,1,0:T(8,128)(2,1)S(1)}, u32[]{:S(2)}, u32[]{:S(2)}) %collective-permute-start.2) | collective-permute-done | bytes 131104 | tf_op jit(solution)/shard_map/ppermute | solution.py:401
  70.0 0.9 shard_map.72.ours
  70.9 2.8 %collective-permute-start.5 = (bf16[36,128,128]{2,1,0:T(8,128)(2,1)S(1)}, bf16[36,128,128]{2,1,0:T(8,128)(2,1)}, u32[]{:S(2)}, u32[]{:S(2)}) collective-permute-start(bf16[36,128,128]{2,1,0:T(8,128)(2,1)S(1)} %shard_map.72.ours), channel_id=1, source_target_pairs={{0,8},{8,0},{1,9},{9,1},{2,10},{10,2},{3,11},{11,3},{4,12},{12,4},... | collective-permute-start | bytes 3538952 | tf_op jit(solution)/shard_map/ppermute | solution.py:402
  73.7 7.0 %all-to-all-start.2 = ((f32[32,2,256]{2,1,0:T(2,128)}), f32[32,2,256]{2,1,0:T(2,128)S(1)}, u32[]{:S(2)}, u32[]{:S(2)}) async-start(f32[32,2,256]{2,1,0:T(2,128)} %get-tuple-element.16), calls=%async_computation.2 | async-start | bytes 131072 | tf_op jit(solution)/shard_map/all_to_all | solution.py:52
  80.7 7.2 %shard_map.73 = (bf16[5,256,128]{2,1,0:T(8,128)(2,1)}, bf16[36,128,128]{2,1,0:T(8,128)(2,1)S(1)}, bf16[36,128,128]{2,1,0:T(8,128)(2,1)}, f32[8,128]{1,0:T(8,128)S(1)}) custom-call(s32[1,16]{1,0:T(1,128)S(1)} %copy-done.4, s32[1,8]{1,0:T(1,128)S(1)} %copy-done.5, s32[1]{0:T(128)} %bitcast.1.position, ...), custom_call_target="tpu_custom_call", output_to_operand_aliasing={{1}: (4, {}), {2}: (5, {})} | custom-call | flops 1006632960 | bytes 2097152 | tf_op jit(solution)/shard_map/pallas_call | solution.py:358
  87.9 4.0 %all-to-all-done.2.stats = f32[32,2,256]{2,1,0:T(2,128)S(1)} async-done(((f32[32,2,256]{2,1,0:T(2,128)}), f32[32,2,256]{2,1,0:T(2,128)S(1)}, u32[]{:S(2)}, u32[]{:S(2)}) %all-to-all-start.2) | async-done | bytes 65568 | tf_op jit(solution)/shard_map/all_to_all | solution.py:52
  91.9 1.0 shard_map.75
  92.9 5.7 %all-to-all-start.3 = ((f32[16,1,256]{2,1,0:T(1,128)}), f32[16,1,256]{2,1,0:T(1,128)S(1)}, u32[]{:S(2)}, u32[]{:S(2)}) async-start(f32[16,1,256]{2,1,0:T(1,128)} %shard_map.75), calls=%async_computation.3 | async-start | bytes 32768 | tf_op jit(solution)/shard_map/all_to_all | solution.py:52
  98.6 4.5 %shard_map.74 = bf16[5,256,128]{2,1,0:T(8,128)(2,1)} custom-call(bf16[5,256,128]{2,1,0:T(8,128)(2,1)S(1)} %bitcast.8, bf16[36,128,128]{2,1,0:T(8,128)(2,1)S(1)} %get-tuple-element.13.ours, bf16[36,128,128]{2,1,0:T(8,128)(2,1)} %get-tuple-element.14.theirs, bf16[5,256,128]{2,1,0:T(8,128)(2,1)} %get-tuple-element.15.before), custom_call_target="tpu_custom_call", output_to_operand_aliasing={{}: (3, {})} | custom-call | flops 1006632960 | bytes 2097152 | tf_op jit(solution)/shard_map/pallas_call | solution.py:381
  103.1 1.0 all-to-all-done.3
  (18 shorter events, 1.9 us)
Async XLA Ops:
  2.4 33.2 %all-to-all-start = ((bf16[64,16,128]{2,1,0:T(8,128)(2,1)}), bf16[64,16,128]{2,1,0:T(8,128)(2,1)S(1)}, u32[]{:S(2)}, u32[]{:S(2)}) async-start(bf16[64,16,128]{2,1,0:T(8,128)(2,1)} %get-tuple-element.11), calls=%async_computation | async-start | bytes 524288 | tf_op jit(solution)/shard_map/all_to_all | solution.py:52
  20.0 14.9 %collective-permute-start.1 = (bf16[4,128,128]{2,1,0:T(8,128)(2,1)}, bf16[4,128,128]{2,1,0:T(8,128)(2,1)S(1)}, u32[]{:S(2)}, u32[]{:S(2)}) collective-permute-start(bf16[4,128,128]{2,1,0:T(8,128)(2,1)} %get-tuple-element.10.refs_0_), channel_id=1, source_target_pairs={{0,48},{16,64},{32,80},{48,96},{64,112},{80,128},{96,144},{112,160... | collective-permute-start | bytes 393224 | tf_op jit(solution)/shard_map/ppermute | solution.py:401
  25.4 3.9 %collective-permute-start.4 = (bf16[256,128]{1,0:T(8,128)(2,1)}, bf16[256,128]{1,0:T(8,128)(2,1)S(1)}, u32[]{:S(2)}, u32[]{:S(2)}) collective-permute-start(bf16[256,128]{1,0:T(8,128)(2,1)} %bitcast.11), channel_id=1, source_target_pairs={{0,8},{8,0},{1,9},{9,1},{2,10},{10,2},{3,11},{11,3},{4,12},{12,4},... | collective-permute-start | bytes 196616 | tf_op jit(solution)/shard_map/ppermute | solution.py:402
  28.0 0.7 copy-start.3
  29.3 14.6 %copy-start.2 = (bf16[4,128,128]{2,1,0:T(8,128)(2,1)S(1)}, bf16[4,128,128]{2,1,0:T(8,128)(2,1)}, u32[]{:S(2)}) copy-start(bf16[4,128,128]{2,1,0:T(8,128)(2,1)} %get-tuple-element.10.refs_0_) | copy-start | bytes 393220
  29.3 33.2 %copy-start.1 = (bf16[256,1,128]{2,0,1:T(8,128)(2,1)S(1)}, bf16[256,1,128]{2,0,1:T(8,128)(2,1)}, u32[]{:S(2)}) copy-start(bf16[256,1,128]{2,0,1:T(8,128)(2,1)} %param.6) | copy-start | bytes 196612
  36.7 25.9 %all-to-all-start.1 = ((bf16[16,144,128]{2,1,0:T(8,128)(2,1)}), bf16[16,144,128]{2,1,0:T(8,128)(2,1)S(1)}, u32[]{:S(2)}, u32[]{:S(2)}) async-start(bf16[16,144,128]{2,1,0:T(8,128)(2,1)} %shard_map.70), calls=%async_computation.1 | async-start | bytes 1179648 | tf_op jit(solution)/shard_map/all_to_all | solution.py:52
  43.9 19.7 %collective-permute-start.3 = (bf16[4,128,128]{2,1,0:T(8,128)(2,1)S(1)}, bf16[4,128,128]{2,1,0:T(8,128)(2,1)S(1)}, u32[]{:S(2)}, u32[]{:S(2)}) collective-permute-start(bf16[4,128,128]{2,1,0:T(8,128)(2,1)S(1)} %copy-done.2), channel_id=1, source_target_pairs={{0,64},{16,80},{32,96},{48,112},{64,128},{80,144},{96,160},{112,17... | collective-permute-start | bytes 393224 | tf_op jit(solution)/shard_map/ppermute | solution.py:401
  47.2 20.1 %collective-permute-start = (bf16[4,128,128]{2,1,0:T(8,128)(2,1)S(1)}, bf16[4,128,128]{2,1,0:T(8,128)(2,1)S(1)}, u32[]{:S(2)}, u32[]{:S(2)}) collective-permute-start(bf16[4,128,128]{2,1,0:T(8,128)(2,1)S(1)} %copy-done.2), channel_id=1, source_target_pairs={{0,16},{16,32},{32,48},{48,64},{64,80},{80,96},{96,112},{112,128},... | collective-permute-start | bytes 393224 | tf_op jit(solution)/shard_map/ppermute | solution.py:401
  51.2 18.8 %collective-permute-start.2 = (bf16[4,128,128]{2,1,0:T(8,128)(2,1)S(1)}, bf16[4,128,128]{2,1,0:T(8,128)(2,1)S(1)}, u32[]{:S(2)}, u32[]{:S(2)}) collective-permute-start(bf16[4,128,128]{2,1,0:T(8,128)(2,1)S(1)} %collective-permute-done.1.three.refs_3_), channel_id=1, source_target_pairs={{0,496},{16,0},{32,16},{48,32},{64,48},{80,64},{96,80},{112,96},{1... | collective-permute-start | bytes 393224 | tf_op jit(solution)/shard_map/ppermute | solution.py:401
  69.9 10.7 %copy-start = (bf16[256,5,128]{2,0,1:T(8,128)(2,1)S(1)}, bf16[256,5,128]{2,0,1:T(8,128)(2,1)}, u32[]{:S(2)}) copy-start(bf16[256,5,128]{2,0,1:T(8,128)(2,1)} %param.5) | copy-start | bytes 983044
  69.9 10.7 %copy-start.4 = (s32[1,16]{1,0:T(1,128)S(1)}, s32[1,16]{1,0:T(1,128)}, u32[]{:S(2)}) copy-start(s32[1,16]{1,0:T(1,128)} %vertical.1) | copy-start | bytes 196
  69.9 10.7 %copy-start.5 = (s32[1,8]{1,0:T(1,128)S(1)}, s32[1,8]{1,0:T(1,128)}, u32[]{:S(2)}) copy-start(s32[1,8]{1,0:T(1,128)} %slash.1) | copy-start | bytes 100
  70.9 9.8 %collective-permute-start.5 = (bf16[36,128,128]{2,1,0:T(8,128)(2,1)S(1)}, bf16[36,128,128]{2,1,0:T(8,128)(2,1)}, u32[]{:S(2)}, u32[]{:S(2)}) collective-permute-start(bf16[36,128,128]{2,1,0:T(8,128)(2,1)S(1)} %shard_map.72.ours), channel_id=1, source_target_pairs={{0,8},{8,0},{1,9},{9,1},{2,10},{10,2},{3,11},{11,3},{4,12},{12,4},... | collective-permute-start | bytes 3538952 | tf_op jit(solution)/shard_map/ppermute | solution.py:402
  73.7 18.2 %all-to-all-start.2 = ((f32[32,2,256]{2,1,0:T(2,128)}), f32[32,2,256]{2,1,0:T(2,128)S(1)}, u32[]{:S(2)}, u32[]{:S(2)}) async-start(f32[32,2,256]{2,1,0:T(2,128)} %get-tuple-element.16), calls=%async_computation.2 | async-start | bytes 131072 | tf_op jit(solution)/shard_map/all_to_all | solution.py:52
  92.9 11.2 %all-to-all-start.3 = ((f32[16,1,256]{2,1,0:T(1,128)}), f32[16,1,256]{2,1,0:T(1,128)S(1)}, u32[]{:S(2)}, u32[]{:S(2)}) async-start(f32[16,1,256]{2,1,0:T(1,128)} %shard_map.75), calls=%async_computation.3 | async-start | bytes 32768 | tf_op jit(solution)/shard_map/all_to_all | solution.py:52

commit v9 on v8

--- a/solution.py
+++ b/solution.py
@@ -138,27 +138,25 @@
 
 
 def together_kernel(*refs):
-    *parts, mine, after, out, sems = refs
-    n = len(parts)
+    *parts, after, out, sems = refs
     each = parts[0].shape[0]
     copies = [pltpu.make_async_copy(part, out.at[pl.ds(each * i, each)], sems.at[i]) for i, part in enumerate(parts)]
-    copies.append(pltpu.make_async_copy(mine.at[:, pl.ds(0, LISTED)], out.at[pl.ds(each * n, PIECES)], sems.at[n]))
     for copy in copies:
         copy.start()
     for copy in copies:
         copy.wait()
 
 
-def together(parts, mine, after):
+def together(parts, after):
     n = len(parts)
     return pl.pallas_call(
         together_kernel,
-        out_shape=shape(BF16, n * parts[0].shape[0] + PIECES, UNIT, HD),
-        in_specs=[ANY] * (n + 2),
+        out_shape=shape(BF16, n * parts[0].shape[0], UNIT, HD),
+        in_specs=[ANY] * (n + 1),
         out_specs=ANY,
         scratch_shapes=[pltpu.SemaphoreType.DMA((n + 1,))],
         compiler_params=SMALL,
-    )(*parts, mine, after)
+    )(*parts, after)
 
 
 def estimate_kernel(total_len, position, q, k_mine, k_theirs, scores, stats):
@@ -236,7 +234,7 @@
     return copies
 
 
-def fill(e, near, core, vertical, ours, theirs, k_all, v_all, copies):
+def fill(e, near, core, vertical, mine, theirs, own, k_all, v_all, copies):
     per = BLK // UNIT
     row = lax.broadcasted_iota(jnp.int32, (UNIT, HD), 0)
     drop = jnp.zeros((UNIT, HD), jnp.int32)
@@ -248,16 +246,15 @@
         drop = jnp.where(row // PIECE == j, bad.astype(jnp.int32), drop)
     drop = drop.astype(F32)
     keep = (1.0 - drop).astype(BF16)
-    first = ours[e * per, 0:1, :]
+    first = own[e * per, 0:1, :]
     instead = first * drop.astype(BF16)
-    listed = ours.shape[0] - PIECES
-    for c, (k, v) in enumerate(((ours, theirs), (theirs, ours))):
+    for c, (k, v) in enumerate(((mine, theirs), (theirs, mine))):
 
         @pl.when(core == c)
         def _(k=k, v=v):
             for i in range(PIECES):
-                k_all[NEAR + i] = k[listed + i] * keep + instead
-                v_all[NEAR + i, :, :HD] = v[listed + i] * keep
+                k_all[NEAR + i] = k[i, :LISTED, :] * keep + instead
+                v_all[NEAR + i, :, :HD] = v[i, :LISTED, :] * keep
 
     for copy in copies:
         copy.wait()
@@ -312,82 +309,102 @@
     return copies
 
 
-def first_kernel(vertical, slash, position, q, ours, theirs, out, ours_next, theirs_next, token, q_buf, o_buf, k_all, v_all, k_next, v_next, sems, near_sems, next_sems):
+def handed_on(k, v, u, mine, theirs, near_mine, near_theirs):
+    near, far, rows = pl.ds(0, NEAR), pl.ds(NEAR, PIECES), pl.ds(0, LISTED)
+    left = pl.ds(0, HD)
+    return (
+        (k.at[near], near_mine.at[near]),
+        (k.at[far], mine.at[:, rows]),
+        (v.at[near, :, left], near_theirs.at[near]),
+        (v.at[far, :, left], theirs.at[:, rows]),
+        (u, near_mine.at[pl.ds(NEAR, NEAR + 1)]),
+    )
+
+
+def first_kernel(vertical, slash, position, q, mine, theirs, near_mine, near_theirs, *rest):
+    out, *places, token, q_buf, o_buf, k_all, v_all, k_next, v_next, u_next, sems, near_sems, next_sems = rest
     token[...] = jnp.zeros_like(token)
     core = position[0] & 1
     copy = pltpu.make_async_copy(q.at[:, pl.ds(0, BLK)], q_buf, sems.at[0])
     copy.start()
     near = block_numbers(0, slash, position)
-    copies = fetch(near, core, position, ours, theirs, k_all, v_all, near_sems)
+    copies = fetch(near, core, position, near_mine, near_theirs, k_all, v_all, near_sems)
     near_next = block_numbers(1, slash, position)
-    copies_next = fetch(near_next, core, position, ours, theirs, k_next, v_next, next_sems)
-    count(v_all, fill(0, near, core, vertical, ours, theirs, k_all, v_all, copies))
+    copies_next = fetch(near_next, core, position, near_mine, near_theirs, k_next, v_next, next_sems)
+    count(v_all, fill(0, near, core, vertical, mine, theirs, near_mine, k_all, v_all, copies))
     copy.wait()
     written = heads(0, q_buf, o_buf, k_all, v_all, out, sems)
-    counts = fill(1, near_next, core, vertical, ours, theirs, k_next, v_next, copies_next)
-    n = NEAR + PIECES
-    ours_next[:n] = k_next[...]
-    copy = pltpu.make_async_copy(v_next, theirs_next.at[pl.ds(0, n)], sems.at[GROUP])
-    copy.start()
-    for j, x in enumerate(counts):
-        ours_next[n + j] = x
-    for copy in written + [copy]:
+    for j, x in enumerate(fill(1, near_next, core, vertical, mine, theirs, near_mine, k_next, v_next, copies_next)):
+        u_next[j] = x
+    for i, (source, target) in enumerate(handed_on(k_next, v_next, u_next, *places)):
+        written.append(pltpu.make_async_copy(source, target, sems.at[GROUP + i]))
+        written[-1].start()
+    for copy in written:
         copy.wait()
 
 
-def second_kernel(q, ours, theirs, before, out, q_buf, o_buf, v_all, sems):
-    n = NEAR + PIECES
-    copy = pltpu.make_async_copy(q.at[:, pl.ds(BLK, BLK)], q_buf, sems.at[0])
-    copy.start()
-    values = pltpu.make_async_copy(theirs.at[pl.ds(0, n)], v_all.at[:, :, pl.ds(0, HD)], sems.at[1])
-    values.start()
-    count(v_all, [ours[n + j] for j in range(NEAR + 1)])
-    copy.wait()
-    values.wait()
-    for copy in heads(1, q_buf, o_buf, ours.at[pl.ds(0, n)], v_all, out, sems):
+def second_kernel(q, mine, theirs, near_mine, near_theirs, before, out, q_buf, o_buf, k_all, v_all, u, sems):
+    copies = [pltpu.make_async_copy(q.at[:, pl.ds(BLK, BLK)], q_buf, sems.at[0])]
+    for i, (target, source) in enumerate(handed_on(k_all, v_all, u, mine, theirs, near_mine, near_theirs)):
+        copies.append(pltpu.make_async_copy(source, target, sems.at[GROUP + i]))
+    for copy in copies:
+        copy.start()
+    for copy in copies:
+        copy.wait()
+    count(v_all, [u[j] for j in range(NEAR + 1)])
+    for copy in heads(1, q_buf, o_buf, k_all, v_all, out, sems):
         copy.wait()
 
 
 COST = pl.CostEstimate(flops=4 * GROUP * (NV + NS) * BLK**3, bytes_accessed=2 * 1024 * 1024, transcendentals=GROUP * (NV + NS) * BLK**2)
 KEYS = (NEAR + PIECES, UNIT, HD)
 VALUES = (NEAR + PIECES, UNIT, 2 * HD)
+COUNTS = (NEAR + 1, UNIT, HD)
 TILE = (GROUP, BLK, HD)
 
 
-def attend_first(vertical, slash, position, q_t, ours, theirs):
+def attend_first(vertical, slash, position, q_t, *given):
     return pl.pallas_call(
         first_kernel,
-        out_shape=(shape(BF16, *q_t.shape), shape(BF16, *ours.shape), shape(BF16, *ours.shape), shape(F32, 8, 128)),
-        in_specs=[SMEM] * 3 + [HBM, VMEM, VMEM],
-        out_specs=(ANY, VMEM, ANY, VMEM),
-        input_output_aliases={4: 1, 5: 2},
+        out_shape=(shape(BF16, *q_t.shape), *(shape(BF16, *x.shape) for x in given), shape(F32, 8, 128)),
+        in_specs=[SMEM] * 3 + [HBM] + [VMEM] * 4,
+        out_specs=(ANY, ANY, ANY, ANY, ANY, VMEM),
+        input_output_aliases={4 + i: 1 + i for i in range(4)},
         scratch_shapes=[
             pltpu.VMEM(TILE, BF16),
             pltpu.VMEM(TILE, BF16),
             pltpu.VMEM(KEYS, BF16),
             pltpu.VMEM(VALUES, BF16),
             pltpu.VMEM(KEYS, BF16),
-            pltpu.VMEM(KEYS, BF16),
-            pltpu.SemaphoreType.DMA((GROUP + 1,)),
+            pltpu.VMEM(VALUES, BF16),
+            pltpu.VMEM(COUNTS, BF16),
+            pltpu.SemaphoreType.DMA((GROUP + 5,)),
             pltpu.SemaphoreType.DMA((2 * NS,)),
             pltpu.SemaphoreType.DMA((2 * NS,)),
         ],
         compiler_params=MIDDLE,
         cost_estimate=COST,
-    )(vertical, slash, position, q_t, ours, theirs)
-
-
-def attend_second(q_t, ours, theirs, out):
+    )(vertical, slash, position, q_t, *given)
+
+
+def attend_second(q_t, *given):
     return pl.pallas_call(
         second_kernel,
         out_shape=shape(BF16, *q_t.shape),
-        in_specs=[HBM, VMEM, ANY, ANY],
+        in_specs=[HBM] + [ANY] * 5,
         out_specs=ANY,
-        scratch_shapes=[pltpu.VMEM(TILE, BF16), pltpu.VMEM(TILE, BF16), pltpu.VMEM(VALUES, BF16), pltpu.SemaphoreType.DMA((GROUP,))],
-        input_output_aliases={3: 0},
+        scratch_shapes=[
+            pltpu.VMEM(TILE, BF16),
+            pltpu.VMEM(TILE, BF16),
+            pltpu.VMEM(KEYS, BF16),
+            pltpu.VMEM(VALUES, BF16),
+            pltpu.VMEM(COUNTS, BF16),
+            pltpu.SemaphoreType.DMA((GROUP + 5,)),
+        ],
+        input_output_aliases={5: 0},
         compiler_params=MIDDLE,
         cost_estimate=COST,
-    )(q_t, ours, theirs, out)
+    )(q_t, *given)
 
 
 def on_device(queries, key_rows, value_rows, vertical, slash_offsets):
@@ -405,13 +422,14 @@
     mine = exchange(pick(choose(vertical), r, three, k_theirs), ("y", "zlo"))
     one, two, four = back(kv, 1), back(three, -1), back(kv, 4)
     scores, stats = estimate(place, mine[:, LISTED:].reshape(QALL, HD), k, k_theirs, total_len)
-    ours = together([kv, one, two, three, four], mine, scores)
-    theirs = swap(ours)
-
-    out, ours, theirs, token = attend_first(vertical, slash_offsets, place, q_t, ours, theirs)
+    theirs = swap(mine)
+    near_mine = together([kv, one, two, three, four], scores)
+    near_theirs = swap(near_mine)
+
+    out, *handed, token = attend_first(vertical, slash_offsets, place, q_t, mine, theirs, near_mine, near_theirs)
     stats = exchange(stats, CHIP)
     part = exchange(mass(stats, scores, token, lax.axis_size("kvh"), total_len / LAST / HEADS), ("core", "kvh"))
-    out = attend_second(q_t, ours, theirs, out)
+    out = attend_second(q_t, *handed, out)
     profile = jnp.sum(part, axis=(0, 1))
     return jnp.transpose(out, (1, 0, 2)), profile
 

time: 105 us -> 108 us (1.029)
  starting transfers between devices: 61 us -> 63.4 us
    ppermute x2 -> x3, starting transfers between devices: 5.32 us -> 7.23 us  [on_device(): swap = lambda x: lax.ppermute(x, 'core', [(0, 1), (1, 0)])]
  transfers between devices with their start and end apart: 10 -> 11, of which waited for: 7 -> 8; matrix products, arithmetic and copies ran while one was open for 0% -> 0% of each run, Pallas kernels for 13% -> 12%
where the time goes in v9:
time: 108 us; the launch traced here: 107 us
  starting transfers between devices  63.4 us (59%)
  waiting for transfers between devices  24.4 us (23%)
  Pallas kernels  17.7 us (16%)
    all_to_all x4, starting transfers between devices, exchange(): return lax.all_to_all(x, axis, 0, 0)  38 us
    ppermute x4, starting transfers between devices, on_device(): lax.ppermute(x, CHIP, [(i, (i + chips) % CHIPS) for i in range(CHIPS)])  18.2 us
    ppermute x4, waiting for transfers between devices, on_device(): lax.ppermute(x, CHIP, [(i, (i + chips) % CHIPS) for i in range(CHIPS)])  12.5 us
    all_to_all x4, waiting for transfers between devices, exchange(): return lax.all_to_all(x, axis, 0, 0)  11.7 us
    ppermute x3, starting transfers between devices, on_device(): swap = lambda x: lax.ppermute(x, 'core', [(0, 1), (1, 0)])  7.23 us
    pallas_call x1, Pallas kernels, attend_first(): pl.pallas_call(first_kernel, out_shape=(shape(BF16, *q_t.shape), *(shape(...  6.79 us
    pallas_call x1, Pallas kernels, attend_second(): pl.pallas_call(second_kernel, out_shape=shape(BF16, *q_t.shape), in_specs...  4.62 us
  transfers between devices with their start and end apart: 11, of which 8 were waited for; matrix products, arithmetic and copies ran while one was open for 0% of the time, Pallas kernels for 12%

profile of v9, /device:TPU:1, one launch (start us, length us, event | category | flops | bytes accessed | tf_op | source)
XLA Modules:
  0.0 107.0 jit_solution(626172553708454537)
XLA Ops:
  0.6 1.7 %shard_map.69 = (bf16[64,16,128]{2,1,0:T(8,128)(2,1)}, bf16[4,128,128]{2,1,0:T(8,128)(2,1)}) custom-call(s32[1]{0:T(128)} %bitcast.1.position, bf16[5,256,128]{2,1,0:T(8,128)(2,1)} %bitcast.6, bf16[256,128]{1,0:T(8,128)(2,1)} %bitcast.10, bf16[256,128]{1,0:T(8,128)(2,1)} %bitcast.13), custom_call_target="tpu_custom_call" | custom-call | tf_op jit(solution)/shard_map/pallas_call | solution.py:87
  2.4 17.8 %all-to-all-start = ((bf16[64,16,128]{2,1,0:T(8,128)(2,1)}), bf16[64,16,128]{2,1,0:T(8,128)(2,1)S(1)}, u32[]{:S(2)}, u32[]{:S(2)}) async-start(bf16[64,16,128]{2,1,0:T(8,128)(2,1)} %get-tuple-element.12), calls=%async_computation | async-start | bytes 524288 | tf_op jit(solution)/shard_map/all_to_all | solution.py:52
  20.2 5.4 %collective-permute-start = (bf16[4,128,128]{2,1,0:T(8,128)(2,1)S(1)}, bf16[4,128,128]{2,1,0:T(8,128)(2,1)S(1)}, u32[]{:S(2)}, u32[]{:S(2)}) collective-permute-start(bf16[4,128,128]{2,1,0:T(8,128)(2,1)S(1)} %copy-done.2), channel_id=1, source_target_pairs={{0,48},{16,64},{32,80},{48,96},{64,112},{80,128},{96,144},{112,160... | collective-permute-start | bytes 393224 | tf_op jit(solution)/shard_map/ppermute | solution.py:418
  25.6 2.5 %collective-permute-start.1 = (bf16[256,128]{1,0:T(8,128)(2,1)S(1)}, bf16[256,128]{1,0:T(8,128)(2,1)S(1)}, u32[]{:S(2)}, u32[]{:S(2)}) collective-permute-start(bf16[256,128]{1,0:T(8,128)(2,1)S(1)} %bitcast.11), channel_id=1, source_target_pairs={{0,8},{8,0},{1,9},{9,1},{2,10},{10,2},{3,11},{11,3},{4,12},{12,4},... | collective-permute-start | bytes 196616 | tf_op jit(solution)/shard_map/ppermute | solution.py:419
  29.1 6.0 %collective-permute-done.three.refs_3_ = bf16[4,128,128]{2,1,0:T(8,128)(2,1)S(1)} collective-permute-done((bf16[4,128,128]{2,1,0:T(8,128)(2,1)S(1)}, bf16[4,128,128]{2,1,0:T(8,128)(2,1)S(1)}, u32[]{:S(2)}, u32[]{:S(2)}) %collective-permute-start) | collective-permute-done | bytes 131104 | tf_op jit(solution)/shard_map/ppermute | solution.py:418
  35.7 1.1 shard_map.70
  36.8 7.2 %all-to-all-start.1 = ((bf16[16,144,128]{2,1,0:T(8,128)(2,1)}), bf16[16,144,128]{2,1,0:T(8,128)(2,1)S(1)}, u32[]{:S(2)}, u32[]{:S(2)}) async-start(bf16[16,144,128]{2,1,0:T(8,128)(2,1)} %shard_map.70), calls=%async_computation.1 | async-start | bytes 1179648 | tf_op jit(solution)/shard_map/all_to_all | solution.py:52
  44.0 3.3 %collective-permute-start.5 = (bf16[4,128,128]{2,1,0:T(8,128)(2,1)S(1)}, bf16[4,128,128]{2,1,0:T(8,128)(2,1)S(1)}, u32[]{:S(2)}, u32[]{:S(2)}) collective-permute-start(bf16[4,128,128]{2,1,0:T(8,128)(2,1)S(1)} %copy-done.2), channel_id=1, source_target_pairs={{0,64},{16,80},{32,96},{48,112},{64,128},{80,144},{96,160},{112,17... | collective-permute-start | bytes 393224 | tf_op jit(solution)/shard_map/ppermute | solution.py:418
  47.3 4.0 %collective-permute-start.3 = (bf16[4,128,128]{2,1,0:T(8,128)(2,1)S(1)}, bf16[4,128,128]{2,1,0:T(8,128)(2,1)S(1)}, u32[]{:S(2)}, u32[]{:S(2)}) collective-permute-start(bf16[4,128,128]{2,1,0:T(8,128)(2,1)S(1)} %copy-done.2), channel_id=1, source_target_pairs={{0,16},{16,32},{32,48},{48,64},{64,80},{80,96},{96,112},{112,128},... | collective-permute-start | bytes 393224 | tf_op jit(solution)/shard_map/ppermute | solution.py:418
  51.3 5.5 %collective-permute-start.4 = (bf16[4,128,128]{2,1,0:T(8,128)(2,1)S(1)}, bf16[4,128,128]{2,1,0:T(8,128)(2,1)S(1)}, u32[]{:S(2)}, u32[]{:S(2)}) collective-permute-start(bf16[4,128,128]{2,1,0:T(8,128)(2,1)S(1)} %collective-permute-done.three.refs_3_), channel_id=1, source_target_pairs={{0,496},{16,0},{32,16},{48,32},{64,48},{80,64},{96,80},{112,96},{1... | collective-permute-start | bytes 393224 | tf_op jit(solution)/shard_map/ppermute | solution.py:418
  56.8 5.8 %all-to-all-done.1.mine = bf16[16,144,128]{2,1,0:T(8,128)(2,1)S(1)} async-done(((bf16[16,144,128]{2,1,0:T(8,128)(2,1)}), bf16[16,144,128]{2,1,0:T(8,128)(2,1)S(1)}, u32[]{:S(2)}, u32[]{:S(2)}) %all-to-all-start.1) | async-done | bytes 589856 | tf_op jit(solution)/shard_map/all_to_all | solution.py:52
  62.6 1.0 shard_map.71
  63.6 4.1 %collective-permute-done.3.refs_1_ = bf16[4,128,128]{2,1,0:T(8,128)(2,1)S(1)} collective-permute-done((bf16[4,128,128]{2,1,0:T(8,128)(2,1)S(1)}, bf16[4,128,128]{2,1,0:T(8,128)(2,1)S(1)}, u32[]{:S(2)}, u32[]{:S(2)}) %collective-permute-start.3) | collective-permute-done | bytes 131104 | tf_op jit(solution)/shard_map/ppermute | solution.py:418
  67.7 2.3 %collective-permute-done.4.refs_2_ = bf16[4,128,128]{2,1,0:T(8,128)(2,1)S(1)} collective-permute-done((bf16[4,128,128]{2,1,0:T(8,128)(2,1)S(1)}, bf16[4,128,128]{2,1,0:T(8,128)(2,1)S(1)}, u32[]{:S(2)}, u32[]{:S(2)}) %collective-permute-start.4) | collective-permute-done | bytes 131104 | tf_op jit(solution)/shard_map/ppermute | solution.py:418
  70.1 0.9 shard_map.72.near_mine
  71.0 2.8 %collective-permute-start.6 = (bf16[20,128,128]{2,1,0:T(8,128)(2,1)S(1)}, bf16[20,128,128]{2,1,0:T(8,128)(2,1)S(1)}, u32[]{:S(2)}, u32[]{:S(2)}) collective-permute-start(bf16[20,128,128]{2,1,0:T(8,128)(2,1)S(1)} %shard_map.72.near_mine), channel_id=1, source_target_pairs={{0,8},{8,0},{1,9},{9,1},{2,10},{10,2},{3,11},{11,3},{4,12},{12,4},... | collective-permute-start | bytes 1966088 | tf_op jit(solution)/shard_map/ppermute | solution.py:419
  73.8 1.9 %collective-permute-start.2 = (bf16[16,144,128]{2,1,0:T(8,128)(2,1)S(1)}, bf16[16,144,128]{2,1,0:T(8,128)(2,1)}, u32[]{:S(2)}, u32[]{:S(2)}) collective-permute-start(bf16[16,144,128]{2,1,0:T(8,128)(2,1)S(1)} %all-to-all-done.1.mine), channel_id=1, source_target_pairs={{0,8},{8,0},{1,9},{9,1},{2,10},{10,2},{3,11},{11,3},{4,12},{12,4},... | collective-permute-start | bytes 1769480 | tf_op jit(solution)/shard_map/ppermute | solution.py:419
  75.7 7.0 %all-to-all-start.2 = ((f32[32,2,256]{2,1,0:T(2,128)}), f32[32,2,256]{2,1,0:T(2,128)S(1)}, u32[]{:S(2)}, u32[]{:S(2)}) async-start(f32[32,2,256]{2,1,0:T(2,128)} %get-tuple-element.20), calls=%async_computation.2 | async-start | bytes 131072 | tf_op jit(solution)/shard_map/all_to_all | solution.py:52
  82.7 6.8 %shard_map.73 = (bf16[5,256,128]{2,1,0:T(8,128)(2,1)}, bf16[16,144,128]{2,1,0:T(8,128)(2,1)S(1)}, bf16[16,144,128]{2,1,0:T(8,128)(2,1)}, bf16[20,128,128]{2,1,0:...) custom-call(s32[1,16]{1,0:T(1,128)S(1)} %copy-done.3, ...), custom_call_target="tpu_custom_call", output_to_operand_aliasing={{1}: (4, {}), {2}: (5, {}), {3}: (6, {}), {4}: (7, {})} | custom-call | flops 1006632960 | bytes 2097152 | tf_op jit(solution)/shard_map/pallas_call | solution.py:367
  89.5 4.3 %all-to-all-done.2.stats = f32[32,2,256]{2,1,0:T(2,128)S(1)} async-done(((f32[32,2,256]{2,1,0:T(2,128)}), f32[32,2,256]{2,1,0:T(2,128)S(1)}, u32[]{:S(2)}, u32[]{:S(2)}) %all-to-all-start.2) | async-done | bytes 65568 | tf_op jit(solution)/shard_map/all_to_all | solution.py:52
  93.9 1.0 shard_map.75
  94.8 6.1 %all-to-all-start.3 = ((f32[16,1,256]{2,1,0:T(1,128)}), f32[16,1,256]{2,1,0:T(1,128)S(1)}, u32[]{:S(2)}, u32[]{:S(2)}) async-start(f32[16,1,256]{2,1,0:T(1,128)} %shard_map.75), calls=%async_computation.3 | async-start | bytes 32768 | tf_op jit(solution)/shard_map/all_to_all | solution.py:52
  100.9 4.6 %shard_map.74 = bf16[5,256,128]{2,1,0:T(8,128)(2,1)} custom-call(bf16[5,256,128]{2,1,0:T(8,128)(2,1)S(1)} %bitcast.8, bf16[16,144,128]{2,1,0:T(8,128)(2,1)S(1)} %get-tuple-element.15.mine, bf16[16,144,128]{2,1,0:T(8,128)(2,1)} %get-tuple-element.16.theirs, bf16[20,128,128]{2,1,0:T(8,128)(2,1)S(1)} %get-tuple-element.17.near_mine, ...), custom_call_target="tpu_custom_call", output_to_operand_aliasing={{}: (5, {})} | custom-call | flops 1006632960 | bytes 2097152 | tf_op jit(solution)/shard_map/pallas_call | solution.py:391
  105.5 0.9 all-to-all-done.3
  (18 shorter events, 2.2 us)
Async XLA Ops:
  2.4 17.8 %copy-start.2 = (bf16[4,128,128]{2,1,0:T(8,128)(2,1)S(1)}, bf16[4,128,128]{2,1,0:T(8,128)(2,1)}, u32[]{:S(2)}) copy-start(bf16[4,128,128]{2,1,0:T(8,128)(2,1)} %get-tuple-element.13.refs_0_) | copy-start | bytes 393220
  2.4 23.2 %copy-start.1 = (bf16[256,1,128]{2,0,1:T(8,128)(2,1)S(1)}, bf16[256,1,128]{2,0,1:T(8,128)(2,1)}, u32[]{:S(2)}) copy-start(bf16[256,1,128]{2,0,1:T(8,128)(2,1)} %param.6) | copy-start | bytes 196612
  2.4 33.3 %all-to-all-start = ((bf16[64,16,128]{2,1,0:T(8,128)(2,1)}), bf16[64,16,128]{2,1,0:T(8,128)(2,1)S(1)}, u32[]{:S(2)}, u32[]{:S(2)}) async-start(bf16[64,16,128]{2,1,0:T(8,128)(2,1)} %get-tuple-element.12), calls=%async_computation | async-start | bytes 524288 | tf_op jit(solution)/shard_map/all_to_all | solution.py:52
  20.2 8.0 %copy-start.3 = (s32[1,16]{1,0:T(1,128)S(1)}, s32[1,16]{1,0:T(1,128)}, u32[]{:S(2)}) copy-start(s32[1,16]{1,0:T(1,128)} %vertical.1) | copy-start | bytes 196
  20.2 14.8 %collective-permute-start = (bf16[4,128,128]{2,1,0:T(8,128)(2,1)S(1)}, bf16[4,128,128]{2,1,0:T(8,128)(2,1)S(1)}, u32[]{:S(2)}, u32[]{:S(2)}) collective-permute-start(bf16[4,128,128]{2,1,0:T(8,128)(2,1)S(1)} %copy-done.2), channel_id=1, source_target_pairs={{0,48},{16,64},{32,80},{48,96},{64,112},{80,128},{96,144},{112,160... | collective-permute-start | bytes 393224 | tf_op jit(solution)/shard_map/ppermute | solution.py:418
  25.6 3.4 %collective-permute-start.1 = (bf16[256,128]{1,0:T(8,128)(2,1)S(1)}, bf16[256,128]{1,0:T(8,128)(2,1)S(1)}, u32[]{:S(2)}, u32[]{:S(2)}) collective-permute-start(bf16[256,128]{1,0:T(8,128)(2,1)S(1)} %bitcast.11), channel_id=1, source_target_pairs={{0,8},{8,0},{1,9},{9,1},{2,10},{10,2},{3,11},{11,3},{4,12},{12,4},... | collective-permute-start | bytes 196616 | tf_op jit(solution)/shard_map/ppermute | solution.py:419
  36.8 25.8 %all-to-all-start.1 = ((bf16[16,144,128]{2,1,0:T(8,128)(2,1)}), bf16[16,144,128]{2,1,0:T(8,128)(2,1)S(1)}, u32[]{:S(2)}, u32[]{:S(2)}) async-start(bf16[16,144,128]{2,1,0:T(8,128)(2,1)} %shard_map.70), calls=%async_computation.1 | async-start | bytes 1179648 | tf_op jit(solution)/shard_map/all_to_all | solution.py:52
  44.0 19.6 %collective-permute-start.5 = (bf16[4,128,128]{2,1,0:T(8,128)(2,1)S(1)}, bf16[4,128,128]{2,1,0:T(8,128)(2,1)S(1)}, u32[]{:S(2)}, u32[]{:S(2)}) collective-permute-start(bf16[4,128,128]{2,1,0:T(8,128)(2,1)S(1)} %copy-done.2), channel_id=1, source_target_pairs={{0,64},{16,80},{32,96},{48,112},{64,128},{80,144},{96,160},{112,17... | collective-permute-start | bytes 393224 | tf_op jit(solution)/shard_map/ppermute | solution.py:418
  47.3 20.5 %collective-permute-start.3 = (bf16[4,128,128]{2,1,0:T(8,128)(2,1)S(1)}, bf16[4,128,128]{2,1,0:T(8,128)(2,1)S(1)}, u32[]{:S(2)}, u32[]{:S(2)}) collective-permute-start(bf16[4,128,128]{2,1,0:T(8,128)(2,1)S(1)} %copy-done.2), channel_id=1, source_target_pairs={{0,16},{16,32},{32,48},{48,64},{64,80},{80,96},{96,112},{112,128},... | collective-permute-start | bytes 393224 | tf_op jit(solution)/shard_map/ppermute | solution.py:418
  51.3 18.8 %collective-permute-start.4 = (bf16[4,128,128]{2,1,0:T(8,128)(2,1)S(1)}, bf16[4,128,128]{2,1,0:T(8,128)(2,1)S(1)}, u32[]{:S(2)}, u32[]{:S(2)}) collective-permute-start(bf16[4,128,128]{2,1,0:T(8,128)(2,1)S(1)} %collective-permute-done.three.refs_3_), channel_id=1, source_target_pairs={{0,496},{16,0},{32,16},{48,32},{64,48},{80,64},{96,80},{112,96},{1... | collective-permute-start | bytes 393224 | tf_op jit(solution)/shard_map/ppermute | solution.py:418
  70.1 12.6 %copy-start = (bf16[256,5,128]{2,0,1:T(8,128)(2,1)S(1)}, bf16[256,5,128]{2,0,1:T(8,128)(2,1)}, u32[]{:S(2)}) copy-start(bf16[256,5,128]{2,0,1:T(8,128)(2,1)} %param.5) | copy-start | bytes 983044
  71.0 11.7 %collective-permute-start.6 = (bf16[20,128,128]{2,1,0:T(8,128)(2,1)S(1)}, bf16[20,128,128]{2,1,0:T(8,128)(2,1)S(1)}, u32[]{:S(2)}, u32[]{:S(2)}) collective-permute-start(bf16[20,128,128]{2,1,0:T(8,128)(2,1)S(1)} %shard_map.72.near_mine), channel_id=1, source_target_pairs={{0,8},{8,0},{1,9},{9,1},{2,10},{10,2},{3,11},{11,3},{4,12},{12,4},... | collective-permute-start | bytes 1966088 | tf_op jit(solution)/shard_map/ppermute | solution.py:419
  73.8 8.9 %collective-permute-start.2 = (bf16[16,144,128]{2,1,0:T(8,128)(2,1)S(1)}, bf16[16,144,128]{2,1,0:T(8,128)(2,1)}, u32[]{:S(2)}, u32[]{:S(2)}) collective-permute-start(bf16[16,144,128]{2,1,0:T(8,128)(2,1)S(1)} %all-to-all-done.1.mine), channel_id=1, source_target_pairs={{0,8},{8,0},{1,9},{9,1},{2,10},{10,2},{3,11},{11,3},{4,12},{12,4},... | collective-permute-start | bytes 1769480 | tf_op jit(solution)/shard_map/ppermute | solution.py:419
  75.7 7.1 %copy-start.4 = (s32[1,8]{1,0:T(1,128)S(1)}, s32[1,8]{1,0:T(1,128)}, u32[]{:S(2)}) copy-start(s32[1,8]{1,0:T(1,128)} %slash.1) | copy-start | bytes 100
  75.7 18.2 %all-to-all-start.2 = ((f32[32,2,256]{2,1,0:T(2,128)}), f32[32,2,256]{2,1,0:T(2,128)S(1)}, u32[]{:S(2)}, u32[]{:S(2)}) async-start(f32[32,2,256]{2,1,0:T(2,128)} %get-tuple-element.20), calls=%async_computation.2 | async-start | bytes 131072 | tf_op jit(solution)/shard_map/all_to_all | solution.py:52
  94.8 11.6 %all-to-all-start.3 = ((f32[16,1,256]{2,1,0:T(1,128)}), f32[16,1,256]{2,1,0:T(1,128)S(1)}, u32[]{:S(2)}, u32[]{:S(2)}) async-start(f32[16,1,256]{2,1,0:T(1,128)} %shard_map.75), calls=%async_computation.3 | async-start | bytes 32768 | tf_op jit(solution)/shard_map/all_to_all | solution.py:52

commit v10 on v9

--- a/solution.py
+++ b/solution.py
@@ -138,7 +138,7 @@
 
 
 def together_kernel(*refs):
-    *parts, after, out, sems = refs
+    *parts, _, _, out, sems = refs
     each = parts[0].shape[0]
     copies = [pltpu.make_async_copy(part, out.at[pl.ds(each * i, each)], sems.at[i]) for i, part in enumerate(parts)]
     for copy in copies:
@@ -147,16 +147,16 @@
         copy.wait()
 
 
-def together(parts, after):
+def together(parts, *after):
     n = len(parts)
     return pl.pallas_call(
         together_kernel,
         out_shape=shape(BF16, n * parts[0].shape[0], UNIT, HD),
-        in_specs=[ANY] * (n + 1),
+        in_specs=[ANY] * (n + len(after)),
         out_specs=ANY,
         scratch_shapes=[pltpu.SemaphoreType.DMA((n + 1,))],
         compiler_params=SMALL,
-    )(*parts, after)
+    )(*parts, *after)
 
 
 def estimate_kernel(total_len, position, q, k_mine, k_theirs, scores, stats):
@@ -423,7 +423,7 @@
     one, two, four = back(kv, 1), back(three, -1), back(kv, 4)
     scores, stats = estimate(place, mine[:, LISTED:].reshape(QALL, HD), k, k_theirs, total_len)
     theirs = swap(mine)
-    near_mine = together([kv, one, two, three, four], scores)
+    near_mine = together([kv, one, two, three, four], scores, theirs)
     near_theirs = swap(near_mine)
 
     out, *handed, token = attend_first(vertical, slash_offsets, place, q_t, mine, theirs, near_mine, near_theirs)

time: 108 us -> 120 us (1.11)
  blocking collectives: 0 us -> 26.1 us
  waiting for transfers between devices: 24.4 us -> 14.5 us
  starting transfers between devices: 63.4 us -> 60.9 us
    all_to_all x0 -> x1, blocking collectives: none -> 26.1 us  [exchange(): return lax.all_to_all(x, axis, 0, 0)]
    all_to_all x4 -> x3, waiting for transfers between devices: 11.7 us -> 6.22 us  [exchange(): return lax.all_to_all(x, axis, 0, 0)]
    all_to_all x4 -> x3, starting transfers between devices: 38 us -> 33 us  [exchange(): return lax.all_to_all(x, axis, 0, 0)]
    ppermute x4, waiting for transfers between devices: 12.5 us -> 8.04 us  [on_device(): lax.ppermute(x, CHIP, [(i, (i + chips) % CHIPS) for i in range(CHIPS)])]
    ppermute x3, starting transfers between devices: 7.23 us -> 10.8 us  [on_device(): swap = lambda x: lax.ppermute(x, 'core', [(0, 1), (1, 0)])]
  transfers between devices with their start and end apart: 11 -> 10, of which waited for: 8 -> 6; matrix products, arithmetic and copies ran while one was open for 0% -> 0% of each run, Pallas kernels for 12% -> 11%
where the time goes in v10:
time: 120 us
  starting transfers between devices  60.9 us (51%)
  blocking collectives  26.1 us (22%)
  Pallas kernels  16.6 us (14%)
  waiting for transfers between devices  14.5 us (12%)
    all_to_all x3, starting transfers between devices, exchange(): return lax.all_to_all(x, axis, 0, 0)  33 us
    all_to_all x1, blocking collectives, exchange(): return lax.all_to_all(x, axis, 0, 0)  26.1 us
    ppermute x4, starting transfers between devices, on_device(): lax.ppermute(x, CHIP, [(i, (i + chips) % CHIPS) for i in range(CHIPS)])  17.1 us
    ppermute x3, starting transfers between devices, on_device(): swap = lambda x: lax.ppermute(x, 'core', [(0, 1), (1, 0)])  10.8 us
    ppermute x4, waiting for transfers between devices, on_device(): lax.ppermute(x, CHIP, [(i, (i + chips) % CHIPS) for i in range(CHIPS)])  8.04 us
    pallas_call x1, Pallas kernels, attend_first(): pl.pallas_call(first_kernel, out_shape=(shape(BF16, *q_t.shape), *(shape(...  6.66 us
    all_to_all x3, waiting for transfers between devices, exchange(): return lax.all_to_all(x, axis, 0, 0)  6.22 us
    pallas_call x1, Pallas kernels, attend_second(): pl.pallas_call(second_kernel, out_shape=shape(BF16, *q_t.shape), in_specs...  4.49 us
  transfers between devices with their start and end apart: 10, of which 6 were waited for; matrix products, arithmetic and copies ran while one was open for 0% of the time, Pallas kernels for 11%

profile of v10, /device:TPU:1, one launch (start us, length us, event | category | flops | bytes accessed | tf_op | source)
XLA Modules:
  0.0 119.7 jit_solution(9161625355205507850)
XLA Ops:
  0.6 1.7 %shard_map.69 = (bf16[64,16,128]{2,1,0:T(8,128)(2,1)}, bf16[4,128,128]{2,1,0:T(8,128)(2,1)}) custom-call(s32[1]{0:T(128)} %bitcast.1.position, bf16[5,256,128]{2,1,0:T(8,128)(2,1)} %bitcast.6, bf16[256,128]{1,0:T(8,128)(2,1)} %bitcast.10, bf16[256,128]{1,0:T(8,128)(2,1)} %bitcast.13), custom_call_target="tpu_custom_call" | custom-call | tf_op jit(solution)/shard_map/pallas_call | solution.py:87
  2.4 17.8 %all-to-all-start = ((bf16[64,16,128]{2,1,0:T(8,128)(2,1)}), bf16[64,16,128]{2,1,0:T(8,128)(2,1)S(1)}, u32[]{:S(2)}, u32[]{:S(2)}) async-start(bf16[64,16,128]{2,1,0:T(8,128)(2,1)} %get-tuple-element.12), calls=%async_computation | async-start | bytes 524288 | tf_op jit(solution)/shard_map/all_to_all | solution.py:52
  20.2 5.4 %collective-permute-start = (bf16[4,128,128]{2,1,0:T(8,128)(2,1)S(1)}, bf16[4,128,128]{2,1,0:T(8,128)(2,1)S(1)}, u32[]{:S(2)}, u32[]{:S(2)}) collective-permute-start(bf16[4,128,128]{2,1,0:T(8,128)(2,1)S(1)} %copy-done.2), channel_id=1, source_target_pairs={{0,48},{16,64},{32,80},{48,96},{64,112},{80,128},{96,144},{112,160... | collective-permute-start | bytes 393224 | tf_op jit(solution)/shard_map/ppermute | solution.py:418
  25.6 2.5 %collective-permute-start.1 = (bf16[256,128]{1,0:T(8,128)(2,1)S(1)}, bf16[256,128]{1,0:T(8,128)(2,1)S(1)}, u32[]{:S(2)}, u32[]{:S(2)}) collective-permute-start(bf16[256,128]{1,0:T(8,128)(2,1)S(1)} %bitcast.11), channel_id=1, source_target_pairs={{0,8},{8,0},{1,9},{9,1},{2,10},{10,2},{3,11},{11,3},{4,12},{12,4},... | collective-permute-start | bytes 196616 | tf_op jit(solution)/shard_map/ppermute | solution.py:419
  28.2 0.6 shard_map.68.chosen
  29.1 6.0 %collective-permute-done.three.refs_3_ = bf16[4,128,128]{2,1,0:T(8,128)(2,1)S(1)} collective-permute-done((bf16[4,128,128]{2,1,0:T(8,128)(2,1)S(1)}, bf16[4,128,128]{2,1,0:T(8,128)(2,1)S(1)}, u32[]{:S(2)}, u32[]{:S(2)}) %collective-permute-start) | collective-permute-done | bytes 131104 | tf_op jit(solution)/shard_map/ppermute | solution.py:418
  35.1 0.7 all-to-all-done.r
  36.0 26.1 %all_to_all.20.mine = bf16[16,144,128]{2,1,0:T(8,128)(2,1)S(1)} all-to-all(bf16[16,144,128]{2,1,0:T(8,128)(2,1)S(1)} %shard_map.70), channel_id=1, replica_groups=mesh['y'=8,'zhi'=2,'zlo'=2,'core'=2,'kvh'=8] {'y','zlo'}, dimensions={0} | all-to-all | bytes 1179648 | tf_op jit(solution)/shard_map/all_to_all | solution.py:52
  62.1 4.2 %collective-permute-start.2 = (bf16[16,144,128]{2,1,0:T(8,128)(2,1)S(1)}, bf16[16,144,128]{2,1,0:T(8,128)(2,1)S(1)}, u32[]{:S(2)}, u32[]{:S(2)}) collective-permute-start(bf16[16,144,128]{2,1,0:T(8,128)(2,1)S(1)} %all_to_all.20.mine), channel_id=1, source_target_pairs={{0,8},{8,0},{1,9},{9,1},{2,10},{10,2},{3,11},{11,3},{4,12},{12,4},... | collective-permute-start | bytes 1769480 | tf_op jit(solution)/shard_map/ppermute | solution.py:419
  66.3 2.1 %collective-permute-start.5 = (bf16[4,128,128]{2,1,0:T(8,128)(2,1)S(1)}, bf16[4,128,128]{2,1,0:T(8,128)(2,1)S(1)}, u32[]{:S(2)}, u32[]{:S(2)}) collective-permute-start(bf16[4,128,128]{2,1,0:T(8,128)(2,1)S(1)} %copy-done.2), channel_id=1, source_target_pairs={{0,64},{16,80},{32,96},{48,112},{64,128},{80,144},{96,160},{112,17... | collective-permute-start | bytes 393224 | tf_op jit(solution)/shard_map/ppermute | solution.py:418
  68.5 2.2 %collective-permute-start.3 = (bf16[4,128,128]{2,1,0:T(8,128)(2,1)S(1)}, bf16[4,128,128]{2,1,0:T(8,128)(2,1)S(1)}, u32[]{:S(2)}, u32[]{:S(2)}) collective-permute-start(bf16[4,128,128]{2,1,0:T(8,128)(2,1)S(1)} %copy-done.2), channel_id=1, source_target_pairs={{0,16},{16,32},{32,48},{48,64},{64,80},{80,96},{96,112},{112,128},... | collective-permute-start | bytes 393224 | tf_op jit(solution)/shard_map/ppermute | solution.py:418
  70.7 7.3 %collective-permute-start.4 = (bf16[4,128,128]{2,1,0:T(8,128)(2,1)S(1)}, bf16[4,128,128]{2,1,0:T(8,128)(2,1)S(1)}, u32[]{:S(2)}, u32[]{:S(2)}) collective-permute-start(bf16[4,128,128]{2,1,0:T(8,128)(2,1)S(1)} %collective-permute-done.three.refs_3_), channel_id=1, source_target_pairs={{0,496},{16,0},{32,16},{48,32},{64,48},{80,64},{96,80},{112,96},{1... | collective-permute-start | bytes 393224 | tf_op jit(solution)/shard_map/ppermute | solution.py:418
  78.0 1.0 shard_map.71
  79.0 2.1 %collective-permute-done.3.refs_1_ = bf16[4,128,128]{2,1,0:T(8,128)(2,1)S(1)} collective-permute-done((bf16[4,128,128]{2,1,0:T(8,128)(2,1)S(1)}, bf16[4,128,128]{2,1,0:T(8,128)(2,1)S(1)}, u32[]{:S(2)}, u32[]{:S(2)}) %collective-permute-start.3) | collective-permute-done | bytes 131104 | tf_op jit(solution)/shard_map/ppermute | solution.py:418
  81.1 0.9 shard_map.72.near_mine
  82.0 4.1 %collective-permute-start.6 = (bf16[20,128,128]{2,1,0:T(8,128)(2,1)S(1)}, bf16[20,128,128]{2,1,0:T(8,128)(2,1)}, u32[]{:S(2)}, u32[]{:S(2)}) collective-permute-start(bf16[20,128,128]{2,1,0:T(8,128)(2,1)S(1)} %shard_map.72.near_mine), channel_id=1, source_target_pairs={{0,8},{8,0},{1,9},{9,1},{2,10},{10,2},{3,11},{11,3},{4,12},{12,4},... | collective-permute-start | bytes 1966088 | tf_op jit(solution)/shard_map/ppermute | solution.py:419
  86.1 8.4 %all-to-all-start.2 = ((f32[32,2,256]{2,1,0:T(2,128)}), f32[32,2,256]{2,1,0:T(2,128)S(1)}, u32[]{:S(2)}, u32[]{:S(2)}) async-start(f32[32,2,256]{2,1,0:T(2,128)} %get-tuple-element.20), calls=%async_computation.2 | async-start | bytes 131072 | tf_op jit(solution)/shard_map/all_to_all | solution.py:52
  94.5 6.7 %shard_map.73 = (bf16[5,256,128]{2,1,0:T(8,128)(2,1)}, bf16[16,144,128]{2,1,0:T(8,128)(2,1)S(1)}, bf16[16,144,128]{2,1,0:T(8,128)(2,1)S(1)}, bf16[20,128,128]{2,...) custom-call(s32[1,16]{1,0:T(1,128)S(1)} %copy-done.3, ...), custom_call_target="tpu_custom_call", output_to_operand_aliasing={{1}: (4, {}), {2}: (5, {}), {3}: (6, {}), {4}: (7, {})} | custom-call | flops 1006632960 | bytes 2097152 | tf_op jit(solution)/shard_map/pallas_call | solution.py:367
  101.2 4.5 %all-to-all-done.2.stats = f32[32,2,256]{2,1,0:T(2,128)S(1)} async-done(((f32[32,2,256]{2,1,0:T(2,128)}), f32[32,2,256]{2,1,0:T(2,128)S(1)}, u32[]{:S(2)}, u32[]{:S(2)}) %all-to-all-start.2) | async-done | bytes 65568 | tf_op jit(solution)/shard_map/all_to_all | solution.py:52
  105.7 1.0 shard_map.75
  106.7 6.9 %all-to-all-start.3 = ((f32[16,1,256]{2,1,0:T(1,128)}), f32[16,1,256]{2,1,0:T(1,128)S(1)}, u32[]{:S(2)}, u32[]{:S(2)}) async-start(f32[16,1,256]{2,1,0:T(1,128)} %shard_map.75), calls=%async_computation.3 | async-start | bytes 32768 | tf_op jit(solution)/shard_map/all_to_all | solution.py:52
  113.6 4.5 %shard_map.74 = bf16[5,256,128]{2,1,0:T(8,128)(2,1)} custom-call(bf16[5,256,128]{2,1,0:T(8,128)(2,1)S(1)} %bitcast.8, bf16[16,144,128]{2,1,0:T(8,128)(2,1)S(1)} %get-tuple-element.15.mine, bf16[16,144,128]{2,1,0:T(8,128)(2,1)S(1)} %get-tuple-element.16.theirs, bf16[20,128,128]{2,1,0:T(8,128)(2,1)S(1)} %get-tuple-element.17.near_mine, ...), custom_call_target="tpu_custom_call", output_to_operand_aliasing={{}: (5, {})} | custom-call | flops 1006632960 | bytes 2097152 | tf_op jit(solution)/shard_map/pallas_call | solution.py:391
  118.1 1.0 all-to-all-done.3
  119.1 0.6 reduce_sum.9
  (17 shorter events, 0.5 us)
Async XLA Ops:
  2.4 17.8 %copy-start.2 = (bf16[4,128,128]{2,1,0:T(8,128)(2,1)S(1)}, bf16[4,128,128]{2,1,0:T(8,128)(2,1)}, u32[]{:S(2)}) copy-start(bf16[4,128,128]{2,1,0:T(8,128)(2,1)} %get-tuple-element.13.refs_0_) | copy-start | bytes 393220
  2.4 23.2 %copy-start.1 = (bf16[256,1,128]{2,0,1:T(8,128)(2,1)S(1)}, bf16[256,1,128]{2,0,1:T(8,128)(2,1)}, u32[]{:S(2)}) copy-start(bf16[256,1,128]{2,0,1:T(8,128)(2,1)} %param.6) | copy-start | bytes 196612
  2.4 33.3 %all-to-all-start = ((bf16[64,16,128]{2,1,0:T(8,128)(2,1)}), bf16[64,16,128]{2,1,0:T(8,128)(2,1)S(1)}, u32[]{:S(2)}, u32[]{:S(2)}) async-start(bf16[64,16,128]{2,1,0:T(8,128)(2,1)} %get-tuple-element.12), calls=%async_computation | async-start | bytes 524288 | tf_op jit(solution)/shard_map/all_to_all | solution.py:52
  20.2 8.0 %copy-start.3 = (s32[1,16]{1,0:T(1,128)S(1)}, s32[1,16]{1,0:T(1,128)}, u32[]{:S(2)}) copy-start(s32[1,16]{1,0:T(1,128)} %vertical.1) | copy-start | bytes 196
  20.2 14.8 %collective-permute-start = (bf16[4,128,128]{2,1,0:T(8,128)(2,1)S(1)}, bf16[4,128,128]{2,1,0:T(8,128)(2,1)S(1)}, u32[]{:S(2)}, u32[]{:S(2)}) collective-permute-start(bf16[4,128,128]{2,1,0:T(8,128)(2,1)S(1)} %copy-done.2), channel_id=1, source_target_pairs={{0,48},{16,64},{32,80},{48,96},{64,112},{80,128},{96,144},{112,160... | collective-permute-start | bytes 393224 | tf_op jit(solution)/shard_map/ppermute | solution.py:418
  25.6 3.4 %collective-permute-start.1 = (bf16[256,128]{1,0:T(8,128)(2,1)S(1)}, bf16[256,128]{1,0:T(8,128)(2,1)S(1)}, u32[]{:S(2)}, u32[]{:S(2)}) collective-permute-start(bf16[256,128]{1,0:T(8,128)(2,1)S(1)} %bitcast.11), channel_id=1, source_target_pairs={{0,8},{8,0},{1,9},{9,1},{2,10},{10,2},{3,11},{11,3},{4,12},{12,4},... | collective-permute-start | bytes 196616 | tf_op jit(solution)/shard_map/ppermute | solution.py:419
  62.1 19.0 %collective-permute-start.2 = (bf16[16,144,128]{2,1,0:T(8,128)(2,1)S(1)}, bf16[16,144,128]{2,1,0:T(8,128)(2,1)S(1)}, u32[]{:S(2)}, u32[]{:S(2)}) collective-permute-start(bf16[16,144,128]{2,1,0:T(8,128)(2,1)S(1)} %all_to_all.20.mine), channel_id=1, source_target_pairs={{0,8},{8,0},{1,9},{9,1},{2,10},{10,2},{3,11},{11,3},{4,12},{12,4},... | collective-permute-start | bytes 1769480 | tf_op jit(solution)/shard_map/ppermute | solution.py:419
  66.3 12.7 %collective-permute-start.5 = (bf16[4,128,128]{2,1,0:T(8,128)(2,1)S(1)}, bf16[4,128,128]{2,1,0:T(8,128)(2,1)S(1)}, u32[]{:S(2)}, u32[]{:S(2)}) collective-permute-start(bf16[4,128,128]{2,1,0:T(8,128)(2,1)S(1)} %copy-done.2), channel_id=1, source_target_pairs={{0,64},{16,80},{32,96},{48,112},{64,128},{80,144},{96,160},{112,17... | collective-permute-start | bytes 393224 | tf_op jit(solution)/shard_map/ppermute | solution.py:418
  68.5 12.6 %collective-permute-start.3 = (bf16[4,128,128]{2,1,0:T(8,128)(2,1)S(1)}, bf16[4,128,128]{2,1,0:T(8,128)(2,1)S(1)}, u32[]{:S(2)}, u32[]{:S(2)}) collective-permute-start(bf16[4,128,128]{2,1,0:T(8,128)(2,1)S(1)} %copy-done.2), channel_id=1, source_target_pairs={{0,16},{16,32},{32,48},{48,64},{64,80},{80,96},{96,112},{112,128},... | collective-permute-start | bytes 393224 | tf_op jit(solution)/shard_map/ppermute | solution.py:418
  70.7 10.4 %collective-permute-start.4 = (bf16[4,128,128]{2,1,0:T(8,128)(2,1)S(1)}, bf16[4,128,128]{2,1,0:T(8,128)(2,1)S(1)}, u32[]{:S(2)}, u32[]{:S(2)}) collective-permute-start(bf16[4,128,128]{2,1,0:T(8,128)(2,1)S(1)} %collective-permute-done.three.refs_3_), channel_id=1, source_target_pairs={{0,496},{16,0},{32,16},{48,32},{64,48},{80,64},{96,80},{112,96},{1... | collective-permute-start | bytes 393224 | tf_op jit(solution)/shard_map/ppermute | solution.py:418
  81.1 13.4 %copy-start = (bf16[256,5,128]{2,0,1:T(8,128)(2,1)S(1)}, bf16[256,5,128]{2,0,1:T(8,128)(2,1)}, u32[]{:S(2)}) copy-start(bf16[256,5,128]{2,0,1:T(8,128)(2,1)} %param.5) | copy-start | bytes 983044
  82.0 12.5 %collective-permute-start.6 = (bf16[20,128,128]{2,1,0:T(8,128)(2,1)S(1)}, bf16[20,128,128]{2,1,0:T(8,128)(2,1)}, u32[]{:S(2)}, u32[]{:S(2)}) collective-permute-start(bf16[20,128,128]{2,1,0:T(8,128)(2,1)S(1)} %shard_map.72.near_mine), channel_id=1, source_target_pairs={{0,8},{8,0},{1,9},{9,1},{2,10},{10,2},{3,11},{11,3},{4,12},{12,4},... | collective-permute-start | bytes 1966088 | tf_op jit(solution)/shard_map/ppermute | solution.py:419
  86.1 8.4 %copy-start.4 = (s32[1,8]{1,0:T(1,128)S(1)}, s32[1,8]{1,0:T(1,128)}, u32[]{:S(2)}) copy-start(s32[1,8]{1,0:T(1,128)} %slash.1) | copy-start | bytes 100
  86.1 19.6 %all-to-all-start.2 = ((f32[32,2,256]{2,1,0:T(2,128)}), f32[32,2,256]{2,1,0:T(2,128)S(1)}, u32[]{:S(2)}, u32[]{:S(2)}) async-start(f32[32,2,256]{2,1,0:T(2,128)} %get-tuple-element.20), calls=%async_computation.2 | async-start | bytes 131072 | tf_op jit(solution)/shard_map/all_to_all | solution.py:52
  106.7 12.4 %all-to-all-start.3 = ((f32[16,1,256]{2,1,0:T(1,128)}), f32[16,1,256]{2,1,0:T(1,128)S(1)}, u32[]{:S(2)}, u32[]{:S(2)}) async-start(f32[16,1,256]{2,1,0:T(1,128)} %shard_map.75), calls=%async_computation.3 | async-start | bytes 32768 | tf_op jit(solution)/shard_map/all_to_all | solution.py:52
